TPU v7x, 256 devices: a whole 4x4x8 slice. The times are simulated.
256 devices in a mesh: gx: 16 (over y, x), gy: 16 (over z, core).
Axes of the slice: x: 4, y: 4, z: 8, core: 2. Of those that a mesh axis runs over, the one named last changes fastest.
Arguments:
- zonal_wind_field: float32 [32, 128, 2048], P(None, 'gx', 'gy'), may hold values from -6 to 6
- meridional_wind_field: float32 [32, 128, 2048], P(None, 'gx', 'gy'), may hold values from -6 to 6
- vertical_wind_field: float32 [32, 128, 2048], P(None, 'gx', 'gy'), may hold values from -6 to 6
- theta_anomaly_field: float32 [32, 128, 2048], P(None, 'gx', 'gy'), may hold values from -6 to 6
- moisture: float32 [32, 128, 2048], P(None, 'gx', 'gy'), may hold values from -6 to 6
- droplets: float32 [48, 48, 10, 1024], P('gx', 'gy'), may hold values from -6 to 6, as said below
- droplet_cell_index: int32 [48, 48, 1024], P('gx', 'gy'), may hold values from 0 to 32767
- droplet_block_count: int32 [48, 48], P('gx', 'gy'), may hold values from 0 to 1024, as said below
Outputs:
- east_next: float32 [32, 128, 2048], P(None, 'gx', 'gy')
- north_next: float32 [32, 128, 2048], P(None, 'gx', 'gy')
- upward_next: float32 [32, 128, 2048], P(None, 'gx', 'gy')
- heat_next: float32 [32, 128, 2048], P(None, 'gx', 'gy')
- moisture_next: float32 [32, 128, 2048], P(None, 'gx', 'gy')
- droplets_next: float32 [48, 48, 10, 1024], P('gx', 'gy')
Inputs may be any that keep to these rules, and one draw needn't show every extreme that they name: `droplets`: rows 0 to 2 of a slot hold position offsets within the cell, in [0, 1); rows 3 to 5 velocities; row 6 the radius, in [0.5, 2]; row 7 the weight, in [0.2, 2]; row 8 the solute mass, in [0.05, 0.5]; row 9 the age, in [0, 2]. Dead slots hold values of the same kinds. `droplet_block_count`: the live droplets of a block fill its first slots. In every draw some device receives 1024 live droplets from each of its nine sources.
All inputs are finite; a program needn't handle non-finite values.
Results may differ from a plain program's by a relative error of at most 0.00075.
Values sent between devices are 32-bit elements; how exact they have to be, the bound alone decides.
No kernel may reach another device: no remote copies, remote signals or barrier semaphores. Data moves between devices by JAX's collectives and lax.ppermute only.
A program may use at most 128 MiB of HBM per device.

v0:
```python
import math

import jax
import jax.numpy as jnp
from jax import lax
from jax.sharding import PartitionSpec as P

TIME_STEP = 0.2
RELAX_TIME = 0.2
GROWTH = 0.5
CURVATURE = 0.1
SOLUTE_EFFECT = 0.05
RADIUS_FLOOR = 0.3
SATURATION_RATE = 0.1
MOIST_LOAD = 0.5
HEAT_LOAD = 1.25
CELL_ASPECT = 0.0625
PLUS_TAPS = (-2.0, 15.0, -60.0, 20.0, 30.0, -3.0)
MINUS_TAPS = (3.0, -30.0, -20.0, 60.0, -15.0, 2.0)
HIGHEST = lax.Precision.HIGHEST


def extended_2(block, sides, width):
    for axis, dim in sides:
        count = lax.axis_size(axis)
        forward = [(i, i + 1) for i in range(count - 1)]
        forward.append((count - 1, 0))
        backward = [(target, source) for source, target in forward]
        low = lax.ppermute(
            lax.slice_in_dim(block, block.shape[dim] - width, None, axis=dim), axis, forward
        )
        high = lax.ppermute(lax.slice_in_dim(block, 0, width, axis=dim), axis, backward)
        block = jnp.concatenate([low, block, high], axis=dim)
    return block


def upwind_sliced(padded, velocity, which_axis, length):
    plus_side = sum(
        (
            weight_tap * lax.slice_in_dim(padded, 3 + offset, 3 + offset + length, axis=which_axis)
            for offset, weight_tap in zip(range(-3, 3), PLUS_TAPS)
        )
    )
    minus_side = sum(
        (
            weight_tap * lax.slice_in_dim(padded, 3 + offset, 3 + offset + length, axis=which_axis)
            for offset, weight_tap in zip(range(-2, 4), MINUS_TAPS)
        )
    )
    return velocity * jnp.where(velocity >= 0.0, plus_side, minus_side) / 60.0


def upwind_vertical(quantity, velocity, which_axis):
    levels = quantity.shape[which_axis]
    widths = [(0, 0)] * quantity.ndim
    widths[which_axis] = (3, 3)
    padded = jnp.pad(quantity, widths, mode="edge")
    plus_side = sum(
        (
            weight_tap * lax.slice_in_dim(padded, 3 + offset, 3 + offset + levels, axis=which_axis)
            for offset, weight_tap in zip(range(-3, 3), PLUS_TAPS)
        )
    )
    minus_side = sum(
        (
            weight_tap * lax.slice_in_dim(padded, 3 + offset, 3 + offset + levels, axis=which_axis)
            for offset, weight_tap in zip(range(-2, 4), MINUS_TAPS)
        )
    )
    return velocity * jnp.where(velocity >= 0.0, plus_side, minus_side) / 60.0


def cosine_table(levels):
    mode_index = lax.broadcasted_iota(jnp.int32, (levels, levels), 0)
    level_index = lax.broadcasted_iota(jnp.int32, (levels, levels), 1)
    phases = (mode_index * (2 * level_index + 1) % (4 * levels)).astype(jnp.float32) * (
        math.pi / (2 * levels)
    )
    factor = jnp.where(mode_index == 0, math.sqrt(1.0 / levels), math.sqrt(2.0 / levels))
    return factor * jnp.cos(phases)


def hartley_table(length):
    row_index = lax.broadcasted_iota(jnp.int32, (length, length), 0)
    col_index = lax.broadcasted_iota(jnp.int32, (length, length), 1)
    phases = (row_index * col_index % length).astype(jnp.float32) * (2.0 * math.pi / length)
    return (jnp.cos(phases) + jnp.sin(phases)) / math.sqrt(length)


def eigen_value(wave_index, period):
    return 2.0 - 2.0 * jnp.cos((wave_index % period).astype(jnp.float32) * (2.0 * math.pi / period))


def next_along(values, block_axis, cell_axis):
    head_part = lax.slice_in_dim(values, 0, 1, axis=cell_axis)
    rest_part = lax.slice_in_dim(values, 1, values.shape[cell_axis], axis=cell_axis)
    return jnp.concatenate([rest_part, jnp.roll(head_part, -1, axis=block_axis)], axis=cell_axis)


def across_x(blocks):
    return lax.all_to_all(blocks, "gx", split_axis=0, concat_axis=0, tiled=True)


def across_y(blocks):
    return lax.all_to_all(blocks, "gy", split_axis=0, concat_axis=0, tiled=True)


def grow_droplets(attributes, air_east, air_north, air_upward, air_heat, air_moist, live_slots):
    radius = attributes[..., 6, :]
    radius_cubed = radius * radius * radius
    keeping = jnp.exp(-TIME_STEP / (RELAX_TIME * radius * radius))
    east_speed = air_east + (attributes[..., 3, :] - air_east) * keeping
    north_speed = air_north + (attributes[..., 4, :] - air_north) * keeping
    rise_speed = air_upward + (attributes[..., 5, :] - air_upward) * keeping
    saturation = air_moist * jnp.exp(-SATURATION_RATE * air_heat) - 1.0
    squared = radius * radius + GROWTH * (
        saturation - CURVATURE / radius + SOLUTE_EFFECT * attributes[..., 8, :] / radius_cubed
    )
    new_radius = jnp.sqrt(jnp.maximum(squared, RADIUS_FLOOR * RADIUS_FLOOR))
    water_gain = (
        live_slots * attributes[..., 7, :] * (new_radius * new_radius * new_radius - radius_cubed)
    )
    rows_out = [
        attributes[..., 0, :] + TIME_STEP * east_speed,
        attributes[..., 1, :] + TIME_STEP * north_speed,
        attributes[..., 2, :] + TIME_STEP * rise_speed,
        east_speed,
        north_speed,
        rise_speed,
        new_radius,
        attributes[..., 7, :],
        attributes[..., 8, :],
        attributes[..., 9, :] + TIME_STEP,
    ]
    moved_drops = jnp.stack(rows_out, axis=-2) * live_slots[..., None, :]
    return (moved_drops, water_gain)


def per_device(
    zonal_wind_field,
    meridional_wind_field,
    vertical_wind_field,
    theta_anomaly_field,
    moisture,
    droplets,
    droplet_cell_index,
    droplet_block_count,
):
    levels, width_x, width_y = zonal_wind_field.shape
    span_x = width_x + 1
    span_y = width_y + 1
    stacked_fields = jnp.stack(
        [
            zonal_wind_field,
            meridional_wind_field,
            vertical_wind_field,
            theta_anomaly_field,
            moisture,
        ]
    )
    extended = extended_2(stacked_fields, (("gx", 2), ("gy", 3)), 4)
    center = extended[:, :, 3 : 3 + span_x, 3 : 3 + span_y]
    tendency = (
        upwind_sliced(extended[:, :, :, 3 : 3 + span_y], center[0], 2, span_x)
        + upwind_sliced(extended[:, :, 3 : 3 + span_x, :], center[1], 3, span_y)
        + upwind_vertical(center, center[2], 1)
    )
    starred = center - TIME_STEP * tendency
    interior = starred[:, :, 1:, 1:]
    level_index = lax.broadcasted_iota(jnp.int32, interior[2].shape, 0)
    upward_star = jnp.where(level_index == levels - 1, 0.0, interior[2])
    upward_below = jnp.concatenate([jnp.zeros_like(upward_star[:1]), upward_star[:-1]], axis=0)
    diverge = (
        interior[0]
        - starred[0, :, :-1, 1:]
        + (interior[1] - starred[1, :, 1:, :-1])
        + (upward_star - upward_below)
    )
    devices_x = lax.axis_size("gx")
    devices_y = lax.axis_size("gy")
    modes_here = levels // devices_x
    total_x = width_x * devices_x
    total_y = width_y * devices_y
    kx_here = total_x // devices_y
    zblock = cosine_table(levels).reshape(devices_x, modes_here, levels)
    source_hat = jnp.einsum("kxy,gmk->gmxy", diverge, zblock, precision=HIGHEST)
    source_hat = across_x(source_hat)
    xtable = hartley_table(total_x)
    spectrum = jnp.einsum(
        "smxy,sxbk->bkmy",
        source_hat,
        xtable.reshape(devices_x, width_x, devices_y, kx_here),
        precision=HIGHEST,
    )
    spectrum = across_y(spectrum)
    ytable = hartley_table(total_y).reshape(devices_y, width_y, total_y)
    full_hat = jnp.einsum("skmy,syl->kml", spectrum, ytable, precision=HIGHEST)
    wave_x = lax.axis_index("gy") * kx_here + lax.broadcasted_iota(jnp.int32, (kx_here, 1, 1), 0)
    mode_index = lax.axis_index("gx") * modes_here + lax.broadcasted_iota(
        jnp.int32, (1, modes_here, 1), 1
    )
    wave_y = lax.broadcasted_iota(jnp.int32, (1, 1, total_y), 2)
    eigen_sum = (
        eigen_value(mode_index, 2 * levels) + eigen_value(wave_x, total_x)
    ) * CELL_ASPECT + eigen_value(wave_y, total_y)
    zero_mode = (mode_index == 0) & (wave_x == 0) & (wave_y == 0)
    pressure_hat = jnp.where(zero_mode, 0.0, -full_hat / jnp.where(zero_mode, 1.0, eigen_sum))
    pressure_y = jnp.einsum("kml,syl->skmy", pressure_hat, ytable, precision=HIGHEST)
    xinverse = xtable.reshape(devices_y, kx_here, devices_x, width_x)
    grad_y = next_along(pressure_y, 0, 3) - pressure_y
    pressure_y, grad_y = across_y((pressure_y, grad_y))
    press_x = jnp.einsum("skmy,skgx->gmxy", pressure_y, xinverse, precision=HIGHEST)
    grad_yx = jnp.einsum("skmy,skgx->gmxy", grad_y, xinverse, precision=HIGHEST)
    grad_xx = next_along(press_x, 0, 2) - press_x
    grad_xx, grad_yx, press_x = across_x((grad_xx, grad_yx, press_x))
    east_grad = jnp.einsum("gmxy,gmk->kxy", grad_xx, zblock, precision=HIGHEST) * CELL_ASPECT
    north_grad = jnp.einsum("gmxy,gmk->kxy", grad_yx, zblock, precision=HIGHEST)
    pressure = jnp.einsum("gmxy,gmk->kxy", press_x, zblock, precision=HIGHEST)
    upward_grad = (
        jnp.concatenate([pressure[1:] - pressure[:-1], jnp.zeros_like(pressure[:1])], axis=0)
        * CELL_ASPECT
    )
    east_next = interior[0] - east_grad
    north_next = interior[1] - north_grad
    upward_next = upward_star - upward_grad
    arrived = (
        extended_2(droplets, (("gx", 0), ("gy", 1)), 1),
        extended_2(droplet_cell_index.astype(jnp.float32), (("gx", 0), ("gy", 1)), 1),
        extended_2(droplet_block_count.astype(jnp.float32), (("gx", 0), ("gy", 1)), 1),
    )
    moved_in, cells_float, counts_float = jax.tree.map(lambda padded: padded[0::2, 0::2], arrived)
    cells_in = cells_float.astype(jnp.int32)
    counts_in = counts_float.astype(jnp.int32)
    slot_index = lax.broadcasted_iota(jnp.int32, cells_in.shape, 2)
    live_slots = (slot_index < counts_in[:, :, None]).astype(jnp.float32)
    air_values = [
        quantity.reshape(-1)[cells_in]
        for quantity in (east_next, north_next, upward_next, interior[3], interior[4])
    ]
    moved_drops, water_gain = grow_droplets(
        moved_in,
        air_values[0],
        air_values[1],
        air_values[2],
        air_values[3],
        air_values[4],
        live_slots,
    )
    condensed = (
        jnp.zeros((levels * width_x * width_y,), jnp.float32)
        .at[cells_in.reshape(-1)]
        .add(water_gain.reshape(-1))
    )
    condensed = condensed.reshape(levels, width_x, width_y)
    heat_next = interior[3] + HEAT_LOAD * condensed
    moisture_next = interior[4] - MOIST_LOAD * condensed
    return (east_next, north_next, upward_next, heat_next, moisture_next, moved_drops)


def solution(mesh):
    in_specs = (
        P(None, "gx", "gy"),
        P(None, "gx", "gy"),
        P(None, "gx", "gy"),
        P(None, "gx", "gy"),
        P(None, "gx", "gy"),
        P("gx", "gy", None, None),
        P("gx", "gy", None),
        P("gx", "gy"),
    )
    out_specs = (
        P(None, "gx", "gy"),
        P(None, "gx", "gy"),
        P(None, "gx", "gy"),
        P(None, "gx", "gy"),
        P(None, "gx", "gy"),
        P("gx", "gy", None, None),
    )
    return jax.shard_map(
        per_device, mesh=mesh, in_specs=in_specs, out_specs=out_specs, check_vma=False
    )
```

profile of v0, /device:TPU:1, one launch (start us, length us, event | category | flops | bytes accessed | tf_op | source)
XLA Modules:
  0.0 641.2 jit_solution(7965528153281404918)
XLA Ops:
  0.7 1.0 bitcast_dynamic-update-slice_fusion.4
  1.7 0.9 bitcast_dynamic-update-slice_fusion.3
  2.6 0.9 bitcast_dynamic-update-slice_fusion.2
  3.5 0.9 bitcast_dynamic-update-slice_fusion.1
  4.5 0.9 bitcast_dynamic-update-slice_fusion
  5.4 2.1 collective-permute-start
  7.6 3.8 collective-permute-start.1
  11.5 4.8 collective-permute-start.5
  19.4 70.1 %fusion.208 = f32[16,128,2048,1]{2,1,3,0:T(8,128)} fusion(s32[16,128]{1,0:T(8,128)S(1)} %multiply_add_fusion.5), kind=kLoop, calls=%fused_computation.13.clone.clone.clone.1 | loop fusion | flops 67108864 | bytes 16785408 | tf_op jit(solution)/shard_map/kml,syl->skmy/dot_general | solution.py:208
  90.1 4.8 collective-permute-start.9
  95.7 4.2 collective-permute-start.10
  99.9 0.9 collective-permute-done.10
  100.8 3.6 collective-permute-start.11
  104.4 0.8 collective-permute-done.11
  105.4 1.2 collective-permute-start.7
  107.3 5.7 collective-permute-start.13
  114.8 0.8 collective-permute-done.13
  115.6 1.0 fusion.193
  116.6 2.4 collective-permute-start.14
  119.0 2.2 collective-permute-start.15
  121.2 1.2 pad_maximum_fusion.4
  124.0 3.0 collective-permute-start.3
  127.0 1.2 pad_maximum_fusion.1
  128.3 0.9 fusion.195
  129.7 1.5 copy.142
  131.2 2.2 pad_maximum_fusion
  134.4 1.1 pad_maximum_fusion.6
  135.6 5.3 fusion.39
  141.3 51.2 %gather_fusion = f32[9216]{0:T(1024)S(1)} fusion(f32[32768]{0:T(1024)S(1)} %bitcast.205, s32[9216]{0:T(1024)S(1)} %broadcast_clamp_fusion), kind=kCustom, calls=%fused_computation | custom fusion | bytes 110592 | tf_op jit(solution)/shard_map/gather | solution.py:237
  192.5 51.2 %gather_fusion.1 = f32[9216]{0:T(1024)S(1)} fusion(f32[32768]{0:T(1024)S(1)} %bitcast.206, s32[9216]{0:T(1024)S(1)} %broadcast_clamp_fusion), kind=kCustom, calls=%fused_computation.1 | custom fusion | bytes 110592 | tf_op jit(solution)/shard_map/gather | solution.py:237
  243.8 48.7 %scatter_custom_fusion = f32[32768]{0:T(1024)S(1)} fusion(s32[9216]{0:T(1024)} %bitcast.215, f32[9216]{0:T(1024)S(1)} %get-tuple-element.43, f32[]{:T(128)} %constant.55.clone.1), kind=kCustom, calls=%fused_computation.153 | custom fusion | flops 9216 | bytes 131584 | tf_op jit(solution)/shard_map/scatter-add | solution.py:252
  293.9 7.1 %all-to-all-start = ((f32[16,2,8,128]{3,2,1,0:T(8,128)}), f32[16,2,8,128]{3,2,1,0:T(8,128)S(1)}, u32[]{:S(2)}, u32[]{:S(2)}) async-start(f32[16,2,8,128]{3,2,1,0:T(8,128)} %copy.148), calls=%async_computation | async-start | bytes 262144 | tf_op jit(solution)/shard_map/all_to_all | solution.py:101
  301.2 6.6 %all-to-all-done = f32[16,2,8,128]{3,2,1,0:T(8,128)S(1)} async-done(((f32[16,2,8,128]{3,2,1,0:T(8,128)}), f32[16,2,8,128]{3,2,1,0:T(8,128)S(1)}, u32[]{:S(2)}, u32[]{:S(2)}) %all-to-all-start) | async-done | bytes 131104 | tf_op jit(solution)/shard_map/all_to_all | solution.py:101
  307.8 3.3 convolution_bitcast_fusion.2
  311.1 10.7 %all-to-all-start.1 = ((f32[16,8,2,128]{3,1,2,0:T(8,128)}), f32[16,8,2,128]{3,1,2,0:T(8,128)S(1)}, u32[]{:S(2)}, u32[]{:S(2)}) async-start(f32[16,8,2,128]{3,1,2,0:T(8,128)} %convolution_bitcast_fusion.2), calls=%async_computation.1 | async-start | bytes 262144 | tf_op jit(solution)/shard_map/all_to_all | solution.py:105
  321.9 9.0 %all-to-all-done.1 = f32[16,8,2,128]{3,1,2,0:T(8,128)S(1)} async-done(((f32[16,8,2,128]{3,1,2,0:T(8,128)}), f32[16,8,2,128]{3,1,2,0:T(8,128)S(1)}, u32[]{:S(2)}, u32[]{:S(2)}) %all-to-all-start.1) | async-done | bytes 131104 | tf_op jit(solution)/shard_map/all_to_all | solution.py:105
  331.0 77.8 %fusion.22 = f32[8,2,2048,1]{2,0,1,3:T(8,128)S(1)} fusion(f32[16,8,2,128]{3,1,2,0:T(8,128)S(1)} %all-to-all-done.1, s32[16,128]{1,0:T(8,128)S(1)} %multiply_add_fusion.5, f32[2048]{0:T(1024)S(1)} %fusion.122, f32[8,2]{0,1:T(2,128)S(1)} %add_multiply_fusion.7, pred[2048]{0:T(1024)(128)(4,1)S(1)} %copy-done.13, pred[8,2]{0,1:T(4,128)(4,1)S(1)} %copy-done.15), kind=kOutput, calls=%fused_computation.30 | convolution fusion | flops 872611840 | bytes 280656 | tf_op jit(solution)/shard_map/skmy,syl->kml/dot_general | solution.py:197
  408.8 17.3 %fusion.60 = f32[16,8,2,128]{3,1,2,0:T(8,128)} fusion(f32[8,2,2048,1]{2,0,1,3:T(8,128)S(1)} %fusion.22, f32[16,128,2048,1]{2,1,3,0:T(8,128)} %fusion.208), kind=kOutput, calls=%fused_computation.86 | convolution fusion | flops 805306368 | bytes 17039360 | tf_op jit(solution)/shard_map/kml,syl->skmy/dot_general | solution.py:208
  426.1 3.5 all-to-all-start.2
  429.6 1.0 slice.411
  430.7 0.9 slice.412
  432.3 1.7 maximum_subtract_fusion.1
  433.9 4.2 all-to-all-done.2
  438.1 3.6 all-to-all-start.4
  441.8 0.7 copy.169
  443.2 3.3 convolution_bitcast_fusion.1
  446.6 0.9 slice.408
  447.5 0.9 slice.409
  449.1 1.7 all-to-all-done.4
  450.8 3.5 all-to-all-start.6
  454.3 2.6 convolution_bitcast_fusion
  457.7 1.6 maximum_subtract_fusion
  459.3 2.4 all-to-all-done.6
  461.7 4.2 all-to-all-start.5
  466.5 0.7 copy.168
  467.2 5.8 all-to-all-done.5
  473.0 3.5 all-to-all-start.3
  477.8 5.5 all-to-all-done.3
  483.9 0.7 copy.166
  484.7 51.2 %gather_fusion.4 = f32[9216]{0:T(1024)S(1)} fusion(f32[32768]{0:T(1024)S(1)} %bitcast.202, s32[9216]{0:T(1024)S(1)} %broadcast_clamp_fusion), kind=kCustom, calls=%fused_computation.4 | custom fusion | bytes 110592 | tf_op jit(solution)/shard_map/gather | solution.py:237
  535.8 51.2 %gather_fusion.3 = f32[9216]{0:T(1024)S(1)} fusion(f32[32768]{0:T(1024)S(1)} %bitcast.203, s32[9216]{0:T(1024)S(1)} %broadcast_clamp_fusion), kind=kCustom, calls=%fused_computation.3 | custom fusion | bytes 110592 | tf_op jit(solution)/shard_map/gather | solution.py:237
  587.0 51.2 %gather_fusion.2 = f32[9216]{0:T(1024)S(1)} fusion(f32[32768]{0:T(1024)S(1)} %bitcast.204, s32[9216]{0:T(1024)S(1)} %broadcast_clamp_fusion), kind=kCustom, calls=%fused_computation.2 | custom fusion | bytes 110592 | tf_op jit(solution)/shard_map/gather | solution.py:237
  638.7 1.1 stack.36
  640.0 1.0 copy.171
  (128 shorter events, 18.6 us)
Async XLA Ops:
  0.6 10.7 %copy-start.8 = (s32[3,3,1024]{2,1,0:T(4,128)S(1)}, s32[3,3,1024]{2,1,0:T(4,128)}, u32[]{:S(2)}) copy-start(s32[3,3,1024]{2,1,0:T(4,128)} %param.14) | copy-start | bytes 110596
  0.6 15.6 %copy-start.12 = (s32[3,3]{1,0:T(4,128)S(1)}, s32[3,3]{1,0:T(4,128)}, u32[]{:S(2)}) copy-start(s32[3,3]{1,0:T(4,128)} %param.15) | copy-start | bytes 112
  0.7 18.4 %copy-start.4 = (f32[3,3,10,1024]{3,1,2,0:T(4,128)S(1)}, f32[3,3,10,1024]{3,1,2,0:T(4,128)}, u32[]{:S(2)}) copy-start(f32[3,3,10,1024]{3,1,2,0:T(4,128)} %param.13) | copy-start | bytes 1105924
  5.4 115.8 %collective-permute-start = (f32[5,32,4,128]{3,1,2,0:T(8,128)S(1)}, f32[5,32,4,128]{3,1,2,0:T(8,128)}, u32[]{:S(2)}, u32[]{:S(2)}) collective-permute-start(f32[5,32,4,128]{3,1,2,0:T(8,128)S(1)} %get-tuple-element.64), channel_id=1, source_target_pairs={{0,16},{16,32},{32,48},{48,64},{64,80},{80,96},{96,112},{112,128},... | collective-permute-start | bytes 983048 | tf_op jit(solution)/shard_map/ppermute | solution.py:29
  7.6 113.6 %collective-permute-start.1 = (f32[5,32,4,128]{3,1,2,0:T(8,128)S(1)}, f32[5,32,4,128]{3,1,2,0:T(8,128)}, u32[]{:S(2)}, u32[]{:S(2)}) collective-permute-start(f32[5,32,4,128]{3,1,2,0:T(8,128)S(1)} %get-tuple-element.65), channel_id=1, source_target_pairs={{16,0},{32,16},{48,32},{64,48},{80,64},{96,80},{112,96},{128,112},... | collective-permute-start | bytes 983048 | tf_op jit(solution)/shard_map/ppermute | solution.py:32
  11.4 94.0 %collective-permute-start.4 = (f32[1,3,1024]{2,1,0:T(4,128)S(1)}, f32[1,3,1024]{2,1,0:T(4,128)S(1)}, u32[]{:S(2)}, u32[]{:S(2)}) collective-permute-start(f32[1,3,1024]{2,1,0:T(4,128)S(1)} %get-tuple-element.82), channel_id=1, source_target_pairs={{0,16},{16,32},{32,48},{48,64},{64,80},{80,96},{96,112},{112,128},... | collective-permute-start | bytes 36872 | tf_op jit(solution)/shard_map/ppermute | solution.py:29
  11.5 93.9 %collective-permute-start.5 = (f32[1,3,1024]{2,1,0:T(4,128)S(1)}, f32[1,3,1024]{2,1,0:T(4,128)S(1)}, u32[]{:S(2)}, u32[]{:S(2)}) collective-permute-start(f32[1,3,1024]{2,1,0:T(4,128)S(1)} %get-tuple-element.83), channel_id=1, source_target_pairs={{16,0},{32,16},{48,32},{64,48},{80,64},{96,80},{112,96},{128,112},... | collective-permute-start | bytes 36872 | tf_op jit(solution)/shard_map/ppermute | solution.py:32
  16.3 73.8 %collective-permute-start.8 = (f32[1,3]{1,0:T(1,128)S(1)}, f32[1,3]{1,0:T(1,128)S(1)}, u32[]{:S(2)}, u32[]{:S(2)}) collective-permute-start(f32[1,3]{1,0:T(1,128)S(1)} %get-tuple-element.88), channel_id=1, source_target_pairs={{0,16},{16,32},{32,48},{48,64},{64,80},{80,96},{96,112},{112,128},... | collective-permute-start | bytes 44 | tf_op jit(solution)/shard_map/ppermute | solution.py:29
  90.1 5.5 collective-permute-start.9
  95.7 5.1 collective-permute-start.10
  100.8 4.4 collective-permute-start.11
  105.2 9.4 %collective-permute-start.12 = (f32[1,3,10,1024]{3,2,1,0:T(8,128)S(1)}, f32[1,3,10,1024]{3,2,1,0:T(8,128)S(1)}, u32[]{:S(2)}, u32[]{:S(2)}) collective-permute-start(f32[1,3,10,1024]{3,2,1,0:T(8,128)S(1)} %copy.213), channel_id=1, source_target_pairs={{0,16},{16,32},{32,48},{48,64},{64,80},{80,96},{96,112},{112,128},... | collective-permute-start | bytes 368648 | tf_op jit(solution)/shard_map/ppermute | solution.py:29
  105.4 1.9 collective-permute-start.6
  105.4 7.6 %collective-permute-start.7 = (f32[5,1,1024]{2,1,0:T(1,128)S(1)}, f32[5,1,1024]{2,1,0:T(1,128)S(1)}, u32[]{:S(2)}, u32[]{:S(2)}) collective-permute-start(f32[5,1,1024]{2,1,0:T(1,128)S(1)} %get-tuple-element.81), channel_id=1, source_target_pairs={{1,0},{2,1},{3,2},{4,3},{5,4},{6,5},{7,6},{8,7},{9,8},{10,9},{11,1... | collective-permute-start | bytes 61448 | tf_op jit(solution)/shard_map/ppermute | solution.py:32
  107.3 8.3 %collective-permute-start.13 = (f32[1,3,10,1024]{3,2,1,0:T(8,128)S(1)}, f32[1,3,10,1024]{3,2,1,0:T(8,128)S(1)}, u32[]{:S(2)}, u32[]{:S(2)}) collective-permute-start(f32[1,3,10,1024]{3,2,1,0:T(8,128)S(1)} %copy.214), channel_id=1, source_target_pairs={{16,0},{32,16},{48,32},{64,48},{80,64},{96,80},{112,96},{128,112},... | collective-permute-start | bytes 368648 | tf_op jit(solution)/shard_map/ppermute | solution.py:32
  115.6 5.6 copy-start
  116.6 10.4 %collective-permute-start.14 = (f32[5,1,10,1024]{3,2,1,0:T(8,128)}, f32[5,1,10,1024]{3,2,1,0:T(8,128)}, u32[]{:S(2)}, u32[]{:S(2)}) collective-permute-start(f32[5,1,10,1024]{3,2,1,0:T(8,128)} %get-tuple-element.62), channel_id=1, source_target_pairs={{0,1},{1,2},{2,3},{3,4},{4,5},{5,6},{6,7},{7,8},{8,9},{9,10},{10,1... | collective-permute-start | bytes 614408 | tf_op jit(solution)/shard_map/ppermute | solution.py:29
  119.0 8.0 %collective-permute-start.15 = (f32[5,1,10,1024]{3,2,1,0:T(8,128)}, f32[5,1,10,1024]{3,2,1,0:T(8,128)}, u32[]{:S(2)}, u32[]{:S(2)}) collective-permute-start(f32[5,1,10,1024]{3,2,1,0:T(8,128)} %get-tuple-element.63), channel_id=1, source_target_pairs={{1,0},{2,1},{3,2},{4,3},{5,4},{6,5},{7,6},{8,7},{9,8},{10,9},{11,1... | collective-permute-start | bytes 614408 | tf_op jit(solution)/shard_map/ppermute | solution.py:32
  123.4 3.6 copy-start.1
  123.4 5.7 collective-permute-start.2
  124.0 5.7 collective-permute-start.3
  128.3 1.4 copy-start.2
  192.4 51.2 %copy-start.5 = (f32[3,3,1,1024]{3,2,1,0:T(1,128)S(1)}, f32[3,3,1,1024]{3,2,1,0:T(1,128)}, u32[]{:S(2)}) copy-start(f32[3,3,1,1024]{3,2,1,0:T(1,128)} %get-tuple-element.73) | copy-start | bytes 110596
  192.4 51.2 %copy-start.6 = (f32[3,3,1,1024]{3,2,1,0:T(1,128)S(1)}, f32[3,3,1,1024]{3,2,1,0:T(1,128)}, u32[]{:S(2)}) copy-start(f32[3,3,1,1024]{3,2,1,0:T(1,128)} %get-tuple-element.74) | copy-start | bytes 110596
  192.5 51.2 %copy-start.7 = (f32[3,3,1,1024]{3,2,1,0:T(1,128)S(1)}, f32[3,3,1,1024]{3,2,1,0:T(1,128)}, u32[]{:S(2)}) copy-start(f32[3,3,1,1024]{3,2,1,0:T(1,128)} %get-tuple-element.75) | copy-start | bytes 110596
  192.5 100.1 %copy-start.14 = (pred[32]{0:T(512)(128)(4,1)S(1)}, pred[32]{0:T(512)(128)(4,1)}, u32[]{:S(2)}) copy-start(pred[32]{0:T(512)(128)(4,1)} %iota_compare_fusion.2) | copy-start | bytes 100
  243.6 49.1 %copy-start.9 = (f32[16,2]{0,1:T(2,128)S(1)}, f32[16,2]{0,1:T(2,128)}, u32[]{:S(2)}) copy-start(f32[16,2]{0,1:T(2,128)} %compare_select_fusion.6) | copy-start | bytes 388
  243.7 49.1 %copy-start.10 = (s32[16,2]{0,1:T(2,128)S(1)}, s32[16,2]{0,1:T(2,128)}, u32[]{:S(2)}) copy-start(s32[16,2]{0,1:T(2,128)} %multiply_add_fusion.7) | copy-start | bytes 388
  243.7 49.1 %copy-start.11 = (s32[32]{0:T(128)S(1)}, s32[32]{0:T(128)}, u32[]{:S(2)}) copy-start(s32[32]{0:T(128)} %multiply_add_fusion.8) | copy-start | bytes 388
  293.9 13.9 %all-to-all-start = ((f32[16,2,8,128]{3,2,1,0:T(8,128)}), f32[16,2,8,128]{3,2,1,0:T(8,128)S(1)}, u32[]{:S(2)}, u32[]{:S(2)}) async-start(f32[16,2,8,128]{3,2,1,0:T(8,128)} %copy.148), calls=%async_computation | async-start | bytes 262144 | tf_op jit(solution)/shard_map/all_to_all | solution.py:101
  301.2 29.8 %copy-start.13 = (pred[2048]{0:T(1024)(128)(4,1)S(1)}, pred[2048]{0:T(1024)(128)(4,1)}, u32[]{:S(2)}) copy-start(pred[2048]{0:T(1024)(128)(4,1)} %iota_compare_fusion.1) | copy-start | bytes 6148
  301.2 29.8 %copy-start.15 = (pred[8,2]{0,1:T(4,128)(4,1)S(1)}, pred[8,2]{0,1:T(4,128)(4,1)}, u32[]{:S(2)}) copy-start(pred[8,2]{0,1:T(4,128)(4,1)} %broadcast_and_fusion) | copy-start | bytes 52
  311.1 19.9 %all-to-all-start.1 = ((f32[16,8,2,128]{3,1,2,0:T(8,128)}), f32[16,8,2,128]{3,1,2,0:T(8,128)S(1)}, u32[]{:S(2)}, u32[]{:S(2)}) async-start(f32[16,8,2,128]{3,1,2,0:T(8,128)} %convolution_bitcast_fusion.2), calls=%async_computation.1 | async-start | bytes 262144 | tf_op jit(solution)/shard_map/all_to_all | solution.py:105
  426.1 15.7 %copy-start.3 = (f32[3,3,10,1024]{3,2,1,0:T(8,128)S(1)}, f32[3,3,10,1024]{3,2,1,0:T(8,128)}, u32[]{:S(2)}) copy-start(f32[3,3,10,1024]{3,2,1,0:T(8,128)} %copy-done.2) | copy-start | bytes 1105924
  426.1 12.0 %all-to-all-start.2 = ((f32[16,8,2,128]{3,1,2,0:T(8,128)}), f32[16,8,2,128]{3,1,2,0:T(8,128)S(1)}, u32[]{:S(2)}, u32[]{:S(2)}) async-start(f32[16,8,2,128]{3,1,2,0:T(8,128)} %fusion.60), calls=%async_computation.2 | async-start | bytes 262144 | tf_op jit(solution)/shard_map/all_to_all | solution.py:105
  438.1 12.7 %all-to-all-start.4 = ((f32[16,8,2,128]{3,1,2,0:T(8,128)}), f32[16,8,2,128]{3,1,2,0:T(8,128)S(1)}, u32[]{:S(2)}, u32[]{:S(2)}) async-start(f32[16,8,2,128]{3,1,2,0:T(8,128)} %maximum_subtract_fusion.1), calls=%async_computation.4 | async-start | bytes 262144 | tf_op jit(solution)/shard_map/all_to_all | solution.py:105
  450.8 10.9 %all-to-all-start.6 = ((f32[16,2,8,128]{3,2,1,0:T(8,128)}), f32[16,2,8,128]{3,2,1,0:T(8,128)S(1)}, u32[]{:S(2)}, u32[]{:S(2)}) async-start(f32[16,2,8,128]{3,2,1,0:T(8,128)} %convolution_bitcast_fusion.1), calls=%async_computation.6 | async-start | bytes 262144 | tf_op jit(solution)/shard_map/all_to_all | solution.py:101
  461.7 11.3 %all-to-all-start.5 = ((f32[16,2,8,128]{3,1,2,0:T(2,128)}), f32[16,2,8,128]{3,1,2,0:T(2,128)S(1)}, u32[]{:S(2)}, u32[]{:S(2)}) async-start(f32[16,2,8,128]{3,1,2,0:T(2,128)} %copy.153), calls=%async_computation.5 | async-start | bytes 262144 | tf_op jit(solution)/shard_map/all_to_all | solution.py:101
  473.0 10.4 %all-to-all-start.3 = ((f32[16,2,8,128]{3,2,1,0:T(8,128)}), f32[16,2,8,128]{3,2,1,0:T(8,128)S(1)}, u32[]{:S(2)}, u32[]{:S(2)}) async-start(f32[16,2,8,128]{3,2,1,0:T(8,128)} %maximum_subtract_fusion), calls=%async_computation.3 | async-start | bytes 262144 | tf_op jit(solution)/shard_map/all_to_all | solution.py:101
where the time goes:
time: 649 us; the launch traced here: 641 us
  local copies, waits for them, and re-layouts  280 us (43%)
  other arithmetic  140 us (22%)
  matrix products  106 us (16%)
  starting transfers between devices  74.1 us (11%)
  waiting for transfers between devices  39.6 us (6%)
    gather x5, local copies, waits for them, and re-layouts, per_device(): quantity.reshape(-1)[cells_in]  256 us
    dot_general x1, matrix products, per_device(): full_hat = jnp.einsum('skmy,syl->kml', spectrum, ytable, precision=HIGHEST)  77.8 us
    dot_general x1, other arithmetic, per_device(): jnp.einsum('kml,syl->skmy', pressure_hat, ytable, precision=HIGHEST)  70.1 us
    scatter-add x1, other arithmetic, per_device(): condensed = jnp.zeros((levels * width_x * width_y,), jnp.float32).at[cell...  48.7 us
    ppermute x8, starting transfers between devices, extended_2(): lax.ppermute(lax.slice_in_dim(block, 0, width, axis=dim), axis, backward)  29 us
    all_to_all x4, waiting for transfers between devices, across_x(): return lax.all_to_all(blocks, 'gx', split_axis=0, concat_axis=0, tiled=True)  20.4 us
    all_to_all x4, starting transfers between devices, across_x(): return lax.all_to_all(blocks, 'gx', split_axis=0, concat_axis=0, tiled=True)  18.3 us
    all_to_all x3, starting transfers between devices, across_y(): return lax.all_to_all(blocks, 'gy', split_axis=0, concat_axis=0, tiled=True)  17.9 us
  transfers between devices with their start and end apart: 23, of which 13 were waited for; matrix products, arithmetic and copies ran while one was open for 16% of the time, Pallas kernels for 0%

commit v1 on v0

v1 whole, which is shorter than its diff:
```python
import math

import jax
import jax.numpy as jnp
import numpy as np
from jax import lax
from jax.experimental import pallas as pl
from jax.experimental.pallas import tpu as pltpu
from jax.sharding import PartitionSpec as P

DT = 0.2
RELAX_TIME = 0.2
GROWTH = 0.5
CURVATURE = 0.1
SOLUTE_EFFECT = 0.05
RADIUS_FLOOR = 0.3
SATURATION_RATE = 0.1
MOIST_LOAD = 0.5
HEAT_LOAD = 1.25
ASPECT = 0.0625
HIGHEST = lax.Precision.HIGHEST

NZ = 32
NX = 8
NY = 128
GX = 16
GY = 16
TX = NX * GX
TY = NY * GY
CAP = 1024
ROWS = NZ * NX
SLOT = 12
BLK = 2 * SLOT
F32 = jnp.float32
BF16 = jnp.bfloat16


def make_tables():
    m = np.arange(NZ)
    ztab = np.cos(np.pi * m[:, None] * (2 * m[None, :] + 1) / (2 * NZ)) * np.where(
        m[:, None] == 0, math.sqrt(1.0 / NZ), math.sqrt(2.0 / NZ)
    )
    zdiff = np.zeros((NZ, NZ))
    zdiff[:-1] = (ztab.T[1:] - ztab.T[:-1]) * ASPECT
    zback = np.concatenate([ztab.T, zdiff], axis=0)
    p = np.arange(TX)

    def cas(a):
        return np.cos(a) + np.sin(a)

    w = 2 * np.pi / TX
    har = cas(w * (p[:, None] * p[None, :] % TX)) / math.sqrt(TX)
    wmain = np.zeros((2, TX, GX, 2, SLOT))
    for X in range(GX):
        for t in range(NX + 1):
            for b in range(2):
                wmain[b, :, X, b, t] = har[:, (NX * X + t) % TX]
    wmain = wmain.reshape(2 * TX, GX * BLK)
    X = np.arange(GX)
    t12 = np.concatenate(
        [cas(w * p[:, None] * NX * X[None, :]), cas(-w * p[:, None] * NX * X[None, :])], axis=0
    ) / math.sqrt(TX)
    lane = np.arange(NY)
    cosx = np.where(lane[None, :] < NX, np.cos(w * p[:, None] * lane[None, :]), 0.0)
    sinx = np.where(lane[None, :] < NX, np.sin(w * p[:, None] * lane[None, :]), 0.0)
    cs = np.concatenate([cosx, sinx], axis=0)
    lam = (
        (2 - 2 * np.cos(np.pi * m[:, None] / NZ)) + (2 - 2 * np.cos(w * p[None, :]))
    ) * ASPECT
    zero = lam <= 0
    lam = np.where(zero, 0.5, lam)
    lnr = -2.0 * np.arcsinh(np.sqrt(lam) / 2.0)
    coef = np.where(zero, 0.0, -1.0 / (2.0 * np.sinh(-lnr)))
    lnr = lnr.reshape(2, GX, TX).transpose(1, 0, 2).reshape(GX, 2 * TX)
    coef = coef.reshape(2, GX, TX).transpose(1, 0, 2).reshape(GX, 2 * TX)
    rpow = np.exp(lnr[:, :, None] * lane)
    rrev = np.exp(lnr[:, :, None] * (NY - lane))
    misc = np.zeros((GX, 2 * TX, NY))
    for k in range(8):
        misc[:, :, k] = np.exp(lnr * (1 << k))
    misc[:, :, 8] = coef
    rowtab = np.zeros((GX, 8, 2 * TX))
    rowtab[:, 0] = NY * lnr
    rowtab[:, 1] = 1.0 / (1.0 - np.exp(lnr * TY))
    absd = np.abs(lane[:, None] - lane[None, :])

    def f(a):
        return jnp.asarray(np.asarray(a, np.float32))

    return dict(
        ztab=f(ztab),
        zback=f(zback),
        wmain=f(wmain),
        wback=f(wmain.T),
        t12=f(t12),
        t12t=f(t12.T),
        cs=f(cs),
        rpow=f(rpow),
        rrev=f(rrev),
        misc=f(misc),
        rowtab=f(rowtab),
        absd=f(absd),
    )


def iota(shape, dim):
    return lax.broadcasted_iota(jnp.int32, shape, dim)


def dot(a, b):
    return jnp.dot(a, b, precision=HIGHEST, preferred_element_type=F32)


def row_of(ref, x):
    return ref[pl.ds(x, NZ, stride=NX), :]


def pair_of(f0, lo, hi):
    d1, d2, d3 = (h - l for l, h in zip(lo, hi))
    s1, s2, s3 = (h + l for l, h in zip(lo, hi))
    return (45.0 * d1 - 9.0 * d2 + d3, 20.0 * f0 - 15.0 * s1 + 6.0 * s2 - s3)


def star_row(x, rows, ylo, yhi, slot, velocity, zs, lane):
    f0 = rows[x + 3]
    zs[8 : 8 + NZ, :] = f0
    zs[0:8, :] = jnp.broadcast_to(f0[0:1], (8, NY))
    zs[8 + NZ : 16 + NZ, :] = jnp.broadcast_to(f0[NZ - 1 : NZ], (8, NY))
    au, bu, av, bv, aw, bw = velocity
    a, b = pair_of(
        f0, [rows[x + 3 - k] for k in (1, 2, 3)], [rows[x + 3 + k] for k in (1, 2, 3)]
    )
    total = au * a + bu * b
    where_lo = 16 * x + 3 * slot
    halo = jnp.where(
        lane >= 64,
        pltpu.roll(ylo, (125 - where_lo) % NY, 1),
        pltpu.roll(yhi, (NY - where_lo) % NY, 1),
    )
    lo = [pltpu.roll(jnp.where(lane >= NY - k, halo, f0), k, 1) for k in (1, 2, 3)]
    hi = [pltpu.roll(jnp.where(lane < k, halo, f0), NY - k, 1) for k in (1, 2, 3)]
    a, b = pair_of(f0, lo, hi)
    total = total + (av * a + bv * b)
    a, b = pair_of(
        f0,
        [zs[8 - k : 8 - k + NZ, :] for k in (1, 2, 3)],
        [zs[8 + k : 8 + k + NZ, :] for k in (1, 2, 3)],
    )
    return f0 - (total + (aw * a + bw * b))


def velocity_rows(u, v, w, x):
    out = []
    for ref in (u, v, w):
        a = row_of(ref, x) * (DT / 60.0)
        out += [a, jnp.abs(a)]
    return out


def yhalo_of(msg):
    return jnp.concatenate([msg[40:48, g * NY : (g + 1) * NY] for g in range(4)], axis=0)


def pack_blocks(out, blocks):
    for n, (drops, cells, count) in enumerate(blocks):
        out[n * SLOT : n * SLOT + 10, :] = drops
        out[n * SLOT + 10 : n * SLOT + 11, :] = cells
        out[n * SLOT + 11 : n * SLOT + 12, :] = count
    out[36:40, :] = jnp.zeros((4, CAP), F32)


def own_block(drops, cells, counts, n):
    return (
        drops[n],
        cells[n : n + 1, :].astype(F32),
        jnp.full((1, CAP), counts[n], jnp.int32).astype(F32),
    )


def pack_kernel(u, v, w, h, q, drops, cells, counts, xlo, xhi, up, down):
    for f, ref in enumerate((u, v, w)):
        for i in range(3):
            n = f * 3 + i
            xlo[n * NZ : (n + 1) * NZ, :] = row_of(ref, 5 + i)
            xhi[n * NZ : (n + 1) * NZ, :] = row_of(ref, i)
    lane = iota((NZ, NY), 1)
    tlo = jnp.zeros((NZ, NY), F32)
    thi = jnp.zeros((NZ, NY), F32)
    for x in range(NX):
        for f, ref in enumerate((u, v, w, h, q)):
            at = 16 * x + 3 * f
            row = row_of(ref, x)
            mask = (lane >= at) & (lane < at + 3)
            tlo = jnp.where(mask, pltpu.roll(row, (at - 125) % NY, 1), tlo)
            thi = jnp.where(mask, pltpu.roll(row, at, 1), thi)
    for out, tile, s in ((up, tlo, 2), (down, thi, 0)):
        pack_blocks(out, [own_block(drops, cells, counts, r * 3 + s) for r in range(3)])
        for g in range(4):
            out[40:48, g * NY : (g + 1) * NY] = tile[g * 8 : (g + 1) * 8]
        out[40:48, 4 * NY :] = jnp.zeros((8, 4 * NY), F32)


def block_of(msg, n):
    return (
        msg[n * SLOT : n * SLOT + 10, :],
        msg[n * SLOT + 10 : n * SLOT + 11, :],
        msg[n * SLOT + 11 : n * SLOT + 12, :],
    )


def relay_kernel(h, q, drops, cells, counts, mlo, mhi, up, down):
    for out, r, x0 in ((up, 2, 5), (down, 0, 0)):
        pack_blocks(
            out,
            [block_of(mlo, r), own_block(drops, cells, counts, r * 3 + 1), block_of(mhi, r)],
        )
        for f, ref in enumerate((h, q)):
            for i in range(3):
                row = row_of(ref, x0 + i)
                for g in range(4):
                    n = (f * 3 + i) * 4 + g
                    a, c = 40 + 8 * (n // 8), NY * (n % 8)
                    out[a : a + 8, c : c + NY] = row[g * 8 : (g + 1) * 8]


def wind_kernel(u, v, w, xlo, xhi, mlo, mhi, ztab, stars, send, zs):
    lane = iota((NZ, NY), 1)
    level = iota((NZ, NY), 0)
    ylo = yhalo_of(mlo)
    yhi = yhalo_of(mhi)
    vel = [velocity_rows(u, v, w, x) for x in range(NX)]
    for f, ref in enumerate((u, v, w)):
        rows = [xlo[(f * 3 + i) * NZ : (f * 3 + i + 1) * NZ, :] for i in range(3)]
        rows += [row_of(ref, x) for x in range(NX)]
        rows += [xhi[(f * 3 + i) * NZ : (f * 3 + i + 1) * NZ, :] for i in range(3)]
        for x in range(NX):
            star = star_row(x, rows, ylo, yhi, f, vel[x], zs.at[f * NX + x], lane)
            if f == 2:
                star = jnp.where(level == NZ - 1, 0.0, star)
            at = (f * NX + x) * NZ
            stars[at : at + NZ, :] = star
    tiles = []
    ext = jnp.zeros((NZ, NY), F32)
    for x in range(NX):
        east = stars[x * NZ : (x + 1) * NZ, :]
        north = stars[(NX + x) * NZ : (NX + x + 1) * NZ, :]
        rise = stars[(2 * NX + x) * NZ : (2 * NX + x + 1) * NZ, :]
        d = east + north + rise
        if x > 0:
            d = d - stars[(x - 1) * NZ : x * NZ, :]
        d = d - jnp.where(lane == 0, 0.0, pltpu.roll(north, 1, 1))
        d = d - jnp.where(level == 0, 0.0, pltpu.roll(rise, 1, 0))
        tiles.append(d)
        ext = jnp.where(lane == x, -pltpu.roll(north, (x + 1) % NY, 1), ext)
    tiles.append(-stars[(NX - 1) * NZ : NX * NZ, :])
    tiles.append(ext)
    hat = dot(ztab[...], jnp.concatenate(tiles, axis=1))
    zeros = jnp.zeros((GX, NY), F32)
    for b in range(2):
        for t in range(SLOT):
            if t < NX + 2:
                val = hat[b * GX : (b + 1) * GX, t * NY : (t + 1) * NY]
            else:
                val = zeros
            send[pl.ds(b * SLOT + t, GX, stride=BLK), :] = val


def scan_kernel(sx, recv, wmain, t12, cs, rrev, misc, absd, msg, keep, cols, kink):
    lane = iota((2 * TX, NY), 1)
    d = dot(wmain[...], recv[...])
    ends = []
    for b in range(2):
        e16 = recv[pl.ds(b * SLOT + NX + 1, GX, stride=BLK), :]
        prod = dot(t12[...], e16) * cs[...]
        ends.append(jnp.sum(prod[:TX] + prod[TX:], axis=1, keepdims=True))
    e = jnp.concatenate(ends, axis=0)
    fwd = d
    bwd = d
    for k in range(7):
        s = 1 << k
        a = jnp.broadcast_to(misc[0, :, k : k + 1], (2 * TX, NY))
        fwd = fwd + jnp.where(lane >= s, a * pltpu.roll(fwd, s, 1), 0.0)
        bwd = bwd + jnp.where(lane < NY - s, a * pltpu.roll(bwd, NY - s, 1), 0.0)
    r1 = misc[0, :, 0:1]
    r128 = misc[0, :, 7:8]
    out_right = r1 * fwd[:, NY - 1 : NY] + e
    out_left = bwd[:, 0:1] + r128 * e
    keep[...] = fwd + bwd - d + rrev[0] * e
    table = jnp.where(lane == 0, out_right, jnp.where(lane == 1, out_left, 0.0))
    d8 = d[0:8]
    e8 = e[0:8]
    lane8 = iota((8, NY), 1)
    lanef = lane8.astype(F32)
    s0 = jnp.sum(d8, axis=1, keepdims=True) + e8
    s1 = jnp.sum(d8 * lanef, axis=1, keepdims=True) + float(NY) * e8
    top = jnp.where(lane8 == 2, s0, jnp.where(lane8 == 3, s1, table[0:8]))
    table = jnp.concatenate([top, table[8:]], axis=0)
    cols[...] = table
    turned = table.T[0:8]
    for y in range(GY):
        msg[y * 8 : (y + 1) * 8, :] = turned
    kink[...] = dot(d8, absd[...]) + e8 * (float(NY) - lanef)


def solve_kernel(sx, got, keep, cols, kink, wback, t12t, cs, rpow, rrev, misc, rowtab, send):
    here = sx[1]
    first = (sx[0] == 0).astype(F32)
    who = iota((GY, 2 * TX), 0)
    all_right = jnp.concatenate([got[y * 8 : y * 8 + 1, :] for y in range(GY)], axis=0)
    all_left = jnp.concatenate([got[y * 8 + 1 : y * 8 + 2, :] for y in range(GY)], axis=0)
    s0 = jnp.concatenate([got[y * 8 + 2 : y * 8 + 3, 0:1] for y in range(GY)], axis=0)
    s1 = jnp.concatenate([got[y * 8 + 3 : y * 8 + 4, 0:1] for y in range(GY)], axis=0)
    lnr = rowtab[0, 0:1, :]
    inv = rowtab[0, 1:2, :]
    after = ((here - who - 1) & (GY - 1)).astype(F32)
    before = ((who - here - 1) & (GY - 1)).astype(F32)
    in_left = jnp.sum(jnp.exp(after * lnr) * all_right, axis=0, keepdims=True) * inv
    in_right = jnp.sum(jnp.exp(before * lnr) * all_left, axis=0, keepdims=True) * inv
    row = iota((8, 2 * TX), 0)
    turned = jnp.where(row == 0, in_left, jnp.where(row == 1, in_right, 0.0)).T
    in_left = turned[:, 0:1]
    in_right = turned[:, 1:2]
    coef = misc[0, :, 8:9]
    pres = coef * (keep[...] + rpow[0] * in_left + rrev[0] * in_right)
    edge = coef * (cols[:, 0:1] + misc[0, :, 7:8] * in_left + in_right)
    who1 = iota((GY, 1), 0)
    far = (NY * ((here - who1) & (GY - 1))).astype(F32)
    mine = who1 == here
    sum0 = jnp.sum(s0, axis=0, keepdims=True)
    own0 = jnp.sum(jnp.where(mine, s0, 0.0), axis=0, keepdims=True)
    own1 = jnp.sum(jnp.where(mine, s1, 0.0), axis=0, keepdims=True)
    lin = 0.5 * (sum0 - own0) + jnp.sum(s1 - far * s0, axis=0, keepdims=True) * (1.0 / TY)
    quad = sum0 * (0.5 / TY)
    lanef = iota((8, NY), 1).astype(F32)
    top = 0.5 * kink[...] + lanef * (lin - lanef * quad)
    edge0 = 0.5 * (float(NY) * own0 - own1) + float(NY) * (lin - float(NY) * quad)
    row8 = iota((8, NY), 0)
    top = pres[0:8] + jnp.where(row8 == 0, first * top, 0.0)
    pres = jnp.concatenate([top, pres[8:]], axis=0)
    row1 = iota((2 * TX, 1), 0)
    edge = edge + jnp.where(row1 == 0, first * edge0, 0.0)
    send[...] = dot(wback[...], pres)
    for b in range(2):
        eb = edge[b * TX : (b + 1) * TX]
        spread = jnp.concatenate([cs[0:TX, :] * eb, cs[TX:, :] * eb], axis=0)
        send[pl.ds(b * SLOT + NX + 1, GX, stride=BLK), :] = dot(t12t[...], spread)


def store_table(lhs, n, table):
    turned = table.T
    hi = turned.astype(BF16)
    lhs[n * NY : (n + 1) * NY, :] = hi
    lhs[(n + 1) * NY : (n + 2) * NY, :] = (turned - hi.astype(F32)).astype(BF16)


def masks_of(cells):
    width = cells.shape[1]
    rowid = ((cells >> 7) & (NX - 1)) * NZ + (cells >> 10)
    hot = jnp.where(iota((ROWS, width), 0) == rowid, 1.0, 0.0).astype(BF16)
    pick = iota((NY, width), 0) == (cells & (NY - 1))
    return hot, pick


def gather_one(lhs, n, hot, pick):
    hi = jnp.dot(lhs[n * NY : (n + 1) * NY, :], hot, preferred_element_type=F32)
    lo = jnp.dot(lhs[(n + 1) * NY : (n + 2) * NY, :], hot, preferred_element_type=F32)
    return jnp.sum(jnp.where(pick, hi + lo, 0.0), axis=0, keepdims=True)


CHUNK = 512


def drop_kernel(
    u, v, w, h, q, mlo, mhi, clo, chi, drops, cells, counts,
    heat_next, moist_next, cell_out, state, zs, stars, lhs, acc, air,
):
    lane = iota((NZ, NY), 1)
    ylo = yhalo_of(mlo)
    yhi = yhalo_of(mhi)
    vel = [velocity_rows(u, v, w, x) for x in range(NX)]

    def side(msg, n):
        parts = []
        for g in range(4):
            k = n * 4 + g
            a, c = 40 + 8 * (k // 8), NY * (k % 8)
            parts.append(msg[a : a + 8, c : c + NY])
        return jnp.concatenate(parts, axis=0)

    for f, ref in enumerate((h, q)):
        rows = [side(clo, f * 3 + i) for i in range(3)]
        rows += [row_of(ref, x) for x in range(NX)]
        rows += [side(chi, f * 3 + i) for i in range(3)]
        for x in range(NX):
            star = star_row(x, rows, ylo, yhi, 3 + f, vel[x], zs.at[f * NX + x], lane)
            at = (f * NX + x) * NZ
            stars[at : at + NZ, :] = star
        store_table(lhs, 2 * f, stars[f * ROWS : (f + 1) * ROWS, :])
    for r in range(3):
        for s in range(3):
            n = r * 3 + s
            if r == 0:
                block = block_of(clo, s)
            elif r == 2:
                block = block_of(chi, s)
            elif s == 0:
                block = block_of(mlo, 1)
            elif s == 2:
                block = block_of(mhi, 1)
            else:
                block = own_block(drops, cells, counts, 4)
            values, cell, count = block
            for a in range(10):
                state[a, n : n + 1, :] = values[a : a + 1]
            cell_out[n : n + 1, :] = cell.astype(jnp.int32)
            slot = iota((1, CAP), 1).astype(F32)
            state[10, n : n + 1, :] = jnp.where(slot < count, 1.0, 0.0)

    def gather_block(n, carry):
        for c in range(CAP // CHUNK):
            at = c * CHUNK
            hot, pick = masks_of(cell_out[pl.ds(n, 1), at : at + CHUNK])
            for f in range(2):
                air[f, pl.ds(n, 1), at : at + CHUNK] = gather_one(lhs, 2 * f, hot, pick)
        return carry

    lax.fori_loop(0, 9, gather_block, 0)
    live = state[10]
    radius = state[6]
    cubed = radius * radius * radius
    keeping = jnp.exp(-DT / (RELAX_TIME * radius * radius))
    saturation = air[1] * jnp.exp(-SATURATION_RATE * air[0]) - 1.0
    squared = radius * radius + GROWTH * (
        saturation - CURVATURE / radius + SOLUTE_EFFECT * state[8] / cubed
    )
    new_radius = jnp.sqrt(jnp.maximum(squared, RADIUS_FLOOR * RADIUS_FLOOR))
    gain = live * state[7] * (new_radius * new_radius * new_radius - cubed)
    air[0] = gain
    state[6] = new_radius * live
    state[7] = state[7] * live
    state[8] = state[8] * live
    state[9] = (state[9] + DT) * live
    for a in range(3):
        state[a] = state[a] * live
        state[3 + a] = state[3 + a] * (keeping * live)
    state[10] = (1.0 - keeping) * live
    acc[...] = jnp.zeros_like(acc)

    def scatter_block(n, carry):
        for c in range(CAP // CHUNK):
            at = c * CHUNK
            hot, pick = masks_of(cell_out[pl.ds(n, 1), at : at + CHUNK])
            g = air[0, pl.ds(n, 1), at : at + CHUNK]
            hi = g.astype(BF16).astype(F32)
            lo = g - hi
            z = jnp.concatenate(
                [
                    jnp.where(pick, hi, 0.0).astype(BF16),
                    jnp.where(pick, lo, 0.0).astype(BF16),
                ],
                axis=0,
            )
            acc[...] += lax.dot_general(
                hot, z, (((1,), (1,)), ((), ())), preferred_element_type=F32
            )
        return carry

    lax.fori_loop(0, 9, scatter_block, 0)
    for x in range(NX):
        a = x * NZ
        condensed = acc[a : a + NZ, 0:NY] + acc[a : a + NZ, NY:]
        heat_next[pl.ds(x, NZ, stride=NX), :] = stars[a : a + NZ, :] + HEAT_LOAD * condensed
        moist_next[pl.ds(x, NZ, stride=NX), :] = (
            stars[ROWS + a : ROWS + a + NZ, :] - MOIST_LOAD * condensed
        )


def final_kernel(
    recv, stars, zback, cell, state, east_next, north_next, up_next, drops_out, lhs, next_rows, air
):
    lane = iota((NZ, NY), 1)
    tiles = []
    for t in range(NX + 2):
        tiles.append(
            jnp.concatenate(
                [recv[pl.ds(b * SLOT + t, GX, stride=BLK), :] for b in range(2)], axis=0
            )
        )
    both = dot(zback[...], jnp.concatenate(tiles, axis=1))
    pres = [both[:NZ, t * NY : (t + 1) * NY] for t in range(NX + 2)]
    edge = pres[NX + 1]
    for x in range(NX):
        east = stars[x * NZ : (x + 1) * NZ, :] - (pres[x + 1] - pres[x]) * ASPECT
        ahead = pltpu.roll(
            jnp.where(lane == 0, pltpu.roll(edge, (NY - x) % NY, 1), pres[x]), NY - 1, 1
        )
        north = stars[(NX + x) * NZ : (NX + x + 1) * NZ, :] - (ahead - pres[x])
        rise = (
            stars[(2 * NX + x) * NZ : (2 * NX + x + 1) * NZ, :]
            - both[NZ:, x * NY : (x + 1) * NY]
        )
        for f, (val, ref) in enumerate(
            ((east, east_next), (north, north_next), (rise, up_next))
        ):
            ref[pl.ds(x, NZ, stride=NX), :] = val
            next_rows[f, x * NZ : (x + 1) * NZ, :] = val
    for f in range(3):
        store_table(lhs, 2 * f, next_rows[f])

    def gather_block(n, carry):
        for c in range(CAP // CHUNK):
            at = c * CHUNK
            hot, pick = masks_of(cell[pl.ds(n, 1), at : at + CHUNK])
            for f in range(3):
                air[f, pl.ds(n, 1), at : at + CHUNK] = gather_one(lhs, 2 * f, hot, pick)
        return carry

    lax.fori_loop(0, 9, gather_block, 0)
    mix = state[10]
    for a in range(3):
        speed = air[a] * mix + state[3 + a]
        offset = state[a] + DT * speed
        for n in range(9):
            drops_out[n, 3 + a : 4 + a, :] = speed[n : n + 1]
            drops_out[n, a : a + 1, :] = offset[n : n + 1]
    for n in range(9):
        for a in range(6, 10):
            drops_out[n, a : a + 1, :] = state[a, n : n + 1, :]


VM = pl.BlockSpec(memory_space=pltpu.VMEM)
SM = pl.BlockSpec(memory_space=pltpu.SMEM)


def sds(*shape, dtype=F32):
    return jax.ShapeDtypeStruct(shape, dtype)


def params():
    return pltpu.CompilerParams(vmem_limit_bytes=48 * 1024 * 1024)


def cost(us):
    return pl.CostEstimate(flops=int(us * 5e8), bytes_accessed=int(us * 2e6), transcendentals=0)


def whole(shape):
    zeros = (0,) * len(shape)
    return pl.BlockSpec(shape, lambda i, s: zeros)


def chosen(shape):
    zeros = (0,) * (len(shape) - 1)
    return pl.BlockSpec(shape, lambda i, s: (s[0],) + zeros)


def ring(axis, shift):
    count = lax.axis_size(axis)
    return [(i, (i + shift) % count) for i in range(count)]


def per_device(u, v, w, h, q, droplets, cell_index, block_count):
    tab = make_tables()
    u, v, w, h, q = (a.reshape(ROWS, NY) for a in (u, v, w, h, q))
    drops = droplets.reshape(9, 10, CAP)
    cells = cell_index.reshape(9, CAP)
    counts = block_count.reshape(9)
    xlo, xhi, up, down = pl.pallas_call(
        pack_kernel,
        out_shape=(sds(9 * NZ, NY), sds(9 * NZ, NY), sds(48, CAP), sds(48, CAP)),
        in_specs=[VM] * 7 + [SM],
        out_specs=(VM,) * 4,
        compiler_params=params(),
        cost_estimate=cost(1.5),
        name="pack",
    )(u, v, w, h, q, drops, cells, counts)
    xlo = lax.ppermute(xlo, "gx", ring("gx", 1))
    xhi = lax.ppermute(xhi, "gx", ring("gx", -1))
    mlo = lax.ppermute(up, "gy", ring("gy", 1))
    mhi = lax.ppermute(down, "gy", ring("gy", -1))
    cup, cdown = pl.pallas_call(
        relay_kernel,
        out_shape=(sds(64, CAP), sds(64, CAP)),
        in_specs=[VM] * 4 + [SM] + [VM] * 2,
        out_specs=(VM, VM),
        compiler_params=params(),
        cost_estimate=cost(1.0),
        name="relay",
    )(h, q, drops, cells, counts, mlo, mhi)
    clo = lax.ppermute(cup, "gx", ring("gx", 1))
    chi = lax.ppermute(cdown, "gx", ring("gx", -1))
    stars, send = pl.pallas_call(
        wind_kernel,
        out_shape=(sds(3 * ROWS, NY), sds(GX * BLK, NY)),
        in_specs=[VM] * 8,
        out_specs=(VM, VM),
        scratch_shapes=[pltpu.VMEM((3 * NX, NZ + 16, NY), F32)],
        compiler_params=params(),
        cost_estimate=cost(3.0),
        name="winds",
    )(u, v, w, xlo, xhi, mlo, mhi, tab["ztab"])
    recv = lax.all_to_all(send.reshape(GX, BLK, NY), "gx", 0, 0, tiled=True)
    heat_next, moist_next, cell_in, state = pl.pallas_call(
        drop_kernel,
        out_shape=(
            sds(ROWS, NY), sds(ROWS, NY), sds(9, CAP, dtype=jnp.int32), sds(11, 9, CAP),
        ),
        in_specs=[VM] * 11 + [SM],
        out_specs=(VM,) * 4,
        scratch_shapes=[
            pltpu.VMEM((2 * NX, NZ + 16, NY), F32),
            pltpu.VMEM((2 * ROWS, NY), F32),
            pltpu.VMEM((4 * NY, ROWS), BF16),
            pltpu.VMEM((ROWS, 2 * NY), F32),
            pltpu.VMEM((2, 9, CAP), F32),
        ],
        compiler_params=params(),
        cost_estimate=cost(10.0),
        name="growth",
    )(u, v, w, h, q, mlo, mhi, clo, chi, drops, cells, counts)
    place = jnp.stack([lax.axis_index("gx"), lax.axis_index("gy")]).astype(jnp.int32)
    msg, keep, cols, kink = pl.pallas_call(
        scan_kernel,
        out_shape=(sds(8 * GY, 2 * TX), sds(2 * TX, NY), sds(2 * TX, NY), sds(8, NY)),
        grid_spec=pltpu.PrefetchScalarGridSpec(
            num_scalar_prefetch=1,
            grid=(1,),
            in_specs=[
                whole((GX * BLK, NY)),
                whole((2 * TX, GX * BLK)),
                whole((2 * TX, GX)),
                whole((2 * TX, NY)),
                chosen((1, 2 * TX, NY)),
                chosen((1, 2 * TX, NY)),
                whole((NY, NY)),
            ],
            out_specs=[
                whole((8 * GY, 2 * TX)), whole((2 * TX, NY)), whole((2 * TX, NY)), whole((8, NY)),
            ],
        ),
        compiler_params=params(),
        cost_estimate=cost(2.0),
        name="scan",
    )(
        place, recv.reshape(GX * BLK, NY), tab["wmain"], tab["t12"], tab["cs"],
        tab["rrev"], tab["misc"], tab["absd"],
    )
    got = lax.all_to_all(msg.reshape(GY, 8, 2 * TX), "gy", 0, 0, tiled=True)
    send = pl.pallas_call(
        solve_kernel,
        out_shape=sds(GX * BLK, NY),
        grid_spec=pltpu.PrefetchScalarGridSpec(
            num_scalar_prefetch=1,
            grid=(1,),
            in_specs=[
                whole((8 * GY, 2 * TX)),
                whole((2 * TX, NY)),
                whole((2 * TX, NY)),
                whole((8, NY)),
                whole((GX * BLK, 2 * TX)),
                whole((GX, 2 * TX)),
                whole((2 * TX, NY)),
                chosen((1, 2 * TX, NY)),
                chosen((1, 2 * TX, NY)),
                chosen((1, 2 * TX, NY)),
                chosen((1, 8, 2 * TX)),
            ],
            out_specs=whole((GX * BLK, NY)),
        ),
        compiler_params=params(),
        cost_estimate=cost(2.0),
        name="solve",
    )(
        place, got.reshape(8 * GY, 2 * TX), keep, cols, kink, tab["wback"], tab["t12t"],
        tab["cs"], tab["rpow"], tab["rrev"], tab["misc"], tab["rowtab"],
    )
    recv = lax.all_to_all(send.reshape(GX, BLK, NY), "gx", 0, 0, tiled=True)
    east_next, north_next, up_next, drops_out = pl.pallas_call(
        final_kernel,
        out_shape=(sds(ROWS, NY), sds(ROWS, NY), sds(ROWS, NY), sds(9, 10, CAP)),
        in_specs=[VM] * 5,
        out_specs=(VM,) * 4,
        scratch_shapes=[
            pltpu.VMEM((6 * NY, ROWS), BF16),
            pltpu.VMEM((3, ROWS, NY), F32),
            pltpu.VMEM((3, 9, CAP), F32),
        ],
        compiler_params=params(),
        cost_estimate=cost(8.0),
        name="final",
    )(recv.reshape(GX * BLK, NY), stars, tab["zback"], cell_in, state)
    fields = (
        a.reshape(NZ, NX, NY) for a in (east_next, north_next, up_next, heat_next, moist_next)
    )
    return (*fields, drops_out.reshape(3, 3, 10, CAP))


def solution(mesh):
    grid = P(None, "gx", "gy")
    blocks = P("gx", "gy", None, None)
    return jax.shard_map(
        per_device,
        mesh=mesh,
        in_specs=(grid,) * 5 + (blocks, P("gx", "gy", None), P("gx", "gy")),
        out_specs=(grid,) * 5 + (blocks,),
        check_vma=False,
    )
```

time: 649 us -> 108 us (0.17)
  local copies, waits for them, and re-layouts: 280 us -> 32.3 us
  other arithmetic: 140 us -> 0.6 us
  matrix products: 106 us -> 0 us
  starting transfers between devices: 74.1 us -> 35.8 us
  waiting for transfers between devices: 39.6 us -> 9.02 us
  Pallas kernels: 0 us -> 28 us
    gather x5 -> x0, local copies, waits for them, and re-layouts: 256 us -> none  [per_device(): quantity.reshape(-1)[cells_in]]
    dot_general x9 -> x0, matrix products: 106 us -> none  [the longest x1 77.8 us: per_device(): full_hat = jnp.einsum('skmy,syl->kml', spectrum, ytable, precision=HIGHEST)]
    dot_general x1 -> x0, other arithmetic: 70.1 us -> none  [per_device(): jnp.einsum('kml,syl->skmy', pressure_hat, ytable, precision=HIGHEST)]
    scatter-add x1 -> x0, other arithmetic: 48.7 us -> none  [per_device(): condensed = jnp.zeros((levels * width_x * width_y,), jnp.float32).at[cell...]
    all_to_all x7 -> x3, waiting for transfers between devices: 35.3 us -> 6.59 us  [the longest x2 6.59 us: per_device(): recv = lax.all_to_all(send.reshape(GX, BLK, NY), 'gx', 0, 0, tiled=True)]
    pallas_call x0 -> x7, Pallas kernels: none -> 28 us  [the longest x1 11.3 us: per_device(): pl.pallas_call(drop_kernel, out_shape=(sds(ROWS, NY), sds(ROWS, NY), sds(...]
    ppermute x16 -> x6, starting transfers between devices: 37.9 us -> 13 us  [the longest x1 4.5 us: per_device(): chi = lax.ppermute(cdown, 'gx', ring('gx', -1))]
    unnamed x49 -> x104, local copies, waits for them, and re-layouts: 9.2 us -> 30.7 us
  transfers between devices with their start and end apart: 23 -> 9, of which waited for: 13 -> 2; matrix products, arithmetic and copies ran while one was open for 16% -> 1% of each run, Pallas kernels for 0% -> 15%
where the time goes in v1:
time: 108 us; the launch traced here: 107 us
  starting transfers between devices  35.8 us (33%)
  local copies, waits for them, and re-layouts  32.3 us (30%)
  Pallas kernels  28 us (26%)
  waiting for transfers between devices  9.02 us (8%)
    unnamed x104, local copies, waits for them, and re-layouts  30.7 us
    all_to_all x1, starting transfers between devices, per_device(): got = lax.all_to_all(msg.reshape(GY, 8, 2 * TX), 'gy', 0, 0, tiled=True)  12.7 us
    pallas_call x1, Pallas kernels, per_device(): pl.pallas_call(drop_kernel, out_shape=(sds(ROWS, NY), sds(ROWS, NY), sds(...  11.3 us
    all_to_all x2, starting transfers between devices, per_device(): recv = lax.all_to_all(send.reshape(GX, BLK, NY), 'gx', 0, 0, tiled=True)  10.1 us
    pallas_call x1, Pallas kernels, per_device(): pl.pallas_call(final_kernel, out_shape=(sds(ROWS, NY), sds(ROWS, NY), sds...  7.04 us
    all_to_all x2, waiting for transfers between devices, per_device(): recv = lax.all_to_all(send.reshape(GX, BLK, NY), 'gx', 0, 0, tiled=True)  6.59 us
    ppermute x1, starting transfers between devices, per_device(): chi = lax.ppermute(cdown, 'gx', ring('gx', -1))  4.5 us
    ppermute x1, starting transfers between devices, per_device(): xhi = lax.ppermute(xhi, 'gx', ring('gx', -1))  3.89 us
  transfers between devices with their start and end apart: 9, of which 2 were waited for; matrix products, arithmetic and copies ran while one was open for 1% of the time, Pallas kernels for 15%

profile of v1, /device:TPU:1, one launch (start us, length us, event | category | flops | bytes accessed | tf_op | source)
XLA Modules:
  0.0 106.6 jit_solution(12744916580016757390)
XLA Ops:
  0.6 0.0 copy-start.48
  0.6 1.3 %copy.26 = f32[3,3,10,1024]{3,2,1,0:T(8,128)S(1)} copy(f32[3,3,10,1024]{3,1,2,0:T(4,128)} %param.25) | data formatting | bytes 737280 | tf_op args[5]
  1.9 0.8 reshape.78.cells
  2.7 0.0 copy-start.15
  2.7 0.8 reshape.79.counts
  3.5 0.9 copy-done.32
  4.4 0.9 copy-done.35
  5.3 0.9 copy-done.38
  6.2 0.9 copy-done.41
  7.2 0.9 copy-done.44
  8.1 1.0 pack.1
  9.0 3.0 %collective-permute-start.2 = (f32[48,1024]{1,0:T(8,128)S(1)}, f32[48,1024]{1,0:T(8,128)S(1)}, u32[]{:S(2)}, u32[]{:S(2)}) collective-permute-start(f32[48,1024]{1,0:T(8,128)S(1)} %get-tuple-element.28), channel_id=1, source_target_pairs={{0,1},{1,2},{2,3},{3,4},{4,5},{5,6},{6,7},{7,8},{8,9},{9,10},{10,1... | collective-permute-start | bytes 589832 | tf_op jit(solution)/shard_map/ppermute | solution.py:579
  12.1 0.2 collective-permute-start.3
  12.3 1.0 collective-permute-start
  13.3 0.0 copy-start.5
  13.3 0.0 copy-start.13
  13.3 3.9 %collective-permute-start.1 = (f32[288,128]{1,0:T(8,128)S(1)}, f32[288,128]{1,0:T(8,128)S(1)}, u32[]{:S(2)}, u32[]{:S(2)}) collective-permute-start(f32[288,128]{1,0:T(8,128)S(1)} %get-tuple-element.27), channel_id=1, source_target_pairs={{0,240},{16,0},{32,16},{48,32},{64,48},{80,64},{96,80},{112,96},{1... | collective-permute-start | bytes 442376 | tf_op jit(solution)/shard_map/ppermute | solution.py:578
  17.2 2.4 %collective-permute-done.xlo = f32[288,128]{1,0:T(8,128)S(1)} collective-permute-done((f32[288,128]{1,0:T(8,128)S(1)}, f32[288,128]{1,0:T(8,128)S(1)}, u32[]{:S(2)}, u32[]{:S(2)}) %collective-permute-start) | collective-permute-done | bytes 147488 | tf_op jit(solution)/shard_map/ppermute | solution.py:577
  19.6 0.0 collective-permute-done.1.xhi
  19.6 0.0 collective-permute-done.2.mlo
  19.7 2.2 %winds.1 = (f32[768,128]{1,0:T(8,128)S(1)}, f32[384,128]{1,0:T(8,128)S(1)}) custom-call(f32[256,128]{1,0:T(8,128)S(1)} %bitcast.30, f32[256,128]{1,0:T(8,128)S(1)} %bitcast.33, f32[256,128]{1,0:T(8,128)S(1)} %bitcast.36, f32[288,128]{1,0:T(8,128)S(1)} %collective-permute-done.xlo, f32[288,128]{1,0:T(8,128)S(1)} %collective-permute-done.1.xhi, ...), custom_call_target="tpu_custom_call" | custom-call | flops 1500000000 | bytes 6000000 | tf_op jit(solution)/shard_map/winds/pallas_call | solution.py:592
  21.9 0.7 copy-done.6
  22.6 0.7 copy-done.49
  23.3 6.3 %all-to-all-start = ((f32[16,24,128]{2,1,0:T(8,128)}), f32[16,24,128]{2,1,0:T(8,128)S(1)}, u32[]{:S(2)}, u32[]{:S(2)}) async-start(f32[16,24,128]{2,1,0:T(8,128)} %bitcast.27), calls=%async_computation | async-start | bytes 393216 | tf_op jit(solution)/shard_map/all_to_all | solution.py:602
  29.6 0.6 pad_add_fusion.sx
  30.2 6.6 %all-to-all-done = f32[16,24,128]{2,1,0:T(8,128)S(1)} async-done(((f32[16,24,128]{2,1,0:T(8,128)}), f32[16,24,128]{2,1,0:T(8,128)S(1)}, u32[]{:S(2)}, u32[]{:S(2)}) %all-to-all-start) | async-done | bytes 196640 | tf_op jit(solution)/shard_map/all_to_all | solution.py:602
  36.8 0.0 copy-start.1
  36.8 1.6 %copy-done.1 = f32[16,256,128]{2,1,0:T(8,128)S(1)} copy-done((f32[16,256,128]{2,1,0:T(8,128)S(1)}, f32[16,256,128]{2,1,0:T(8,128)}, u32[]{:S(2)}) %copy-start.1) | copy-done | bytes 2097176
  38.4 0.8 copy-done.14
  39.3 0.6 copy-done.21
  39.9 2.0 %scan.1 = (f32[128,256]{1,0:T(8,128)S(1)}, f32[256,128]{1,0:T(8,128)S(1)}, f32[256,128]{1,0:T(8,128)S(1)}, f32[8,128]{1,0:T(8,128)S(1)}) custom-call(s32[2]{0:T(128)S(1)} %copy-done.21, f32[384,128]{1,0:T(8,128)S(1)} %bitcast.20, f32[256,384]{1,0:T(8,128)S(1)} %copy-done.5, f32[256,16]{1,0:T(8,128)S(1)} %copy-done.13, f32[256,128]{1,0:T(8,128)S(1)} %copy-done.3, ...), custom_call_target="tpu_custom_call" | custom-call | flops 1000000000 | bytes 4000000 | tf_op jit(solution)/shard_map/scan/pallas_call | solution.py:622
  41.9 0.7 copy-done.8
  42.6 0.7 copy-done.10
  43.2 0.7 copy-done.12
  43.9 0.6 copy-done.19
  44.5 12.7 %all-to-all-start.1 = ((f32[16,8,256]{2,1,0:T(8,128)}), f32[16,8,256]{2,1,0:T(8,128)S(1)}, u32[]{:S(2)}, u32[]{:S(2)}) async-start(f32[16,8,256]{2,1,0:T(8,128)} %bitcast.28), calls=%async_computation.1 | async-start | bytes 262144 | tf_op jit(solution)/shard_map/all_to_all | solution.py:648
  57.2 0.8 copy-done.16
  58.0 0.6 copy-done.24
  58.6 0.9 copy-done.27
  59.5 0.9 copy-done.30
  60.5 0.9 copy-done.42
  61.4 0.9 copy-done.45
  62.3 1.4 %relay.1 = (f32[64,1024]{1,0:T(8,128)}, f32[64,1024]{1,0:T(8,128)}) custom-call(f32[256,128]{1,0:T(8,128)S(1)} %bitcast.39, f32[256,128]{1,0:T(8,128)S(1)} %bitcast.42, f32[9,10,1024]{2,1,0:T(8,128)S(1)} %bitcast.22, s32[9,1024]{1,0:T(8,128)S(1)} %copy-done.16, s32[9]{0:T(128)S(1)} %copy-done.24, f32[48,1024]{1,0:T(8,128)S(1)} %copy-done.27, ...), custom_call_target="tpu_custom_call" | custom-call | flops 500000000 | bytes 2000000 | tf_op jit(solution)/shard_map/relay/pallas_call | solution.py:581
  63.6 0.3 collective-permute-start.4
  64.0 4.5 %collective-permute-start.5 = (f32[64,1024]{1,0:T(8,128)}, f32[64,1024]{1,0:T(8,128)}, u32[]{:S(2)}, u32[]{:S(2)}) collective-permute-start(f32[64,1024]{1,0:T(8,128)} %get-tuple-element.37), channel_id=1, source_target_pairs={{0,240},{16,0},{32,16},{48,32},{64,48},{80,64},{96,80},{112,96},{1... | collective-permute-start | bytes 786440 | tf_op jit(solution)/shard_map/ppermute | solution.py:591
  68.5 0.0 copy-start.2
  68.5 1.6 %copy-done.2 = f32[16,256,128]{2,1,0:T(8,128)S(1)} copy-done((f32[16,256,128]{2,1,0:T(8,128)S(1)}, f32[16,256,128]{2,1,0:T(8,128)}, u32[]{:S(2)}) %copy-start.2) | copy-done | bytes 2097176
  70.1 0.9 copy-done.9
  71.0 0.9 copy-done.11
  71.9 0.7 copy-done.20
  72.6 0.6 copy-done.22
  73.2 3.2 %solve.1 = f32[384,128]{1,0:T(8,128)} custom-call(s32[2]{0:T(128)S(1)} %copy-done.22, f32[128,256]{1,0:T(8,128)S(1)} %bitcast.25, f32[256,128]{1,0:T(8,128)S(1)} %copy-done.9, f32[256,128]{1,0:T(8,128)S(1)} %copy-done.11, f32[8,128]{1,0:T(8,128)S(1)} %copy-done.20, f32[384,256]{1,0:T(8,128)S(1)} %copy-done.4, f32[16,256]{1,0:T(8,128)S(1)} %copy-done.18, ...), custom_call_target="tpu_custom_call" | custom-call | flops 1000000000 | bytes 4000000 | tf_op jit(solution)/shard_map/solve/pallas_call | solution.py:649
  76.3 3.8 %all-to-all-start.2 = ((f32[16,24,128]{2,1,0:T(8,128)}), f32[16,24,128]{2,1,0:T(8,128)S(1)}, u32[]{:S(2)}, u32[]{:S(2)}) async-start(f32[16,24,128]{2,1,0:T(8,128)} %bitcast.12), calls=%async_computation.2 | async-start | bytes 393216 | tf_op jit(solution)/shard_map/all_to_all | solution.py:677
  80.2 0.6 copy-done.25
  80.8 0.9 copy-done.28
  81.7 0.9 copy-done.31
  82.7 0.9 copy-done.34
  83.6 0.9 copy-done.37
  84.5 0.9 copy-done.40
  85.4 0.9 copy-done.43
  86.3 0.9 copy-done.46
  87.2 11.3 %growth.1 = (f32[256,128]{1,0:T(8,128)}, f32[256,128]{1,0:T(8,128)}, s32[9,1024]{1,0:T(8,128)S(1)}, f32[11,9,1024]{2,1,0:T(8,128)S(1)}) custom-call(f32[256,128]{1,0:T(8,128)S(1)} %bitcast.31, f32[256,128]{1,0:T(8,128)S(1)} %bitcast.34, f32[256,128]{1,0:T(8,128)S(1)} %bitcast.37, f32[256,128]{1,0:T(8,128)S(1)} %bitcast.40, f32[256,128]{1,0:T(8,128)S(1)} %bitcast.43, ...), custom_call_target="tpu_custom_call" | custom-call | flops 5000000000 | bytes 20000000 | tf_op jit(solution)/shard_map/growth/pallas_call | solution.py:603
  98.5 7.0 %final.1 = (f32[256,128]{1,0:T(8,128)}, f32[256,128]{1,0:T(8,128)}, f32[256,128]{1,0:T(8,128)}, f32[9,10,1024]{2,1,0:T(8,128)S(1)}) custom-call(f32[384,128]{1,0:T(8,128)S(1)} %bitcast.26, f32[768,128]{1,0:T(8,128)S(1)} %copy-done.50, f32[64,32]{1,0:T(8,128)S(1)} %copy-done.47, s32[9,1024]{1,0:T(8,128)S(1)} %get-tuple-element.38.cell, ...), custom_call_target="tpu_custom_call" | custom-call | flops 4000000000 | bytes 16000000 | tf_op jit(solution)/shard_map/final/pallas_call | solution.py:678
  105.6 1.0 copy.27
  (68 shorter events, 0.1 us)
Async XLA Ops:
  0.6 19.0 %copy-start.48 = (f32[32,32]{1,0:T(8,128)S(1)}, f32[32,32]{1,0:T(8,128)}, u32[]{:S(2)}) copy-start(f32[32,32]{1,0:T(8,128)} %constant.31.clone.ztab) | copy-start | bytes 12292
  2.7 10.6 %copy-start.15 = (s32[9,1024]{1,0:T(8,128)}, s32[9,1024]{1,0:T(8,128)S(1)}, u32[]{:S(2)}) copy-start(s32[9,1024]{1,0:T(8,128)S(1)} %reshape.78.cells) | copy-start | bytes 110596
  3.5 9.8 %copy-start.23 = (s32[9]{0:T(128)}, s32[9]{0:T(128)S(1)}, u32[]{:S(2)}) copy-start(s32[9]{0:T(128)S(1)} %reshape.79.counts) | copy-start | bytes 112
  3.5 0.9 copy-start.32
  4.4 0.9 copy-start.35
  5.3 0.9 copy-start.38
  6.2 0.9 copy-start.41
  7.1 0.9 copy-start.44
  8.1 11.6 %copy-start.33 = (f32[32,8,128]{2,1,0:T(8,128)S(1)}, f32[32,8,128]{2,1,0:T(8,128)}, u32[]{:S(2)}) copy-start(f32[32,8,128]{2,1,0:T(8,128)} %param.20) | copy-start | bytes 393220
  8.1 11.6 %copy-start.36 = (f32[32,8,128]{2,1,0:T(8,128)S(1)}, f32[32,8,128]{2,1,0:T(8,128)}, u32[]{:S(2)}) copy-start(f32[32,8,128]{2,1,0:T(8,128)} %param.21) | copy-start | bytes 393220
  8.1 11.6 %copy-start.39 = (f32[32,8,128]{2,1,0:T(8,128)S(1)}, f32[32,8,128]{2,1,0:T(8,128)}, u32[]{:S(2)}) copy-start(f32[32,8,128]{2,1,0:T(8,128)} %param.22) | copy-start | bytes 393220
  9.0 10.6 %collective-permute-start.2 = (f32[48,1024]{1,0:T(8,128)S(1)}, f32[48,1024]{1,0:T(8,128)S(1)}, u32[]{:S(2)}, u32[]{:S(2)}) collective-permute-start(f32[48,1024]{1,0:T(8,128)S(1)} %get-tuple-element.28), channel_id=1, source_target_pairs={{0,1},{1,2},{2,3},{3,4},{4,5},{5,6},{6,7},{7,8},{8,9},{9,10},{10,1... | collective-permute-start | bytes 589832 | tf_op jit(solution)/shard_map/ppermute | solution.py:579
  12.1 7.6 %collective-permute-start.3 = (f32[48,1024]{1,0:T(8,128)S(1)}, f32[48,1024]{1,0:T(8,128)S(1)}, u32[]{:S(2)}, u32[]{:S(2)}) collective-permute-start(f32[48,1024]{1,0:T(8,128)S(1)} %get-tuple-element.29), channel_id=1, source_target_pairs={{0,15},{1,0},{2,1},{3,2},{4,3},{5,4},{6,5},{7,6},{8,7},{9,8},{10,9... | collective-permute-start | bytes 589832 | tf_op jit(solution)/shard_map/ppermute | solution.py:580
  12.3 7.3 %collective-permute-start = (f32[288,128]{1,0:T(8,128)S(1)}, f32[288,128]{1,0:T(8,128)S(1)}, u32[]{:S(2)}, u32[]{:S(2)}) collective-permute-start(f32[288,128]{1,0:T(8,128)S(1)} %get-tuple-element.26), channel_id=1, source_target_pairs={{0,16},{16,32},{32,48},{48,64},{64,80},{80,96},{96,112},{112,128},... | collective-permute-start | bytes 442376 | tf_op jit(solution)/shard_map/ppermute | solution.py:577
  13.3 23.5 %copy-start = (f32[16,256,128]{2,1,0:T(8,128)S(1)}, f32[16,256,128]{2,1,0:T(8,128)}, u32[]{:S(2)}) copy-start(f32[16,256,128]{2,1,0:T(8,128)} %constant.39.clone.rrev) | copy-start | bytes 6291460
  13.3 23.5 %copy-start.3 = (f32[256,128]{1,0:T(8,128)S(1)}, f32[256,128]{1,0:T(8,128)}, u32[]{:S(2)}) copy-start(f32[256,128]{1,0:T(8,128)} %constant.37.clone.cs) | copy-start | bytes 393220
  13.3 23.5 %copy-start.5 = (f32[256,384]{1,0:T(8,128)S(1)}, f32[256,384]{1,0:T(8,128)}, u32[]{:S(2)}) copy-start(f32[256,384]{1,0:T(8,128)} %constant.33.clone.wmain) | copy-start | bytes 1179652
  13.3 23.5 %copy-start.13 = (f32[256,16]{1,0:T(8,128)S(1)}, f32[256,16]{1,0:T(8,128)}, u32[]{:S(2)}) copy-start(f32[256,16]{1,0:T(8,128)} %constant.35.clone.t12) | copy-start | bytes 49156
  13.3 6.3 %collective-permute-start.1 = (f32[288,128]{1,0:T(8,128)S(1)}, f32[288,128]{1,0:T(8,128)S(1)}, u32[]{:S(2)}, u32[]{:S(2)}) collective-permute-start(f32[288,128]{1,0:T(8,128)S(1)} %get-tuple-element.27), channel_id=1, source_target_pairs={{0,240},{16,0},{32,16},{48,32},{64,48},{80,64},{96,80},{112,96},{1... | collective-permute-start | bytes 442376 | tf_op jit(solution)/shard_map/ppermute | solution.py:578
  19.6 2.3 %copy-start.26 = (f32[48,1024]{1,0:T(8,128)}, f32[48,1024]{1,0:T(8,128)S(1)}, u32[]{:S(2)}) copy-start(f32[48,1024]{1,0:T(8,128)S(1)} %collective-permute-done.2.mlo) | copy-start | bytes 589828
  19.7 2.2 %copy-start.29 = (f32[48,1024]{1,0:T(8,128)}, f32[48,1024]{1,0:T(8,128)S(1)}, u32[]{:S(2)}) copy-start(f32[48,1024]{1,0:T(8,128)S(1)} %collective-permute-done.3.mhi) | copy-start | bytes 589828
  21.9 0.7 copy-start.6
  22.6 0.7 copy-start.49
  23.3 13.5 %all-to-all-start = ((f32[16,24,128]{2,1,0:T(8,128)}), f32[16,24,128]{2,1,0:T(8,128)S(1)}, u32[]{:S(2)}, u32[]{:S(2)}) async-start(f32[16,24,128]{2,1,0:T(8,128)} %bitcast.27), calls=%async_computation | async-start | bytes 393216 | tf_op jit(solution)/shard_map/all_to_all | solution.py:602
  36.8 1.6 %copy-start.1 = (f32[16,256,128]{2,1,0:T(8,128)S(1)}, f32[16,256,128]{2,1,0:T(8,128)}, u32[]{:S(2)}) copy-start(f32[16,256,128]{2,1,0:T(8,128)} %constant.40.clone.misc) | copy-start | bytes 6291460
  38.4 0.8 copy-start.14
  39.3 0.6 copy-start.21
  39.9 28.6 %copy-start.18 = (f32[16,256]{1,0:T(8,128)S(1)}, f32[16,256]{1,0:T(8,128)}, u32[]{:S(2)}) copy-start(f32[16,256]{1,0:T(8,128)} %constant.36.clone.t12t) | copy-start | bytes 49156
  41.9 0.7 copy-start.8
  42.6 0.7 copy-start.10
  43.2 0.7 copy-start.12
  43.9 0.6 copy-start.19
  44.5 24.0 %copy-start.4 = (f32[384,256]{1,0:T(8,128)S(1)}, f32[384,256]{1,0:T(8,128)}, u32[]{:S(2)}) copy-start(f32[384,256]{1,0:T(8,128)} %constant.34.clone.wback) | copy-start | bytes 1179652
  44.5 24.0 %copy-start.7 = (f32[16,8,256]{2,1,0:T(8,128)S(1)}, f32[16,8,256]{2,1,0:T(8,128)}, u32[]{:S(2)}) copy-start(f32[16,8,256]{2,1,0:T(8,128)} %constant.41.clone.rowtab) | copy-start | bytes 393220
  44.5 24.0 %all-to-all-start.1 = ((f32[16,8,256]{2,1,0:T(8,128)}), f32[16,8,256]{2,1,0:T(8,128)S(1)}, u32[]{:S(2)}, u32[]{:S(2)}) async-start(f32[16,8,256]{2,1,0:T(8,128)} %bitcast.28), calls=%async_computation.1 | async-start | bytes 262144 | tf_op jit(solution)/shard_map/all_to_all | solution.py:648
  57.2 0.8 copy-start.16
  58.0 0.6 copy-start.24
  58.6 0.9 copy-start.27
  59.5 0.9 copy-start.30
  60.5 0.9 copy-start.42
  61.4 0.9 copy-start.45
  63.6 16.5 %collective-permute-start.4 = (f32[64,1024]{1,0:T(8,128)}, f32[64,1024]{1,0:T(8,128)}, u32[]{:S(2)}, u32[]{:S(2)}) collective-permute-start(f32[64,1024]{1,0:T(8,128)} %get-tuple-element.36), channel_id=1, source_target_pairs={{0,16},{16,32},{32,48},{48,64},{64,80},{80,96},{96,112},{112,128},... | collective-permute-start | bytes 786440 | tf_op jit(solution)/shard_map/ppermute | solution.py:590
  64.0 16.2 %collective-permute-start.5 = (f32[64,1024]{1,0:T(8,128)}, f32[64,1024]{1,0:T(8,128)}, u32[]{:S(2)}, u32[]{:S(2)}) collective-permute-start(f32[64,1024]{1,0:T(8,128)} %get-tuple-element.37), channel_id=1, source_target_pairs={{0,240},{16,0},{32,16},{48,32},{64,48},{80,64},{96,80},{112,96},{1... | collective-permute-start | bytes 786440 | tf_op jit(solution)/shard_map/ppermute | solution.py:591
  68.5 1.6 %copy-start.2 = (f32[16,256,128]{2,1,0:T(8,128)S(1)}, f32[16,256,128]{2,1,0:T(8,128)}, u32[]{:S(2)}) copy-start(f32[16,256,128]{2,1,0:T(8,128)} %constant.38.clone.rpow) | copy-start | bytes 6291460
  70.1 0.9 copy-start.9
  71.0 0.9 copy-start.11
  71.9 0.7 copy-start.20
  72.6 0.6 copy-start.22
  73.2 7.0 %copy-start.17 = (s32[9,1024]{1,0:T(8,128)S(1)}, s32[9,1024]{1,0:T(8,128)}, u32[]{:S(2)}) copy-start(s32[9,1024]{1,0:T(8,128)} %copy-done.15) | copy-start | bytes 110596
  76.3 22.2 %copy-start.47 = (f32[64,32]{1,0:T(8,128)S(1)}, f32[64,32]{1,0:T(8,128)}, u32[]{:S(2)}) copy-start(f32[64,32]{1,0:T(8,128)} %constant.32.clone.zback) | copy-start | bytes 24580
  76.3 22.2 %all-to-all-start.2 = ((f32[16,24,128]{2,1,0:T(8,128)}), f32[16,24,128]{2,1,0:T(8,128)S(1)}, u32[]{:S(2)}, u32[]{:S(2)}) async-start(f32[16,24,128]{2,1,0:T(8,128)} %bitcast.12), calls=%async_computation.2 | async-start | bytes 393216 | tf_op jit(solution)/shard_map/all_to_all | solution.py:677
  80.2 0.6 copy-start.25
  80.8 0.9 copy-start.28
  81.7 0.9 copy-start.31
  82.7 0.9 copy-start.34
  83.6 0.9 copy-start.37
  84.5 0.9 copy-start.40
  85.4 0.9 copy-start.43
  86.3 0.9 copy-start.46
  87.2 11.3 %copy-start.50 = (f32[768,128]{1,0:T(8,128)S(1)}, f32[768,128]{1,0:T(8,128)}, u32[]{:S(2)}) copy-start(f32[768,128]{1,0:T(8,128)} %copy-done.49) | copy-start | bytes 1179652

commit v2 on v1

--- a/solution.py
+++ b/solution.py
@@ -83,6 +83,7 @@
     rowtab[:, 0] = NY * lnr
     rowtab[:, 1] = 1.0 / (1.0 - np.exp(lnr * TY))
     absd = np.abs(lane[:, None] - lane[None, :])
+    own = np.concatenate([rpow, rrev, misc, rowtab[:, :, :NY], rowtab[:, :, NY:]], axis=1)
 
     def f(a):
         return jnp.asarray(np.asarray(a, np.float32))
@@ -95,10 +96,7 @@
         t12=f(t12),
         t12t=f(t12.T),
         cs=f(cs),
-        rpow=f(rpow),
-        rrev=f(rrev),
-        misc=f(misc),
-        rowtab=f(rowtab),
+        own=f(own),
         absd=f(absd),
     )
 
@@ -111,8 +109,8 @@
     return jnp.dot(a, b, precision=HIGHEST, preferred_element_type=F32)
 
 
-def row_of(ref, x):
-    return ref[pl.ds(x, NZ, stride=NX), :]
+def field_row(fields, f, x):
+    return fields[pl.ds(f * ROWS + x, NZ, stride=NX), :]
 
 
 def pair_of(f0, lo, hi):
@@ -149,10 +147,10 @@
     return f0 - (total + (aw * a + bw * b))
 
 
-def velocity_rows(u, v, w, x):
+def velocity_rows(fields, x):
     out = []
-    for ref in (u, v, w):
-        a = row_of(ref, x) * (DT / 60.0)
+    for f in range(3):
+        a = field_row(fields, f, x) * (DT / 60.0)
         out += [a, jnp.abs(a)]
     return out
 
@@ -169,35 +167,49 @@
     out[36:40, :] = jnp.zeros((4, CAP), F32)
 
 
-def own_block(drops, cells, counts, n):
-    return (
-        drops[n],
-        cells[n : n + 1, :].astype(F32),
-        jnp.full((1, CAP), counts[n], jnp.int32).astype(F32),
-    )
-
-
-def pack_kernel(u, v, w, h, q, drops, cells, counts, xlo, xhi, up, down):
-    for f, ref in enumerate((u, v, w)):
+def pack_kernel(
+    u, v, w, h, q, drops_in, cells, counts, own, xlo, xhi, up, down, mid, fields, tabs, drops, sems
+):
+    copies = [
+        pltpu.make_async_copy(ref, fields.at[pl.ds(f * ROWS, ROWS)], sems.at[f])
+        for f, ref in enumerate((u, v, w, h, q))
+    ]
+    copies.append(pltpu.make_async_copy(drops_in, drops, sems.at[5]))
+    copies.append(pltpu.make_async_copy(own.at[lax.axis_index("gx")], tabs, sems.at[6]))
+    for copy in copies:
+        copy.start()
+    for copy in copies[:5]:
+        copy.wait()
+    for f in range(3):
         for i in range(3):
             n = f * 3 + i
-            xlo[n * NZ : (n + 1) * NZ, :] = row_of(ref, 5 + i)
-            xhi[n * NZ : (n + 1) * NZ, :] = row_of(ref, i)
+            xlo[n * NZ : (n + 1) * NZ, :] = field_row(fields, f, 5 + i)
+            xhi[n * NZ : (n + 1) * NZ, :] = field_row(fields, f, i)
     lane = iota((NZ, NY), 1)
     tlo = jnp.zeros((NZ, NY), F32)
     thi = jnp.zeros((NZ, NY), F32)
     for x in range(NX):
-        for f, ref in enumerate((u, v, w, h, q)):
+        for f in range(5):
             at = 16 * x + 3 * f
-            row = row_of(ref, x)
+            row = field_row(fields, f, x)
             mask = (lane >= at) & (lane < at + 3)
             tlo = jnp.where(mask, pltpu.roll(row, (at - 125) % NY, 1), tlo)
             thi = jnp.where(mask, pltpu.roll(row, at, 1), thi)
-    for out, tile, s in ((up, tlo, 2), (down, thi, 0)):
-        pack_blocks(out, [own_block(drops, cells, counts, r * 3 + s) for r in range(3)])
+    for out, tile in ((up, tlo), (down, thi)):
         for g in range(4):
             out[40:48, g * NY : (g + 1) * NY] = tile[g * 8 : (g + 1) * 8]
         out[40:48, 4 * NY :] = jnp.zeros((8, 4 * NY), F32)
+    copies[5].wait()
+    for s, out in ((2, up), (0, down), (1, mid)):
+        for r in range(3):
+            for a in range(10):
+                out[r * SLOT + a : r * SLOT + a + 1, :] = drops[r, a, s : s + 1, :]
+            out[r * SLOT + 10 : r * SLOT + 11, :] = cells[r, s : s + 1, :].astype(F32)
+            out[r * SLOT + 11 : r * SLOT + 12, :] = jnp.full(
+                (1, CAP), counts[r, s], jnp.int32
+            ).astype(F32)
+        out[36:40, :] = jnp.zeros((4, CAP), F32)
+    copies[6].wait()
 
 
 def block_of(msg, n):
@@ -208,30 +220,27 @@
     )
 
 
-def relay_kernel(h, q, drops, cells, counts, mlo, mhi, up, down):
+def relay_kernel(fields, mid, mlo, mhi, up, down):
     for out, r, x0 in ((up, 2, 5), (down, 0, 0)):
-        pack_blocks(
-            out,
-            [block_of(mlo, r), own_block(drops, cells, counts, r * 3 + 1), block_of(mhi, r)],
-        )
-        for f, ref in enumerate((h, q)):
+        pack_blocks(out, [block_of(mlo, r), block_of(mid, r), block_of(mhi, r)])
+        for f in range(2):
             for i in range(3):
-                row = row_of(ref, x0 + i)
+                row = field_row(fields, 3 + f, x0 + i)
                 for g in range(4):
                     n = (f * 3 + i) * 4 + g
                     a, c = 40 + 8 * (n // 8), NY * (n % 8)
                     out[a : a + 8, c : c + NY] = row[g * 8 : (g + 1) * 8]
 
 
-def wind_kernel(u, v, w, xlo, xhi, mlo, mhi, ztab, stars, send, zs):
+def wind_kernel(fields, xlo, xhi, mlo, mhi, ztab, after, stars, send, zs):
     lane = iota((NZ, NY), 1)
     level = iota((NZ, NY), 0)
     ylo = yhalo_of(mlo)
     yhi = yhalo_of(mhi)
-    vel = [velocity_rows(u, v, w, x) for x in range(NX)]
-    for f, ref in enumerate((u, v, w)):
+    vel = [velocity_rows(fields, x) for x in range(NX)]
+    for f in range(3):
         rows = [xlo[(f * 3 + i) * NZ : (f * 3 + i + 1) * NZ, :] for i in range(3)]
-        rows += [row_of(ref, x) for x in range(NX)]
+        rows += [field_row(fields, f, x) for x in range(NX)]
         rows += [xhi[(f * 3 + i) * NZ : (f * 3 + i + 1) * NZ, :] for i in range(3)]
         for x in range(NX):
             star = star_row(x, rows, ylo, yhi, f, vel[x], zs.at[f * NX + x], lane)
@@ -265,7 +274,13 @@
             send[pl.ds(b * SLOT + t, GX, stride=BLK), :] = val
 
 
-def scan_kernel(sx, recv, wmain, t12, cs, rrev, misc, absd, msg, keep, cols, kink):
+def own_tables(tabs):
+    n = 2 * TX
+    return tabs.at[0:n], tabs.at[n : 2 * n], tabs.at[2 * n : 3 * n], tabs.at[3 * n : 3 * n + 16]
+
+
+def scan_kernel(recv, wmain, t12, cs, tabs, absd, after, msg, keep, cols, kink):
+    rpow, rrev, misc, rowtab = own_tables(tabs)
     lane = iota((2 * TX, NY), 1)
     d = dot(wmain[...], recv[...])
     ends = []
@@ -278,14 +293,14 @@
     bwd = d
     for k in range(7):
         s = 1 << k
-        a = jnp.broadcast_to(misc[0, :, k : k + 1], (2 * TX, NY))
+        a = jnp.broadcast_to(misc[:, k : k + 1], (2 * TX, NY))
         fwd = fwd + jnp.where(lane >= s, a * pltpu.roll(fwd, s, 1), 0.0)
         bwd = bwd + jnp.where(lane < NY - s, a * pltpu.roll(bwd, NY - s, 1), 0.0)
-    r1 = misc[0, :, 0:1]
-    r128 = misc[0, :, 7:8]
+    r1 = misc[:, 0:1]
+    r128 = misc[:, 7:8]
     out_right = r1 * fwd[:, NY - 1 : NY] + e
     out_left = bwd[:, 0:1] + r128 * e
-    keep[...] = fwd + bwd - d + rrev[0] * e
+    keep[...] = fwd + bwd - d + rrev[...] * e
     table = jnp.where(lane == 0, out_right, jnp.where(lane == 1, out_left, 0.0))
     d8 = d[0:8]
     e8 = e[0:8]
@@ -302,16 +317,17 @@
     kink[...] = dot(d8, absd[...]) + e8 * (float(NY) - lanef)
 
 
-def solve_kernel(sx, got, keep, cols, kink, wback, t12t, cs, rpow, rrev, misc, rowtab, send):
-    here = sx[1]
-    first = (sx[0] == 0).astype(F32)
+def solve_kernel(got, keep, cols, kink, wback, t12t, cs, tabs, after, send):
+    rpow, rrev, misc, rowtab = own_tables(tabs)
+    here = lax.axis_index("gy")
+    first = (lax.axis_index("gx") == 0).astype(F32)
     who = iota((GY, 2 * TX), 0)
     all_right = jnp.concatenate([got[y * 8 : y * 8 + 1, :] for y in range(GY)], axis=0)
     all_left = jnp.concatenate([got[y * 8 + 1 : y * 8 + 2, :] for y in range(GY)], axis=0)
     s0 = jnp.concatenate([got[y * 8 + 2 : y * 8 + 3, 0:1] for y in range(GY)], axis=0)
     s1 = jnp.concatenate([got[y * 8 + 3 : y * 8 + 4, 0:1] for y in range(GY)], axis=0)
-    lnr = rowtab[0, 0:1, :]
-    inv = rowtab[0, 1:2, :]
+    lnr = jnp.concatenate([rowtab[0:1, :], rowtab[8:9, :]], axis=1)
+    inv = jnp.concatenate([rowtab[1:2, :], rowtab[9:10, :]], axis=1)
     after = ((here - who - 1) & (GY - 1)).astype(F32)
     before = ((who - here - 1) & (GY - 1)).astype(F32)
     in_left = jnp.sum(jnp.exp(after * lnr) * all_right, axis=0, keepdims=True) * inv
@@ -320,9 +336,9 @@
     turned = jnp.where(row == 0, in_left, jnp.where(row == 1, in_right, 0.0)).T
     in_left = turned[:, 0:1]
     in_right = turned[:, 1:2]
-    coef = misc[0, :, 8:9]
-    pres = coef * (keep[...] + rpow[0] * in_left + rrev[0] * in_right)
-    edge = coef * (cols[:, 0:1] + misc[0, :, 7:8] * in_left + in_right)
+    coef = misc[:, 8:9]
+    pres = coef * (keep[...] + rpow[...] * in_left + rrev[...] * in_right)
+    edge = coef * (cols[:, 0:1] + misc[:, 7:8] * in_left + in_right)
     who1 = iota((GY, 1), 0)
     far = (NY * ((here - who1) & (GY - 1))).astype(F32)
     mine = who1 == here
@@ -349,8 +365,8 @@
 def store_table(lhs, n, table):
     turned = table.T
     hi = turned.astype(BF16)
-    lhs[n * NY : (n + 1) * NY, :] = hi
-    lhs[(n + 1) * NY : (n + 2) * NY, :] = (turned - hi.astype(F32)).astype(BF16)
+    lhs[n * NY : (n + 1) * NY, 0:ROWS] = hi
+    lhs[n * NY : (n + 1) * NY, ROWS:] = (turned - hi.astype(F32)).astype(BF16)
 
 
 def masks_of(cells):
@@ -362,22 +378,19 @@
 
 
 def gather_one(lhs, n, hot, pick):
-    hi = jnp.dot(lhs[n * NY : (n + 1) * NY, :], hot, preferred_element_type=F32)
-    lo = jnp.dot(lhs[(n + 1) * NY : (n + 2) * NY, :], hot, preferred_element_type=F32)
-    return jnp.sum(jnp.where(pick, hi + lo, 0.0), axis=0, keepdims=True)
+    both = jnp.concatenate([hot, hot], axis=0)
+    got = jnp.dot(lhs[n * NY : (n + 1) * NY, :], both, preferred_element_type=F32)
+    return jnp.sum(jnp.where(pick, got, 0.0), axis=0, keepdims=True)
 
 
 CHUNK = 512
 
 
-def drop_kernel(
-    u, v, w, h, q, mlo, mhi, clo, chi, drops, cells, counts,
-    heat_next, moist_next, cell_out, state, zs, stars, lhs, acc, air,
-):
+def heat_kernel(fields, mid, mlo, mhi, clo, chi, after, stars, lhs, cell_out, state, zs):
     lane = iota((NZ, NY), 1)
     ylo = yhalo_of(mlo)
     yhi = yhalo_of(mhi)
-    vel = [velocity_rows(u, v, w, x) for x in range(NX)]
+    vel = [velocity_rows(fields, x) for x in range(NX)]
 
     def side(msg, n):
         parts = []
@@ -387,15 +400,15 @@
             parts.append(msg[a : a + 8, c : c + NY])
         return jnp.concatenate(parts, axis=0)
 
-    for f, ref in enumerate((h, q)):
+    for f in range(2):
         rows = [side(clo, f * 3 + i) for i in range(3)]
-        rows += [row_of(ref, x) for x in range(NX)]
+        rows += [field_row(fields, 3 + f, x) for x in range(NX)]
         rows += [side(chi, f * 3 + i) for i in range(3)]
         for x in range(NX):
             star = star_row(x, rows, ylo, yhi, 3 + f, vel[x], zs.at[f * NX + x], lane)
             at = (f * NX + x) * NZ
             stars[at : at + NZ, :] = star
-        store_table(lhs, 2 * f, stars[f * ROWS : (f + 1) * ROWS, :])
+        store_table(lhs, f, stars[f * ROWS : (f + 1) * ROWS, :])
     for r in range(3):
         for s in range(3):
             n = r * 3 + s
@@ -403,12 +416,8 @@
                 block = block_of(clo, s)
             elif r == 2:
                 block = block_of(chi, s)
-            elif s == 0:
-                block = block_of(mlo, 1)
-            elif s == 2:
-                block = block_of(mhi, 1)
             else:
-                block = own_block(drops, cells, counts, 4)
+                block = block_of((mlo, mid, mhi)[s], 1)
             values, cell, count = block
             for a in range(10):
                 state[a, n : n + 1, :] = values[a : a + 1]
@@ -416,12 +425,14 @@
             slot = iota((1, CAP), 1).astype(F32)
             state[10, n : n + 1, :] = jnp.where(slot < count, 1.0, 0.0)
 
+
+def growth_kernel(lhs, cell, state, after, state_out, gain_out, air):
     def gather_block(n, carry):
         for c in range(CAP // CHUNK):
             at = c * CHUNK
-            hot, pick = masks_of(cell_out[pl.ds(n, 1), at : at + CHUNK])
+            hot, pick = masks_of(cell[pl.ds(n, 1), at : at + CHUNK])
             for f in range(2):
-                air[f, pl.ds(n, 1), at : at + CHUNK] = gather_one(lhs, 2 * f, hot, pick)
+                air[f, pl.ds(n, 1), at : at + CHUNK] = gather_one(lhs, f, hot, pick)
         return carry
 
     lax.fori_loop(0, 9, gather_block, 0)
@@ -434,23 +445,25 @@
         saturation - CURVATURE / radius + SOLUTE_EFFECT * state[8] / cubed
     )
     new_radius = jnp.sqrt(jnp.maximum(squared, RADIUS_FLOOR * RADIUS_FLOOR))
-    gain = live * state[7] * (new_radius * new_radius * new_radius - cubed)
-    air[0] = gain
-    state[6] = new_radius * live
-    state[7] = state[7] * live
-    state[8] = state[8] * live
-    state[9] = (state[9] + DT) * live
+    gain_out[...] = live * state[7] * (new_radius * new_radius * new_radius - cubed)
+    state_out[6] = new_radius * live
+    state_out[7] = state[7] * live
+    state_out[8] = state[8] * live
+    state_out[9] = (state[9] + DT) * live
     for a in range(3):
-        state[a] = state[a] * live
-        state[3 + a] = state[3 + a] * (keeping * live)
-    state[10] = (1.0 - keeping) * live
+        state_out[a] = state[a] * live
+        state_out[3 + a] = state[3 + a] * (keeping * live)
+    state_out[10] = (1.0 - keeping) * live
+
+
+def scatter_kernel(stars, cell, gain, after, heat_next, moist_next, acc):
     acc[...] = jnp.zeros_like(acc)
 
     def scatter_block(n, carry):
         for c in range(CAP // CHUNK):
             at = c * CHUNK
-            hot, pick = masks_of(cell_out[pl.ds(n, 1), at : at + CHUNK])
-            g = air[0, pl.ds(n, 1), at : at + CHUNK]
+            hot, pick = masks_of(cell[pl.ds(n, 1), at : at + CHUNK])
+            g = gain[pl.ds(n, 1), at : at + CHUNK]
             hi = g.astype(BF16).astype(F32)
             lo = g - hi
             z = jnp.concatenate(
@@ -505,14 +518,14 @@
             ref[pl.ds(x, NZ, stride=NX), :] = val
             next_rows[f, x * NZ : (x + 1) * NZ, :] = val
     for f in range(3):
-        store_table(lhs, 2 * f, next_rows[f])
+        store_table(lhs, f, next_rows[f])
 
     def gather_block(n, carry):
         for c in range(CAP // CHUNK):
             at = c * CHUNK
             hot, pick = masks_of(cell[pl.ds(n, 1), at : at + CHUNK])
             for f in range(3):
-                air[f, pl.ds(n, 1), at : at + CHUNK] = gather_one(lhs, 2 * f, hot, pick)
+                air[f, pl.ds(n, 1), at : at + CHUNK] = gather_one(lhs, f, hot, pick)
         return carry
 
     lax.fori_loop(0, 9, gather_block, 0)
@@ -520,38 +533,37 @@
     for a in range(3):
         speed = air[a] * mix + state[3 + a]
         offset = state[a] + DT * speed
-        for n in range(9):
-            drops_out[n, 3 + a : 4 + a, :] = speed[n : n + 1]
-            drops_out[n, a : a + 1, :] = offset[n : n + 1]
-    for n in range(9):
-        for a in range(6, 10):
-            drops_out[n, a : a + 1, :] = state[a, n : n + 1, :]
+        for r in range(3):
+            drops_out[r, 3 + a] = speed[3 * r : 3 * r + 3]
+            drops_out[r, a] = offset[3 * r : 3 * r + 3]
+    for a in range(6, 10):
+        for r in range(3):
+            drops_out[r, a] = state[a, 3 * r : 3 * r + 3, :]
 
 
 VM = pl.BlockSpec(memory_space=pltpu.VMEM)
 SM = pl.BlockSpec(memory_space=pltpu.SMEM)
+ANY = pl.BlockSpec(memory_space=pl.ANY)
+HBM = pl.BlockSpec(memory_space=pltpu.HBM)
 
 
 def sds(*shape, dtype=F32):
     return jax.ShapeDtypeStruct(shape, dtype)
 
 
-def params():
-    return pltpu.CompilerParams(vmem_limit_bytes=48 * 1024 * 1024)
-
-
-def cost(us):
-    return pl.CostEstimate(flops=int(us * 5e8), bytes_accessed=int(us * 2e6), transcendentals=0)
-
-
-def whole(shape):
-    zeros = (0,) * len(shape)
-    return pl.BlockSpec(shape, lambda i, s: zeros)
-
-
-def chosen(shape):
-    zeros = (0,) * (len(shape) - 1)
-    return pl.BlockSpec(shape, lambda i, s: (s[0],) + zeros)
+def call(kernel, name, us, out_shape, in_specs, scratch=(), mib=12):
+    return pl.pallas_call(
+        kernel,
+        out_shape=out_shape,
+        in_specs=in_specs,
+        out_specs=tuple(VM for _ in out_shape),
+        scratch_shapes=list(scratch),
+        compiler_params=pltpu.CompilerParams(vmem_limit_bytes=mib * 1024 * 1024),
+        cost_estimate=pl.CostEstimate(
+            flops=int(us * 5e8), bytes_accessed=int(us * 2e6), transcendentals=0
+        ),
+        name=name,
+    )
 
 
 def ring(axis, shift):
@@ -559,140 +571,99 @@
     return [(i, (i + shift) % count) for i in range(count)]
 
 
-def per_device(u, v, w, h, q, droplets, cell_index, block_count):
+def per_device(u, v, w, h, q, droplets, cells, counts):
     tab = make_tables()
     u, v, w, h, q = (a.reshape(ROWS, NY) for a in (u, v, w, h, q))
-    drops = droplets.reshape(9, 10, CAP)
-    cells = cell_index.reshape(9, CAP)
-    counts = block_count.reshape(9)
-    xlo, xhi, up, down = pl.pallas_call(
+    drops = droplets.transpose(0, 2, 1, 3)
+    xlo, xhi, up, down, mid, fields, tabs = call(
         pack_kernel,
-        out_shape=(sds(9 * NZ, NY), sds(9 * NZ, NY), sds(48, CAP), sds(48, CAP)),
-        in_specs=[VM] * 7 + [SM],
-        out_specs=(VM,) * 4,
-        compiler_params=params(),
-        cost_estimate=cost(1.5),
-        name="pack",
-    )(u, v, w, h, q, drops, cells, counts)
+        "pack",
+        2.5,
+        (
+            sds(9 * NZ, NY), sds(9 * NZ, NY), sds(48, CAP), sds(48, CAP), sds(40, CAP),
+            sds(5 * ROWS, NY), sds(6 * TX + 16, NY),
+        ),
+        [HBM] * 6 + [VM, SM, HBM],
+        [pltpu.VMEM((3, 10, 3, CAP), F32), pltpu.SemaphoreType.DMA((7,))],
+    )(u, v, w, h, q, drops, cells, counts, tab["own"])
+    mlo = lax.ppermute(up, "gy", ring("gy", 1))
+    mhi = lax.ppermute(down, "gy", ring("gy", -1))
     xlo = lax.ppermute(xlo, "gx", ring("gx", 1))
     xhi = lax.ppermute(xhi, "gx", ring("gx", -1))
-    mlo = lax.ppermute(up, "gy", ring("gy", 1))
-    mhi = lax.ppermute(down, "gy", ring("gy", -1))
-    cup, cdown = pl.pallas_call(
-        relay_kernel,
-        out_shape=(sds(64, CAP), sds(64, CAP)),
-        in_specs=[VM] * 4 + [SM] + [VM] * 2,
-        out_specs=(VM, VM),
-        compiler_params=params(),
-        cost_estimate=cost(1.0),
-        name="relay",
-    )(h, q, drops, cells, counts, mlo, mhi)
+    cup, cdown = call(
+        relay_kernel, "relay", 1.0, (sds(64, CAP), sds(64, CAP)), [VM] * 4
+    )(fields, mid, mlo, mhi)
     clo = lax.ppermute(cup, "gx", ring("gx", 1))
     chi = lax.ppermute(cdown, "gx", ring("gx", -1))
-    stars, send = pl.pallas_call(
+    stars, send = call(
         wind_kernel,
-        out_shape=(sds(3 * ROWS, NY), sds(GX * BLK, NY)),
-        in_specs=[VM] * 8,
-        out_specs=(VM, VM),
-        scratch_shapes=[pltpu.VMEM((3 * NX, NZ + 16, NY), F32)],
-        compiler_params=params(),
-        cost_estimate=cost(3.0),
-        name="winds",
-    )(u, v, w, xlo, xhi, mlo, mhi, tab["ztab"])
+        "winds",
+        3.0,
+        (sds(3 * ROWS, NY), sds(GX * BLK, NY)),
+        [VM] * 6 + [ANY],
+        [pltpu.VMEM((3 * NX, NZ + 16, NY), F32)],
+    )(fields, xlo, xhi, mlo, mhi, tab["ztab"], cup)
     recv = lax.all_to_all(send.reshape(GX, BLK, NY), "gx", 0, 0, tiled=True)
-    heat_next, moist_next, cell_in, state = pl.pallas_call(
-        drop_kernel,
-        out_shape=(
-            sds(ROWS, NY), sds(ROWS, NY), sds(9, CAP, dtype=jnp.int32), sds(11, 9, CAP),
+    stars_hq, lhs, cell_in, state = call(
+        heat_kernel,
+        "heat",
+        3.0,
+        (
+            sds(2 * ROWS, NY), sds(2 * NY, 2 * ROWS, dtype=BF16),
+            sds(9, CAP, dtype=jnp.int32), sds(11, 9, CAP),
         ),
-        in_specs=[VM] * 11 + [SM],
-        out_specs=(VM,) * 4,
-        scratch_shapes=[
-            pltpu.VMEM((2 * NX, NZ + 16, NY), F32),
-            pltpu.VMEM((2 * ROWS, NY), F32),
-            pltpu.VMEM((4 * NY, ROWS), BF16),
-            pltpu.VMEM((ROWS, 2 * NY), F32),
-            pltpu.VMEM((2, 9, CAP), F32),
-        ],
-        compiler_params=params(),
-        cost_estimate=cost(10.0),
-        name="growth",
-    )(u, v, w, h, q, mlo, mhi, clo, chi, drops, cells, counts)
-    place = jnp.stack([lax.axis_index("gx"), lax.axis_index("gy")]).astype(jnp.int32)
-    msg, keep, cols, kink = pl.pallas_call(
+        [VM] * 6 + [ANY],
+        [pltpu.VMEM((2 * NX, NZ + 16, NY), F32)],
+    )(fields, mid, mlo, mhi, clo, chi, stars)
+    msg, keep, cols, kink = call(
         scan_kernel,
-        out_shape=(sds(8 * GY, 2 * TX), sds(2 * TX, NY), sds(2 * TX, NY), sds(8, NY)),
-        grid_spec=pltpu.PrefetchScalarGridSpec(
-            num_scalar_prefetch=1,
-            grid=(1,),
-            in_specs=[
-                whole((GX * BLK, NY)),
-                whole((2 * TX, GX * BLK)),
-                whole((2 * TX, GX)),
-                whole((2 * TX, NY)),
-                chosen((1, 2 * TX, NY)),
-                chosen((1, 2 * TX, NY)),
-                whole((NY, NY)),
-            ],
-            out_specs=[
-                whole((8 * GY, 2 * TX)), whole((2 * TX, NY)), whole((2 * TX, NY)), whole((8, NY)),
-            ],
-        ),
-        compiler_params=params(),
-        cost_estimate=cost(2.0),
-        name="scan",
+        "scan",
+        2.0,
+        (sds(8 * GY, 2 * TX), sds(2 * TX, NY), sds(2 * TX, NY), sds(8, NY)),
+        [VM] * 6 + [ANY],
     )(
-        place, recv.reshape(GX * BLK, NY), tab["wmain"], tab["t12"], tab["cs"],
-        tab["rrev"], tab["misc"], tab["absd"],
+        recv.reshape(GX * BLK, NY), tab["wmain"], tab["t12"], tab["cs"], tabs, tab["absd"], state
     )
     got = lax.all_to_all(msg.reshape(GY, 8, 2 * TX), "gy", 0, 0, tiled=True)
-    send = pl.pallas_call(
-        solve_kernel,
-        out_shape=sds(GX * BLK, NY),
-        grid_spec=pltpu.PrefetchScalarGridSpec(
-            num_scalar_prefetch=1,
-            grid=(1,),
-            in_specs=[
-                whole((8 * GY, 2 * TX)),
-                whole((2 * TX, NY)),
-                whole((2 * TX, NY)),
-                whole((8, NY)),
-                whole((GX * BLK, 2 * TX)),
-                whole((GX, 2 * TX)),
-                whole((2 * TX, NY)),
-                chosen((1, 2 * TX, NY)),
-                chosen((1, 2 * TX, NY)),
-                chosen((1, 2 * TX, NY)),
-                chosen((1, 8, 2 * TX)),
-            ],
-            out_specs=whole((GX * BLK, NY)),
-        ),
-        compiler_params=params(),
-        cost_estimate=cost(2.0),
-        name="solve",
+    state, gain = call(
+        growth_kernel,
+        "growth",
+        5.0,
+        (sds(11, 9, CAP), sds(9, CAP)),
+        [VM] * 3 + [ANY],
+        [pltpu.VMEM((2, 9, CAP), F32)],
+    )(lhs, cell_in, state, keep)
+    (send,) = call(
+        solve_kernel, "solve", 2.0, (sds(GX * BLK, NY),), [VM] * 8 + [ANY]
     )(
-        place, got.reshape(8 * GY, 2 * TX), keep, cols, kink, tab["wback"], tab["t12t"],
-        tab["cs"], tab["rpow"], tab["rrev"], tab["misc"], tab["rowtab"],
+        got.reshape(8 * GY, 2 * TX), keep, cols, kink, tab["wback"], tab["t12t"], tab["cs"], tabs,
+        gain,
     )
     recv = lax.all_to_all(send.reshape(GX, BLK, NY), "gx", 0, 0, tiled=True)
-    east_next, north_next, up_next, drops_out = pl.pallas_call(
+    heat_next, moist_next = call(
+        scatter_kernel,
+        "scatter",
+        4.0,
+        (sds(ROWS, NY), sds(ROWS, NY)),
+        [VM] * 3 + [ANY],
+        [pltpu.VMEM((ROWS, 2 * NY), F32)],
+    )(stars_hq, cell_in, gain, send)
+    east_next, north_next, up_next, drops_out = call(
         final_kernel,
-        out_shape=(sds(ROWS, NY), sds(ROWS, NY), sds(ROWS, NY), sds(9, 10, CAP)),
-        in_specs=[VM] * 5,
-        out_specs=(VM,) * 4,
-        scratch_shapes=[
-            pltpu.VMEM((6 * NY, ROWS), BF16),
+        "final",
+        8.0,
+        (sds(ROWS, NY), sds(ROWS, NY), sds(ROWS, NY), sds(3, 10, 3, CAP)),
+        [VM] * 5,
+        [
+            pltpu.VMEM((3 * NY, 2 * ROWS), BF16),
             pltpu.VMEM((3, ROWS, NY), F32),
             pltpu.VMEM((3, 9, CAP), F32),
         ],
-        compiler_params=params(),
-        cost_estimate=cost(8.0),
-        name="final",
     )(recv.reshape(GX * BLK, NY), stars, tab["zback"], cell_in, state)
-    fields = (
+    out = (
         a.reshape(NZ, NX, NY) for a in (east_next, north_next, up_next, heat_next, moist_next)
     )
-    return (*fields, drops_out.reshape(3, 3, 10, CAP))
+    return (*out, drops_out.transpose(0, 2, 1, 3))
 
 
 def solution(mesh):

time: 108 us -> 88.5 us (0.82)
  local copies, waits for them, and re-layouts: 32.3 us -> 17.6 us
  starting transfers between devices: 35.8 us -> 32.5 us
    unnamed x104 -> x58, local copies, waits for them, and re-layouts: 30.7 us -> 17.6 us
    all_to_all x2, starting transfers between devices: 10.1 us -> 7.09 us  [per_device(): recv = lax.all_to_all(send.reshape(GX, BLK, NY), 'gx', 0, 0, tiled=True)]
    all_to_all x1, waiting for transfers between devices: 0.01 us -> 2.74 us  [per_device(): got = lax.all_to_all(msg.reshape(GY, 8, 2 * TX), 'gy', 0, 0, tiled=True)]
    ppermute x1, waiting for transfers between devices: 2.41 us -> 0.01 us  [per_device(): xlo = lax.ppermute(xlo, 'gx', ring('gx', 1))]
    reshape x2 -> x0, local copies, waits for them, and re-layouts: 1.61 us -> none  [the longest x1 0.82 us: per_device(): cells = cell_index.reshape(9, CAP)]
    pallas_call x7 -> x9, Pallas kernels: 28 us -> 27.5 us  [the longest x1 7.82 us: per_device(): call(final_kernel, 'final', 8.0, (sds(ROWS, NY), sds(ROWS, NY), sds(ROWS,...]
  transfers between devices with their start and end apart: 9 -> 9, of which waited for: 2 -> 4; matrix products, arithmetic and copies ran while one was open for 1% -> 0% of each run, Pallas kernels for 15% -> 15%
where the time goes in v2:
time: 88.5 us; the launch traced here: 87.7 us
  starting transfers between devices  32.5 us (37%)
  Pallas kernels  27.5 us (31%)
  local copies, waits for them, and re-layouts  17.6 us (20%)
  waiting for transfers between devices  9.32 us (11%)
    unnamed x58, local copies, waits for them, and re-layouts  17.6 us
    all_to_all x1, starting transfers between devices, per_device(): got = lax.all_to_all(msg.reshape(GY, 8, 2 * TX), 'gy', 0, 0, tiled=True)  12.2 us
    pallas_call x1, Pallas kernels, per_device(): call(final_kernel, 'final', 8.0, (sds(ROWS, NY), sds(ROWS, NY), sds(ROWS,...  7.82 us
    all_to_all x2, starting transfers between devices, per_device(): recv = lax.all_to_all(send.reshape(GX, BLK, NY), 'gx', 0, 0, tiled=True)  7.09 us
    all_to_all x2, waiting for transfers between devices, per_device(): recv = lax.all_to_all(send.reshape(GX, BLK, NY), 'gx', 0, 0, tiled=True)  6.21 us
    pallas_call x1, Pallas kernels, per_device(): call(growth_kernel, 'growth', 5.0, (sds(11, 9, CAP), sds(9, CAP)), [VM] *...  4.59 us
    pallas_call x1, Pallas kernels, per_device(): call(scatter_kernel, 'scatter', 4.0, (sds(ROWS, NY), sds(ROWS, NY)), [VM]...  3.99 us
    ppermute x1, starting transfers between devices, per_device(): xhi = lax.ppermute(xhi, 'gx', ring('gx', -1))  3.81 us
  transfers between devices with their start and end apart: 9, of which 4 were waited for; matrix products, arithmetic and copies ran while one was open for 0% of the time, Pallas kernels for 15%

profile of v2, /device:TPU:1, one launch (start us, length us, event | category | flops | bytes accessed | tf_op | source)
XLA Modules:
  0.0 87.7 jit_solution(14730464246164876564)
XLA Ops:
  0.6 0.0 copy-start.16
  0.6 0.0 copy-start
  0.7 2.8 %copy-done = f32[16,784,128]{2,1,0:T(8,128)S(1)} copy-done((f32[16,784,128]{2,1,0:T(8,128)S(1)}, f32[16,784,128]{2,1,0:T(8,128)}, u32[]{:S(2)}) %copy-start) | copy-done | bytes 6422552
  3.5 1.0 %copy-done.1 = f32[3,3,10,1024]{3,1,2,0:T(4,128)S(1)} copy-done((f32[3,3,10,1024]{3,1,2,0:T(4,128)S(1)}, f32[3,3,10,1024]{3,1,2,0:T(4,128)}, u32[]{:S(2)}) %copy-start.1) | copy-done | bytes 368664
  4.5 0.9 %copy-done.2 = f32[32,8,128]{2,1,0:T(8,128)S(1)} copy-done((f32[32,8,128]{2,1,0:T(8,128)S(1)}, f32[32,8,128]{2,1,0:T(8,128)}, u32[]{:S(2)}) %copy-start.2) | copy-done | bytes 131096
  5.4 0.9 %copy-done.3 = f32[32,8,128]{2,1,0:T(8,128)S(1)} copy-done((f32[32,8,128]{2,1,0:T(8,128)S(1)}, f32[32,8,128]{2,1,0:T(8,128)}, u32[]{:S(2)}) %copy-start.3) | copy-done | bytes 131096
  6.3 0.9 %copy-done.4 = f32[32,8,128]{2,1,0:T(8,128)S(1)} copy-done((f32[32,8,128]{2,1,0:T(8,128)S(1)}, f32[32,8,128]{2,1,0:T(8,128)}, u32[]{:S(2)}) %copy-start.4) | copy-done | bytes 131096
  7.2 0.9 %copy-done.5 = f32[32,8,128]{2,1,0:T(8,128)S(1)} copy-done((f32[32,8,128]{2,1,0:T(8,128)S(1)}, f32[32,8,128]{2,1,0:T(8,128)}, u32[]{:S(2)}) %copy-start.5) | copy-done | bytes 131096
  8.1 0.9 %copy-done.6 = f32[32,8,128]{2,1,0:T(8,128)S(1)} copy-done((f32[32,8,128]{2,1,0:T(8,128)S(1)}, f32[32,8,128]{2,1,0:T(8,128)}, u32[]{:S(2)}) %copy-start.6) | copy-done | bytes 131096
  9.0 0.8 copy-done.7
  9.8 0.7 copy-done.8
  10.5 2.5 %pack.1 = (f32[288,128]{1,0:T(8,128)S(1)}, f32[288,128]{1,0:T(8,128)S(1)}, f32[48,1024]{1,0:T(8,128)S(1)}, f32[48,1024]{1,0:T(8,128)S(1)}, f32[40,1024]{1,0:T(8,...) custom-call(f32[256,128]{1,0:T(8,128)S(1)} %bitcast.21, f32[256,128]{1,0:T(8,128)S(1)} %bitcast.22, ...), custom_call_target="tpu_custom_call" | custom-call | flops 1250000000 | bytes 5000000 | tf_op jit(solution)/shard_map/pack/pallas_call | solution.py:578
  13.1 3.0 %collective-permute-start.2 = (f32[48,1024]{1,0:T(8,128)S(1)}, f32[48,1024]{1,0:T(8,128)S(1)}, u32[]{:S(2)}, u32[]{:S(2)}) collective-permute-start(f32[48,1024]{1,0:T(8,128)S(1)} %get-tuple-element.36), channel_id=1, source_target_pairs={{0,1},{1,2},{2,3},{3,4},{4,5},{5,6},{6,7},{7,8},{8,9},{9,10},{10,1... | collective-permute-start | bytes 589832 | tf_op jit(solution)/shard_map/ppermute | solution.py:589
  16.1 0.2 collective-permute-start.3
  16.3 1.0 %collective-permute-start = (f32[288,128]{1,0:T(8,128)S(1)}, f32[288,128]{1,0:T(8,128)S(1)}, u32[]{:S(2)}, u32[]{:S(2)}) collective-permute-start(f32[288,128]{1,0:T(8,128)S(1)} %get-tuple-element.34), channel_id=1, source_target_pairs={{0,16},{16,32},{32,48},{48,64},{64,80},{80,96},{96,112},{112,128},... | collective-permute-start | bytes 442376 | tf_op jit(solution)/shard_map/ppermute | solution.py:591
  17.3 3.8 %collective-permute-start.1 = (f32[288,128]{1,0:T(8,128)S(1)}, f32[288,128]{1,0:T(8,128)S(1)}, u32[]{:S(2)}, u32[]{:S(2)}) collective-permute-start(f32[288,128]{1,0:T(8,128)S(1)} %get-tuple-element.35), channel_id=1, source_target_pairs={{0,240},{16,0},{32,16},{48,32},{64,48},{80,64},{96,80},{112,96},{1... | collective-permute-start | bytes 442376 | tf_op jit(solution)/shard_map/ppermute | solution.py:592
  21.1 0.0 collective-permute-done.2.mlo
  21.1 0.4 collective-permute-done.3.mhi
  21.5 0.1 relay.1
  21.6 1.3 %collective-permute-start.4 = (f32[64,1024]{1,0:T(8,128)S(1)}, f32[64,1024]{1,0:T(8,128)S(1)}, u32[]{:S(2)}, u32[]{:S(2)}) collective-permute-start(f32[64,1024]{1,0:T(8,128)S(1)} %get-tuple-element.39.after), channel_id=1, source_target_pairs={{0,16},{16,32},{32,48},{48,64},{64,80},{80,96},{96,112},{112,128},... | collective-permute-start | bytes 786440 | tf_op jit(solution)/shard_map/ppermute | solution.py:596
  22.9 3.8 %collective-permute-start.5 = (f32[64,1024]{1,0:T(8,128)S(1)}, f32[64,1024]{1,0:T(8,128)S(1)}, u32[]{:S(2)}, u32[]{:S(2)}) collective-permute-start(f32[64,1024]{1,0:T(8,128)S(1)} %get-tuple-element.42), channel_id=1, source_target_pairs={{0,240},{16,0},{32,16},{48,32},{64,48},{80,64},{96,80},{112,96},{1... | collective-permute-start | bytes 786440 | tf_op jit(solution)/shard_map/ppermute | solution.py:597
  26.7 0.0 collective-permute-done.xlo
  26.7 0.0 collective-permute-done.1.xhi
  26.7 0.0 copy-done.16
  26.7 3.0 %winds.1 = (f32[768,128]{1,0:T(8,128)S(1)}, f32[384,128]{1,0:T(8,128)}) custom-call(f32[1280,128]{1,0:T(8,128)S(1)} %get-tuple-element.33.fields, f32[288,128]{1,0:T(8,128)S(1)} %collective-permute-done.xlo, f32[288,128]{1,0:T(8,128)S(1)} %collective-permute-done.1.xhi, f32[48,1024]{1,0:T(8,128)S(1)} %collective-permute-done.2.mlo, ...), custom_call_target="tpu_custom_call" | custom-call | flops 1500000000 | bytes 6000000 | tf_op jit(solution)/shard_map/winds/pallas_call | solution.py:598
  29.7 0.7 copy-done.19
  30.4 3.5 %all-to-all-start = ((f32[16,24,128]{2,1,0:T(8,128)}), f32[16,24,128]{2,1,0:T(8,128)S(1)}, u32[]{:S(2)}, u32[]{:S(2)}) async-start(f32[16,24,128]{2,1,0:T(8,128)} %bitcast.6), calls=%async_computation | async-start | bytes 393216 | tf_op jit(solution)/shard_map/all_to_all | solution.py:606
  33.9 0.0 collective-permute-done.4.clo
  33.9 0.0 collective-permute-done.5.chi
  33.9 0.0 copy-start.20
  34.0 1.0 %copy-done.20 = f32[768,128]{1,0:T(8,128)S(1)} copy-done((f32[768,128]{1,0:T(8,128)S(1)}, f32[768,128]{1,0:T(8,128)}, u32[]{:S(2)}) %copy-start.20) | copy-done | bytes 393240
  34.9 1.6 %heat.1 = (f32[512,128]{1,0:T(8,128)S(1)}, bf16[256,512]{1,0:T(8,128)(2,1)S(1)}, s32[9,1024]{1,0:T(8,128)S(1)}, f32[11,9,1024]{2,1,0:T(8,128)S(1)}) custom-call(f32[1280,128]{1,0:T(8,128)S(1)} %get-tuple-element.33.fields, f32[40,1024]{1,0:T(8,128)S(1)} %get-tuple-element.38.mid, f32[48,1024]{1,0:T(8,128)S(1)} %collective-permute-done.2.mlo, ...), custom_call_target="tpu_custom_call" | custom-call | flops 1500000000 | bytes 6000000 | tf_op jit(solution)/shard_map/heat/pallas_call | solution.py:607
  36.6 0.0 copy-start.17
  36.6 0.9 copy-done.17
  37.5 0.7 copy-done.22
  38.2 0.7 copy-done.24
  38.9 2.2 %all-to-all-done = f32[16,24,128]{2,1,0:T(8,128)S(1)} async-done(((f32[16,24,128]{2,1,0:T(8,128)}), f32[16,24,128]{2,1,0:T(8,128)S(1)}, u32[]{:S(2)}, u32[]{:S(2)}) %all-to-all-start) | async-done | bytes 196640 | tf_op jit(solution)/shard_map/all_to_all | solution.py:606
  41.1 0.0 copy-done.10
  41.1 0.0 copy-done.11
  41.1 0.0 copy-done.12
  41.1 0.0 copy-start.13
  41.1 0.8 copy-done.13
  41.9 1.1 %copy-done.18 = f32[11,9,1024]{2,1,0:T(8,128)S(1)} copy-done((f32[11,9,1024]{2,1,0:T(8,128)S(1)}, f32[11,9,1024]{2,1,0:T(8,128)}, u32[]{:S(2)}) %copy-start.18) | copy-done | bytes 405528
  43.0 2.1 %scan.1 = (f32[128,256]{1,0:T(8,128)}, f32[256,128]{1,0:T(8,128)S(1)}, f32[256,128]{1,0:T(8,128)S(1)}, f32[8,128]{1,0:T(8,128)S(1)}) custom-call(f32[384,128]{1,0:T(8,128)S(1)} %bitcast.19, f32[256,384]{1,0:T(8,128)S(1)} %copy-done.10, f32[256,16]{1,0:T(8,128)S(1)} %copy-done.12, f32[256,128]{1,0:T(8,128)S(1)} %copy-done.11, ...), custom_call_target="tpu_custom_call" | custom-call | flops 1000000000 | bytes 4000000 | tf_op jit(solution)/shard_map/scan/pallas_call | solution.py:618
  45.2 12.2 %all-to-all-start.1 = ((f32[16,8,256]{2,1,0:T(8,128)}), f32[16,8,256]{2,1,0:T(8,128)S(1)}, u32[]{:S(2)}, u32[]{:S(2)}) async-start(f32[16,8,256]{2,1,0:T(8,128)} %bitcast.8), calls=%async_computation.1 | async-start | bytes 262144 | tf_op jit(solution)/shard_map/all_to_all | solution.py:627
  57.4 0.0 copy-done.26
  57.4 0.0 copy-start.25
  57.4 0.9 %copy-done.25 = bf16[256,512]{1,0:T(8,128)(2,1)S(1)} copy-done((bf16[256,512]{1,0:T(8,128)(2,1)S(1)}, bf16[256,512]{1,0:T(8,128)(2,1)}, u32[]{:S(2)}) %copy-start.25) | copy-done | bytes 262168
  58.4 0.8 copy-done.27
  59.2 4.6 %growth.1 = (f32[11,9,1024]{2,1,0:T(8,128)S(1)}, f32[9,1024]{1,0:T(8,128)S(1)}) custom-call(bf16[256,512]{1,0:T(8,128)(2,1)S(1)} %copy-done.25, s32[9,1024]{1,0:T(8,128)S(1)} %copy-done.27, f32[11,9,1024]{2,1,0:T(8,128)S(1)} %copy-done.18, f32[256,128]{1,0:T(8,128)S(1)} %get-tuple-element.46.after.keep), custom_call_target="tpu_custom_call" | custom-call | flops 2500000000 | bytes 10000000 | tf_op jit(solution)/shard_map/growth/pallas_call | solution.py:628
  63.8 0.0 copy-start.14
  63.8 0.0 copy-start.21
  63.8 2.7 %all-to-all-done.1 = f32[16,8,256]{2,1,0:T(8,128)S(1)} async-done(((f32[16,8,256]{2,1,0:T(8,128)}), f32[16,8,256]{2,1,0:T(8,128)S(1)}, u32[]{:S(2)}, u32[]{:S(2)}) %all-to-all-start.1) | async-done | bytes 131104 | tf_op jit(solution)/shard_map/all_to_all | solution.py:627
  66.6 0.0 copy-done.9
  66.6 0.0 copy-done.15
  66.6 1.7 %solve.1.after = f32[384,128]{1,0:T(8,128)} custom-call(f32[128,256]{1,0:T(8,128)S(1)} %bitcast.26, f32[256,128]{1,0:T(8,128)S(1)} %get-tuple-element.46.after.keep, f32[256,128]{1,0:T(8,128)S(1)} %get-tuple-element.47.cols, f32[8,128]{1,0:T(8,128)S(1)} %get-tuple-element.48.kink, f32[384,256]{1,0:T(8,128)S(1)} %copy-done.9, f32[16,256]{1,0:T(8,128)S(1)} %copy-done.15, ...), custom_call_target="tpu_custom_call" | custom-call | flops 1000000000 | bytes 4000000 | tf_op jit(solution)/shard_map/solve/pallas_call | solution.py:636
  68.3 3.6 %all-to-all-start.2 = ((f32[16,24,128]{2,1,0:T(8,128)}), f32[16,24,128]{2,1,0:T(8,128)S(1)}, u32[]{:S(2)}, u32[]{:S(2)}) async-start(f32[16,24,128]{2,1,0:T(8,128)} %bitcast.10), calls=%async_computation.2 | async-start | bytes 393216 | tf_op jit(solution)/shard_map/all_to_all | solution.py:642
  71.9 0.0 copy-done.23
  71.9 0.0 copy-done.28
  71.9 4.0 %scatter.1 = (f32[256,128]{1,0:T(8,128)}, f32[256,128]{1,0:T(8,128)}) custom-call(f32[512,128]{1,0:T(8,128)S(1)} %copy-done.23, s32[9,1024]{1,0:T(8,128)S(1)} %copy-done.28, f32[9,1024]{1,0:T(8,128)S(1)} %get-tuple-element.51.after.gain, f32[384,128]{1,0:T(8,128)} %solve.1.after), custom_call_target="tpu_custom_call" | custom-call | flops 2000000000 | bytes 8000000 | tf_op jit(solution)/shard_map/scatter/pallas_call | solution.py:643
  75.9 4.0 %all-to-all-done.2 = f32[16,24,128]{2,1,0:T(8,128)S(1)} async-done(((f32[16,24,128]{2,1,0:T(8,128)}), f32[16,24,128]{2,1,0:T(8,128)S(1)}, u32[]{:S(2)}, u32[]{:S(2)}) %all-to-all-start.2) | async-done | bytes 196640 | tf_op jit(solution)/shard_map/all_to_all | solution.py:642
  79.9 0.0 copy-done.14
  79.9 0.0 copy-done.21
  79.9 7.8 %final.1 = (f32[256,128]{1,0:T(8,128)}, f32[256,128]{1,0:T(8,128)}, f32[256,128]{1,0:T(8,128)}, f32[3,10,3,1024]{3,2,1,0:T(4,128)}) custom-call(f32[384,128]{1,0:T(8,128)S(1)} %bitcast.20, f32[768,128]{1,0:T(8,128)S(1)} %copy-done.21, f32[64,32]{1,0:T(8,128)S(1)} %copy-done.14, s32[9,1024]{1,0:T(8,128)S(1)} %copy-done.28, ...), custom_call_target="tpu_custom_call" | custom-call | flops 4000000000 | bytes 16000000 | tf_op jit(solution)/shard_map/final/pallas_call | solution.py:651
  (21 shorter events, 0.0 us)
Async XLA Ops:
  0.6 26.0 %copy-start.16 = (f32[32,32]{1,0:T(8,128)S(1)}, f32[32,32]{1,0:T(8,128)}, u32[]{:S(2)}) copy-start(f32[32,32]{1,0:T(8,128)} %constant.18.clone.ztab) | copy-start | bytes 12292
  0.6 2.8 %copy-start = (f32[16,784,128]{2,1,0:T(8,128)S(1)}, f32[16,784,128]{2,1,0:T(8,128)}, u32[]{:S(2)}) copy-start(f32[16,784,128]{2,1,0:T(8,128)} %constant.25.clone.own) | copy-start | bytes 19267588
  3.5 1.0 %copy-start.1 = (f32[3,3,10,1024]{3,1,2,0:T(4,128)S(1)}, f32[3,3,10,1024]{3,1,2,0:T(4,128)}, u32[]{:S(2)}) copy-start(f32[3,3,10,1024]{3,1,2,0:T(4,128)} %param.22) | copy-start | bytes 1105924
  4.5 0.9 %copy-start.2 = (f32[32,8,128]{2,1,0:T(8,128)S(1)}, f32[32,8,128]{2,1,0:T(8,128)}, u32[]{:S(2)}) copy-start(f32[32,8,128]{2,1,0:T(8,128)} %param.17) | copy-start | bytes 393220
  5.4 0.9 %copy-start.3 = (f32[32,8,128]{2,1,0:T(8,128)S(1)}, f32[32,8,128]{2,1,0:T(8,128)}, u32[]{:S(2)}) copy-start(f32[32,8,128]{2,1,0:T(8,128)} %param.18) | copy-start | bytes 393220
  6.3 0.9 %copy-start.4 = (f32[32,8,128]{2,1,0:T(8,128)S(1)}, f32[32,8,128]{2,1,0:T(8,128)}, u32[]{:S(2)}) copy-start(f32[32,8,128]{2,1,0:T(8,128)} %param.19) | copy-start | bytes 393220
  7.2 0.9 %copy-start.5 = (f32[32,8,128]{2,1,0:T(8,128)S(1)}, f32[32,8,128]{2,1,0:T(8,128)}, u32[]{:S(2)}) copy-start(f32[32,8,128]{2,1,0:T(8,128)} %param.20) | copy-start | bytes 393220
  8.1 0.9 %copy-start.6 = (f32[32,8,128]{2,1,0:T(8,128)S(1)}, f32[32,8,128]{2,1,0:T(8,128)}, u32[]{:S(2)}) copy-start(f32[32,8,128]{2,1,0:T(8,128)} %param.21) | copy-start | bytes 393220
  9.0 0.8 copy-start.7
  9.8 0.7 copy-start.8
  13.1 8.1 %collective-permute-start.2 = (f32[48,1024]{1,0:T(8,128)S(1)}, f32[48,1024]{1,0:T(8,128)S(1)}, u32[]{:S(2)}, u32[]{:S(2)}) collective-permute-start(f32[48,1024]{1,0:T(8,128)S(1)} %get-tuple-element.36), channel_id=1, source_target_pairs={{0,1},{1,2},{2,3},{3,4},{4,5},{5,6},{6,7},{7,8},{8,9},{9,10},{10,1... | collective-permute-start | bytes 589832 | tf_op jit(solution)/shard_map/ppermute | solution.py:589
  16.1 5.4 %collective-permute-start.3 = (f32[48,1024]{1,0:T(8,128)S(1)}, f32[48,1024]{1,0:T(8,128)S(1)}, u32[]{:S(2)}, u32[]{:S(2)}) collective-permute-start(f32[48,1024]{1,0:T(8,128)S(1)} %get-tuple-element.37), channel_id=1, source_target_pairs={{0,15},{1,0},{2,1},{3,2},{4,3},{5,4},{6,5},{7,6},{8,7},{9,8},{10,9... | collective-permute-start | bytes 589832 | tf_op jit(solution)/shard_map/ppermute | solution.py:590
  16.3 10.3 %collective-permute-start = (f32[288,128]{1,0:T(8,128)S(1)}, f32[288,128]{1,0:T(8,128)S(1)}, u32[]{:S(2)}, u32[]{:S(2)}) collective-permute-start(f32[288,128]{1,0:T(8,128)S(1)} %get-tuple-element.34), channel_id=1, source_target_pairs={{0,16},{16,32},{32,48},{48,64},{64,80},{80,96},{96,112},{112,128},... | collective-permute-start | bytes 442376 | tf_op jit(solution)/shard_map/ppermute | solution.py:591
  17.3 9.4 %collective-permute-start.1 = (f32[288,128]{1,0:T(8,128)S(1)}, f32[288,128]{1,0:T(8,128)S(1)}, u32[]{:S(2)}, u32[]{:S(2)}) collective-permute-start(f32[288,128]{1,0:T(8,128)S(1)} %get-tuple-element.35), channel_id=1, source_target_pairs={{0,240},{16,0},{32,16},{48,32},{64,48},{80,64},{96,80},{112,96},{1... | collective-permute-start | bytes 442376 | tf_op jit(solution)/shard_map/ppermute | solution.py:592
  21.5 19.6 %copy-start.10 = (f32[256,384]{1,0:T(8,128)S(1)}, f32[256,384]{1,0:T(8,128)}, u32[]{:S(2)}) copy-start(f32[256,384]{1,0:T(8,128)} %constant.20.clone.wmain) | copy-start | bytes 1179652
  21.5 19.6 %copy-start.11 = (f32[256,128]{1,0:T(8,128)S(1)}, f32[256,128]{1,0:T(8,128)}, u32[]{:S(2)}) copy-start(f32[256,128]{1,0:T(8,128)} %constant.24.clone.cs) | copy-start | bytes 393220
  21.5 19.6 %copy-start.12 = (f32[256,16]{1,0:T(8,128)S(1)}, f32[256,16]{1,0:T(8,128)}, u32[]{:S(2)}) copy-start(f32[256,16]{1,0:T(8,128)} %constant.22.clone.t12) | copy-start | bytes 49156
  21.6 12.4 %collective-permute-start.4 = (f32[64,1024]{1,0:T(8,128)S(1)}, f32[64,1024]{1,0:T(8,128)S(1)}, u32[]{:S(2)}, u32[]{:S(2)}) collective-permute-start(f32[64,1024]{1,0:T(8,128)S(1)} %get-tuple-element.39.after), channel_id=1, source_target_pairs={{0,16},{16,32},{32,48},{48,64},{64,80},{80,96},{96,112},{112,128},... | collective-permute-start | bytes 786440 | tf_op jit(solution)/shard_map/ppermute | solution.py:596
  22.9 11.1 %collective-permute-start.5 = (f32[64,1024]{1,0:T(8,128)S(1)}, f32[64,1024]{1,0:T(8,128)S(1)}, u32[]{:S(2)}, u32[]{:S(2)}) collective-permute-start(f32[64,1024]{1,0:T(8,128)S(1)} %get-tuple-element.42), channel_id=1, source_target_pairs={{0,240},{16,0},{32,16},{48,32},{64,48},{80,64},{96,80},{112,96},{1... | collective-permute-start | bytes 786440 | tf_op jit(solution)/shard_map/ppermute | solution.py:597
  29.7 0.7 copy-start.19
  30.4 10.7 %all-to-all-start = ((f32[16,24,128]{2,1,0:T(8,128)}), f32[16,24,128]{2,1,0:T(8,128)S(1)}, u32[]{:S(2)}, u32[]{:S(2)}) async-start(f32[16,24,128]{2,1,0:T(8,128)} %bitcast.6), calls=%async_computation | async-start | bytes 393216 | tf_op jit(solution)/shard_map/all_to_all | solution.py:606
  33.9 1.0 %copy-start.20 = (f32[768,128]{1,0:T(8,128)S(1)}, f32[768,128]{1,0:T(8,128)}, u32[]{:S(2)}) copy-start(f32[768,128]{1,0:T(8,128)} %copy-done.19) | copy-start | bytes 1179652
  36.6 0.9 %copy-start.17 = (f32[11,9,1024]{2,1,0:T(8,128)}, f32[11,9,1024]{2,1,0:T(8,128)S(1)}, u32[]{:S(2)}) copy-start(f32[11,9,1024]{2,1,0:T(8,128)S(1)} %get-tuple-element.44.after.state) | copy-start | bytes 1216516
  37.5 0.7 copy-start.22
  38.2 0.7 copy-start.24
  38.9 18.5 %copy-start.26 = (s32[9,1024]{1,0:T(8,128)}, s32[9,1024]{1,0:T(8,128)S(1)}, u32[]{:S(2)}) copy-start(s32[9,1024]{1,0:T(8,128)S(1)} %get-tuple-element.50.cell) | copy-start | bytes 110596
  41.1 0.8 copy-start.13
  41.9 1.1 %copy-start.18 = (f32[11,9,1024]{2,1,0:T(8,128)S(1)}, f32[11,9,1024]{2,1,0:T(8,128)}, u32[]{:S(2)}) copy-start(f32[11,9,1024]{2,1,0:T(8,128)} %copy-done.17) | copy-start | bytes 1216516
  43.0 23.5 %copy-start.9 = (f32[384,256]{1,0:T(8,128)S(1)}, f32[384,256]{1,0:T(8,128)}, u32[]{:S(2)}) copy-start(f32[384,256]{1,0:T(8,128)} %constant.21.clone.wback) | copy-start | bytes 1179652
  43.0 23.5 %copy-start.15 = (f32[16,256]{1,0:T(8,128)S(1)}, f32[16,256]{1,0:T(8,128)}, u32[]{:S(2)}) copy-start(f32[16,256]{1,0:T(8,128)} %constant.23.clone.t12t) | copy-start | bytes 49156
  45.2 21.4 %all-to-all-start.1 = ((f32[16,8,256]{2,1,0:T(8,128)}), f32[16,8,256]{2,1,0:T(8,128)S(1)}, u32[]{:S(2)}, u32[]{:S(2)}) async-start(f32[16,8,256]{2,1,0:T(8,128)} %bitcast.8), calls=%async_computation.1 | async-start | bytes 262144 | tf_op jit(solution)/shard_map/all_to_all | solution.py:627
  57.4 1.0 %copy-start.25 = (bf16[256,512]{1,0:T(8,128)(2,1)S(1)}, bf16[256,512]{1,0:T(8,128)(2,1)}, u32[]{:S(2)}) copy-start(bf16[256,512]{1,0:T(8,128)(2,1)} %copy-done.24) | copy-start | bytes 786436
  58.4 0.8 copy-start.27
  59.2 12.7 %copy-start.23 = (f32[512,128]{1,0:T(8,128)S(1)}, f32[512,128]{1,0:T(8,128)}, u32[]{:S(2)}) copy-start(f32[512,128]{1,0:T(8,128)} %copy-done.22) | copy-start | bytes 786436
  59.2 12.7 %copy-start.28 = (s32[9,1024]{1,0:T(8,128)S(1)}, s32[9,1024]{1,0:T(8,128)}, u32[]{:S(2)}) copy-start(s32[9,1024]{1,0:T(8,128)} %copy-done.26) | copy-start | bytes 110596
  63.8 16.1 %copy-start.14 = (f32[64,32]{1,0:T(8,128)S(1)}, f32[64,32]{1,0:T(8,128)}, u32[]{:S(2)}) copy-start(f32[64,32]{1,0:T(8,128)} %constant.19.clone.zback) | copy-start | bytes 24580
  63.8 16.1 %copy-start.21 = (f32[768,128]{1,0:T(8,128)S(1)}, f32[768,128]{1,0:T(8,128)}, u32[]{:S(2)}) copy-start(f32[768,128]{1,0:T(8,128)} %copy-done.19) | copy-start | bytes 1179652
  68.3 11.6 %all-to-all-start.2 = ((f32[16,24,128]{2,1,0:T(8,128)}), f32[16,24,128]{2,1,0:T(8,128)S(1)}, u32[]{:S(2)}, u32[]{:S(2)}) async-start(f32[16,24,128]{2,1,0:T(8,128)} %bitcast.10), calls=%async_computation.2 | async-start | bytes 393216 | tf_op jit(solution)/shard_map/all_to_all | solution.py:642

commit v3 on v2

--- a/solution.py
+++ b/solution.py
@@ -82,7 +82,6 @@
     rowtab = np.zeros((GX, 8, 2 * TX))
     rowtab[:, 0] = NY * lnr
     rowtab[:, 1] = 1.0 / (1.0 - np.exp(lnr * TY))
-    absd = np.abs(lane[:, None] - lane[None, :])
     own = np.concatenate([rpow, rrev, misc, rowtab[:, :, :NY], rowtab[:, :, NY:]], axis=1)
 
     def f(a):
@@ -97,7 +96,6 @@
         t12t=f(t12.T),
         cs=f(cs),
         own=f(own),
-        absd=f(absd),
     )
 
 
@@ -155,30 +153,15 @@
     return out
 
 
-def yhalo_of(msg):
-    return jnp.concatenate([msg[40:48, g * NY : (g + 1) * NY] for g in range(4)], axis=0)
-
-
-def pack_blocks(out, blocks):
-    for n, (drops, cells, count) in enumerate(blocks):
-        out[n * SLOT : n * SLOT + 10, :] = drops
-        out[n * SLOT + 10 : n * SLOT + 11, :] = cells
-        out[n * SLOT + 11 : n * SLOT + 12, :] = count
-    out[36:40, :] = jnp.zeros((4, CAP), F32)
-
-
-def pack_kernel(
-    u, v, w, h, q, drops_in, cells, counts, own, xlo, xhi, up, down, mid, fields, tabs, drops, sems
-):
+def sides_kernel(u, v, w, h, q, xlo, xhi, ylo, yhi, done, fields, sems):
+    done[...] = jnp.zeros_like(done)
     copies = [
         pltpu.make_async_copy(ref, fields.at[pl.ds(f * ROWS, ROWS)], sems.at[f])
         for f, ref in enumerate((u, v, w, h, q))
     ]
-    copies.append(pltpu.make_async_copy(drops_in, drops, sems.at[5]))
-    copies.append(pltpu.make_async_copy(own.at[lax.axis_index("gx")], tabs, sems.at[6]))
     for copy in copies:
         copy.start()
-    for copy in copies[:5]:
+    for copy in copies:
         copy.wait()
     for f in range(3):
         for i in range(3):
@@ -195,21 +178,48 @@
             mask = (lane >= at) & (lane < at + 3)
             tlo = jnp.where(mask, pltpu.roll(row, (at - 125) % NY, 1), tlo)
             thi = jnp.where(mask, pltpu.roll(row, at, 1), thi)
-    for out, tile in ((up, tlo), (down, thi)):
-        for g in range(4):
-            out[40:48, g * NY : (g + 1) * NY] = tile[g * 8 : (g + 1) * 8]
-        out[40:48, 4 * NY :] = jnp.zeros((8, 4 * NY), F32)
+    ylo[0:NZ, :] = tlo
+    yhi[0:NZ, :] = thi
+    ylo[NZ:, :] = jnp.zeros((8 * NZ, NY), F32)
+    yhi[NZ:, :] = jnp.zeros((8 * NZ, NY), F32)
+
+
+def pack_kernel(
+    u, v, w, h, q, drops_in, cells, counts, own, after,
+    up, down, mid, part, fields, tabs, drops, sems,
+):
+    copies = [
+        pltpu.make_async_copy(ref, fields.at[pl.ds(f * ROWS, ROWS)], sems.at[f])
+        for f, ref in enumerate((u, v, w, h, q))
+    ]
+    copies.append(pltpu.make_async_copy(drops_in, drops, sems.at[5]))
+    copies.append(pltpu.make_async_copy(own.at[lax.axis_index("gx")], tabs, sems.at[6]))
+    for copy in copies:
+        copy.start()
     copies[5].wait()
-    for s, out in ((2, up), (0, down), (1, mid)):
-        for r in range(3):
-            for a in range(10):
-                out[r * SLOT + a : r * SLOT + a + 1, :] = drops[r, a, s : s + 1, :]
-            out[r * SLOT + 10 : r * SLOT + 11, :] = cells[r, s : s + 1, :].astype(F32)
-            out[r * SLOT + 11 : r * SLOT + 12, :] = jnp.full(
-                (1, CAP), counts[r, s], jnp.int32
-            ).astype(F32)
-        out[36:40, :] = jnp.zeros((4, CAP), F32)
-    copies[6].wait()
+    for out, at, r, s in (
+        [(up, r * SLOT, r, 2) for r in range(3)]
+        + [(down, r * SLOT, r, 0) for r in range(3)]
+        + [(mid, 0, 1, 1), (part, 0, 2, 1), (part, 40, 0, 1)]
+    ):
+        for a in range(10):
+            out[at + a : at + a + 1, :] = drops[r, a, s : s + 1, :]
+        out[at + 10 : at + 11, :] = cells[r, s : s + 1, :].astype(F32)
+        out[at + 11 : at + 12, :] = jnp.full((1, CAP), counts[r, s], jnp.int32).astype(F32)
+    for out, at, rows in ((up, 36, 4), (down, 36, 4), (mid, 12, 4), (part, 12, 4), (part, 52, 4)):
+        out[at : at + rows, :] = jnp.zeros((rows, CAP), F32)
+    copies[3].wait()
+    copies[4].wait()
+    for k, x0 in enumerate((5, 0)):
+        for f in range(2):
+            for i in range(3):
+                row = field_row(fields, 3 + f, x0 + i)
+                for g in range(4):
+                    n = (f * 3 + i) * 4 + g
+                    a, c = 40 * k + 16 + 8 * (n // 8), NY * (n % 8)
+                    part[a : a + 8, c : c + NY] = row[g * 8 : (g + 1) * 8]
+    for k in (0, 1, 2, 6):
+        copies[k].wait()
 
 
 def block_of(msg, n):
@@ -220,23 +230,20 @@
     )
 
 
-def relay_kernel(fields, mid, mlo, mhi, up, down):
-    for out, r, x0 in ((up, 2, 5), (down, 0, 0)):
-        pack_blocks(out, [block_of(mlo, r), block_of(mid, r), block_of(mhi, r)])
-        for f in range(2):
-            for i in range(3):
-                row = field_row(fields, 3 + f, x0 + i)
-                for g in range(4):
-                    n = (f * 3 + i) * 4 + g
-                    a, c = 40 + 8 * (n // 8), NY * (n % 8)
-                    out[a : a + 8, c : c + NY] = row[g * 8 : (g + 1) * 8]
-
-
-def wind_kernel(fields, xlo, xhi, mlo, mhi, ztab, after, stars, send, zs):
+def relay_kernel(part, mlo, mhi, after, up, down, done):
+    done[...] = jnp.zeros_like(done)
+    for n, (out, r) in enumerate(((up, 2), (down, 0))):
+        out[0:12, :] = mlo[r * SLOT : (r + 1) * SLOT, :]
+        out[12:24, :] = mhi[r * SLOT : (r + 1) * SLOT, :]
+        out[24:64, :] = part[n * 40 : (n + 1) * 40, :]
+
+
+def wind_kernel(fields, xlo, xhi, ylo_in, yhi_in, ztab, east_s, north_s, rise_s, send, done, zs):
+    done[...] = jnp.zeros_like(done)
     lane = iota((NZ, NY), 1)
     level = iota((NZ, NY), 0)
-    ylo = yhalo_of(mlo)
-    yhi = yhalo_of(mhi)
+    ylo = ylo_in[0:NZ, :]
+    yhi = yhi_in[0:NZ, :]
     vel = [velocity_rows(fields, x) for x in range(NX)]
     for f in range(3):
         rows = [xlo[(f * 3 + i) * NZ : (f * 3 + i + 1) * NZ, :] for i in range(3)]
@@ -246,22 +253,21 @@
             star = star_row(x, rows, ylo, yhi, f, vel[x], zs.at[f * NX + x], lane)
             if f == 2:
                 star = jnp.where(level == NZ - 1, 0.0, star)
-            at = (f * NX + x) * NZ
-            stars[at : at + NZ, :] = star
+            (east_s, north_s, rise_s)[f][pl.ds(x, NZ, stride=NX), :] = star
     tiles = []
     ext = jnp.zeros((NZ, NY), F32)
     for x in range(NX):
-        east = stars[x * NZ : (x + 1) * NZ, :]
-        north = stars[(NX + x) * NZ : (NX + x + 1) * NZ, :]
-        rise = stars[(2 * NX + x) * NZ : (2 * NX + x + 1) * NZ, :]
+        east = field_row(east_s, 0, x)
+        north = field_row(north_s, 0, x)
+        rise = field_row(rise_s, 0, x)
         d = east + north + rise
         if x > 0:
-            d = d - stars[(x - 1) * NZ : x * NZ, :]
+            d = d - field_row(east_s, 0, x - 1)
         d = d - jnp.where(lane == 0, 0.0, pltpu.roll(north, 1, 1))
         d = d - jnp.where(level == 0, 0.0, pltpu.roll(rise, 1, 0))
         tiles.append(d)
         ext = jnp.where(lane == x, -pltpu.roll(north, (x + 1) % NY, 1), ext)
-    tiles.append(-stars[(NX - 1) * NZ : NX * NZ, :])
+    tiles.append(-field_row(east_s, 0, NX - 1))
     tiles.append(ext)
     hat = dot(ztab[...], jnp.concatenate(tiles, axis=1))
     zeros = jnp.zeros((GX, NY), F32)
@@ -279,7 +285,8 @@
     return tabs.at[0:n], tabs.at[n : 2 * n], tabs.at[2 * n : 3 * n], tabs.at[3 * n : 3 * n + 16]
 
 
-def scan_kernel(recv, wmain, t12, cs, tabs, absd, after, msg, keep, cols, kink):
+def scan_kernel(recv, wmain, t12, cs, tabs, after, msg, keep, kink, done):
+    done[...] = jnp.zeros_like(done)
     rpow, rrev, misc, rowtab = own_tables(tabs)
     lane = iota((2 * TX, NY), 1)
     d = dot(wmain[...], recv[...])
@@ -301,44 +308,53 @@
     out_right = r1 * fwd[:, NY - 1 : NY] + e
     out_left = bwd[:, 0:1] + r128 * e
     keep[...] = fwd + bwd - d + rrev[...] * e
-    table = jnp.where(lane == 0, out_right, jnp.where(lane == 1, out_left, 0.0))
+    lane1 = lane[:TX]
+    table = jnp.zeros((TX, NY), F32)
+    for b in range(2):
+        table = jnp.where(lane1 == b, out_right[b * TX : (b + 1) * TX], table)
+        table = jnp.where(lane1 == 2 + b, out_left[b * TX : (b + 1) * TX], table)
     d8 = d[0:8]
     e8 = e[0:8]
     lane8 = iota((8, NY), 1)
     lanef = lane8.astype(F32)
     s0 = jnp.sum(d8, axis=1, keepdims=True) + e8
     s1 = jnp.sum(d8 * lanef, axis=1, keepdims=True) + float(NY) * e8
-    top = jnp.where(lane8 == 2, s0, jnp.where(lane8 == 3, s1, table[0:8]))
+    top = jnp.where(lane8 == 4, s0, jnp.where(lane8 == 5, s1, table[0:8]))
     table = jnp.concatenate([top, table[8:]], axis=0)
-    cols[...] = table
     turned = table.T[0:8]
     for y in range(GY):
         msg[y * 8 : (y + 1) * 8, :] = turned
-    kink[...] = dot(d8, absd[...]) + e8 * (float(NY) - lanef)
-
-
-def solve_kernel(got, keep, cols, kink, wback, t12t, cs, tabs, after, send):
+    apart = jnp.abs(iota((NY, NY), 0) - iota((NY, NY), 1)).astype(F32)
+    kink[...] = dot(d8, apart) + e8 * (float(NY) - lanef)
+
+
+def solve_kernel(got, keep, kink, wback, t12t, cs, tabs, after, send, done):
+    done[...] = jnp.zeros_like(done)
     rpow, rrev, misc, rowtab = own_tables(tabs)
     here = lax.axis_index("gy")
     first = (lax.axis_index("gx") == 0).astype(F32)
     who = iota((GY, 2 * TX), 0)
-    all_right = jnp.concatenate([got[y * 8 : y * 8 + 1, :] for y in range(GY)], axis=0)
-    all_left = jnp.concatenate([got[y * 8 + 1 : y * 8 + 2, :] for y in range(GY)], axis=0)
-    s0 = jnp.concatenate([got[y * 8 + 2 : y * 8 + 3, 0:1] for y in range(GY)], axis=0)
-    s1 = jnp.concatenate([got[y * 8 + 3 : y * 8 + 4, 0:1] for y in range(GY)], axis=0)
+    def rows(k):
+        return jnp.concatenate([got[y * 8 + k : y * 8 + k + 1, :] for y in range(GY)], axis=0)
+
+    all_right = jnp.concatenate([rows(0), rows(1)], axis=1)
+    all_left = jnp.concatenate([rows(2), rows(3)], axis=1)
+    s0 = rows(4)[:, 0:1]
+    s1 = rows(5)[:, 0:1]
     lnr = jnp.concatenate([rowtab[0:1, :], rowtab[8:9, :]], axis=1)
     inv = jnp.concatenate([rowtab[1:2, :], rowtab[9:10, :]], axis=1)
     after = ((here - who - 1) & (GY - 1)).astype(F32)
     before = ((who - here - 1) & (GY - 1)).astype(F32)
     in_left = jnp.sum(jnp.exp(after * lnr) * all_right, axis=0, keepdims=True) * inv
     in_right = jnp.sum(jnp.exp(before * lnr) * all_left, axis=0, keepdims=True) * inv
+    own_right = jnp.sum(jnp.where(who == here, all_right, 0.0), axis=0, keepdims=True)
     row = iota((8, 2 * TX), 0)
-    turned = jnp.where(row == 0, in_left, jnp.where(row == 1, in_right, 0.0)).T
+    turned = jnp.where(row == 0, in_left, jnp.where(row == 1, in_right, own_right)).T
     in_left = turned[:, 0:1]
     in_right = turned[:, 1:2]
     coef = misc[:, 8:9]
     pres = coef * (keep[...] + rpow[...] * in_left + rrev[...] * in_right)
-    edge = coef * (cols[:, 0:1] + misc[:, 7:8] * in_left + in_right)
+    edge = coef * (turned[:, 2:3] + misc[:, 7:8] * in_left + in_right)
     who1 = iota((GY, 1), 0)
     far = (NY * ((here - who1) & (GY - 1))).astype(F32)
     mine = who1 == here
@@ -365,31 +381,42 @@
 def store_table(lhs, n, table):
     turned = table.T
     hi = turned.astype(BF16)
-    lhs[n * NY : (n + 1) * NY, 0:ROWS] = hi
-    lhs[n * NY : (n + 1) * NY, ROWS:] = (turned - hi.astype(F32)).astype(BF16)
+    lhs[2 * n * NY : (2 * n + 1) * NY, :] = hi
+    lhs[(2 * n + 1) * NY : (2 * n + 2) * NY, :] = (turned - hi.astype(F32)).astype(BF16)
 
 
 def masks_of(cells):
     width = cells.shape[1]
     rowid = ((cells >> 7) & (NX - 1)) * NZ + (cells >> 10)
-    hot = jnp.where(iota((ROWS, width), 0) == rowid, 1.0, 0.0).astype(BF16)
+    each = iota((ROWS, width), 0).astype(F32).astype(BF16)
+    hot = jnp.where(
+        each == rowid.astype(F32).astype(BF16), jnp.array(1.0, BF16), jnp.array(0.0, BF16)
+    )
     pick = iota((NY, width), 0) == (cells & (NY - 1))
     return hot, pick
 
 
-def gather_one(lhs, n, hot, pick):
-    both = jnp.concatenate([hot, hot], axis=0)
-    got = jnp.dot(lhs[n * NY : (n + 1) * NY, :], both, preferred_element_type=F32)
-    return jnp.sum(jnp.where(pick, got, 0.0), axis=0, keepdims=True)
+def gather_all(lhs, count, cell, air):
+    for n in range(9):
+        for at in range(0, CAP, CHUNK):
+            hot, pick = masks_of(cell[n : n + 1, at : at + CHUNK])
+            got = jnp.dot(lhs[...], hot, preferred_element_type=F32)
+            for f in range(count):
+                a = 2 * f * NY
+                both = got[a : a + NY] + got[a + NY : a + 2 * NY]
+                air[f, n : n + 1, at : at + CHUNK] = jnp.sum(
+                    jnp.where(pick, both, 0.0), axis=0, keepdims=True
+                )
 
 
 CHUNK = 512
 
 
-def heat_kernel(fields, mid, mlo, mhi, clo, chi, after, stars, lhs, cell_out, state, zs):
+def heat_kernel(fields, ylo_in, yhi_in, mid, mlo, mhi, clo, chi, after, stars, lhs, cell_out, state, done, zs):
+    done[...] = jnp.zeros_like(done)
     lane = iota((NZ, NY), 1)
-    ylo = yhalo_of(mlo)
-    yhi = yhalo_of(mhi)
+    ylo = ylo_in[0:NZ, :]
+    yhi = yhi_in[0:NZ, :]
     vel = [velocity_rows(fields, x) for x in range(NX)]
 
     def side(msg, n):
@@ -412,12 +439,10 @@
     for r in range(3):
         for s in range(3):
             n = r * 3 + s
-            if r == 0:
-                block = block_of(clo, s)
-            elif r == 2:
-                block = block_of(chi, s)
+            if r == 1:
+                block = block_of((mlo, mid, mhi)[s], (1, 0, 1)[s])
             else:
-                block = block_of((mlo, mid, mhi)[s], 1)
+                block = block_of((clo, None, chi)[r], (0, 2, 1)[s])
             values, cell, count = block
             for a in range(10):
                 state[a, n : n + 1, :] = values[a : a + 1]
@@ -426,16 +451,9 @@
             state[10, n : n + 1, :] = jnp.where(slot < count, 1.0, 0.0)
 
 
-def growth_kernel(lhs, cell, state, after, state_out, gain_out, air):
-    def gather_block(n, carry):
-        for c in range(CAP // CHUNK):
-            at = c * CHUNK
-            hot, pick = masks_of(cell[pl.ds(n, 1), at : at + CHUNK])
-            for f in range(2):
-                air[f, pl.ds(n, 1), at : at + CHUNK] = gather_one(lhs, f, hot, pick)
-        return carry
-
-    lax.fori_loop(0, 9, gather_block, 0)
+def growth_kernel(lhs, cell, state, after, state_out, gain_out, done, air):
+    done[...] = jnp.zeros_like(done)
+    gather_all(lhs, 2, cell, air)
     live = state[10]
     radius = state[6]
     cubed = radius * radius * radius
@@ -459,26 +477,21 @@
 def scatter_kernel(stars, cell, gain, after, heat_next, moist_next, acc):
     acc[...] = jnp.zeros_like(acc)
 
-    def scatter_block(n, carry):
-        for c in range(CAP // CHUNK):
-            at = c * CHUNK
-            hot, pick = masks_of(cell[pl.ds(n, 1), at : at + CHUNK])
-            g = gain[pl.ds(n, 1), at : at + CHUNK]
+    for n in range(9):
+        for at in range(0, CAP, CHUNK):
+            hot, pick = masks_of(cell[n : n + 1, at : at + CHUNK])
+            g = gain[n : n + 1, at : at + CHUNK]
             hi = g.astype(BF16).astype(F32)
-            lo = g - hi
             z = jnp.concatenate(
                 [
                     jnp.where(pick, hi, 0.0).astype(BF16),
-                    jnp.where(pick, lo, 0.0).astype(BF16),
+                    jnp.where(pick, g - hi, 0.0).astype(BF16),
                 ],
                 axis=0,
             )
             acc[...] += lax.dot_general(
                 hot, z, (((1,), (1,)), ((), ())), preferred_element_type=F32
             )
-        return carry
-
-    lax.fori_loop(0, 9, scatter_block, 0)
     for x in range(NX):
         a = x * NZ
         condensed = acc[a : a + NZ, 0:NY] + acc[a : a + NZ, NY:]
@@ -489,7 +502,7 @@
 
 
 def final_kernel(
-    recv, stars, zback, cell, state, east_next, north_next, up_next, drops_out, lhs, next_rows, air
+    recv, east_s, north_s, rise_s, zback, cell, state, east_next, north_next, up_next, drops_out, lhs, next_rows, air
 ):
     lane = iota((NZ, NY), 1)
     tiles = []
@@ -503,15 +516,12 @@
     pres = [both[:NZ, t * NY : (t + 1) * NY] for t in range(NX + 2)]
     edge = pres[NX + 1]
     for x in range(NX):
-        east = stars[x * NZ : (x + 1) * NZ, :] - (pres[x + 1] - pres[x]) * ASPECT
+        east = field_row(east_s, 0, x) - (pres[x + 1] - pres[x]) * ASPECT
         ahead = pltpu.roll(
             jnp.where(lane == 0, pltpu.roll(edge, (NY - x) % NY, 1), pres[x]), NY - 1, 1
         )
-        north = stars[(NX + x) * NZ : (NX + x + 1) * NZ, :] - (ahead - pres[x])
-        rise = (
-            stars[(2 * NX + x) * NZ : (2 * NX + x + 1) * NZ, :]
-            - both[NZ:, x * NY : (x + 1) * NY]
-        )
+        north = field_row(north_s, 0, x) - (ahead - pres[x])
+        rise = field_row(rise_s, 0, x) - both[NZ:, x * NY : (x + 1) * NY]
         for f, (val, ref) in enumerate(
             ((east, east_next), (north, north_next), (rise, up_next))
         ):
@@ -520,15 +530,7 @@
     for f in range(3):
         store_table(lhs, f, next_rows[f])
 
-    def gather_block(n, carry):
-        for c in range(CAP // CHUNK):
-            at = c * CHUNK
-            hot, pick = masks_of(cell[pl.ds(n, 1), at : at + CHUNK])
-            for f in range(3):
-                air[f, pl.ds(n, 1), at : at + CHUNK] = gather_one(lhs, f, hot, pick)
-        return carry
-
-    lax.fori_loop(0, 9, gather_block, 0)
+    gather_all(lhs, 3, cell, air)
     mix = state[10]
     for a in range(3):
         speed = air[a] * mix + state[3 + a]
@@ -551,13 +553,17 @@
     return jax.ShapeDtypeStruct(shape, dtype)
 
 
-def call(kernel, name, us, out_shape, in_specs, scratch=(), mib=12):
+TOKEN = sds(8, NY)
+
+
+def call(kernel, name, us, out_shape, in_specs, scratch=(), mib=6, aliases=None):
     return pl.pallas_call(
         kernel,
         out_shape=out_shape,
         in_specs=in_specs,
         out_specs=tuple(VM for _ in out_shape),
         scratch_shapes=list(scratch),
+        input_output_aliases=aliases or {},
         compiler_params=pltpu.CompilerParams(vmem_limit_bytes=mib * 1024 * 1024),
         cost_estimate=pl.CostEstimate(
             flops=int(us * 5e8), bytes_accessed=int(us * 2e6), transcendentals=0
@@ -575,69 +581,84 @@
     tab = make_tables()
     u, v, w, h, q = (a.reshape(ROWS, NY) for a in (u, v, w, h, q))
     drops = droplets.transpose(0, 2, 1, 3)
-    xlo, xhi, up, down, mid, fields, tabs = call(
+    xlo, xhi, ylo, yhi, done = call(
+        sides_kernel,
+        "sides",
+        2.0,
+        (sds(9 * NZ, NY), sds(9 * NZ, NY), sds(9 * NZ, NY), sds(9 * NZ, NY), TOKEN),
+        [HBM] * 5,
+        [pltpu.VMEM((5 * ROWS, NY), F32), pltpu.SemaphoreType.DMA((5,))],
+        60,
+    )(u, v, w, h, q)
+    xlo = lax.ppermute(xlo, "gx", ring("gx", 1))
+    xhi = lax.ppermute(xhi, "gx", ring("gx", -1))
+    ylo = lax.ppermute(ylo, "gy", ring("gy", 1))
+    yhi = lax.ppermute(yhi, "gy", ring("gy", -1))
+    up, down, mid, part, fields, tabs = call(
         pack_kernel,
         "pack",
         2.5,
         (
-            sds(9 * NZ, NY), sds(9 * NZ, NY), sds(48, CAP), sds(48, CAP), sds(40, CAP),
-            sds(5 * ROWS, NY), sds(6 * TX + 16, NY),
+            sds(40, CAP), sds(40, CAP), sds(16, CAP), sds(80, CAP), sds(5 * ROWS, NY),
+            sds(6 * TX + 16, NY),
         ),
-        [HBM] * 6 + [VM, SM, HBM],
-        [pltpu.VMEM((3, 10, 3, CAP), F32), pltpu.SemaphoreType.DMA((7,))],
-    )(u, v, w, h, q, drops, cells, counts, tab["own"])
+        [HBM] * 6 + [VM, SM, HBM, ANY],
+        [
+            pltpu.VMEM((3, 10, 3, CAP), F32),
+            pltpu.SemaphoreType.DMA((7,)),
+        ],
+        60,
+    )(u, v, w, h, q, drops, cells, counts, tab["own"], done)
     mlo = lax.ppermute(up, "gy", ring("gy", 1))
     mhi = lax.ppermute(down, "gy", ring("gy", -1))
-    xlo = lax.ppermute(xlo, "gx", ring("gx", 1))
-    xhi = lax.ppermute(xhi, "gx", ring("gx", -1))
-    cup, cdown = call(
-        relay_kernel, "relay", 1.0, (sds(64, CAP), sds(64, CAP)), [VM] * 4
-    )(fields, mid, mlo, mhi)
-    clo = lax.ppermute(cup, "gx", ring("gx", 1))
-    chi = lax.ppermute(cdown, "gx", ring("gx", -1))
-    stars, send = call(
+    east_s, north_s, rise_s, send, done = call(
         wind_kernel,
         "winds",
         3.0,
-        (sds(3 * ROWS, NY), sds(GX * BLK, NY)),
-        [VM] * 6 + [ANY],
+        (sds(ROWS, NY), sds(ROWS, NY), sds(ROWS, NY), sds(GX * BLK, NY), TOKEN),
+        [VM] * 6,
         [pltpu.VMEM((3 * NX, NZ + 16, NY), F32)],
-    )(fields, xlo, xhi, mlo, mhi, tab["ztab"], cup)
+    )(fields, xlo, xhi, ylo, yhi, tab["ztab"])
     recv = lax.all_to_all(send.reshape(GX, BLK, NY), "gx", 0, 0, tiled=True)
-    stars_hq, lhs, cell_in, state = call(
+    cup, cdown, done = call(
+        relay_kernel, "relay", 1.0, (sds(64, CAP), sds(64, CAP), TOKEN), [VM] * 3 + [ANY]
+    )(part, mlo, mhi, done)
+    clo = lax.ppermute(cup, "gx", ring("gx", 1))
+    chi = lax.ppermute(cdown, "gx", ring("gx", -1))
+    msg, keep, kink, done = call(
+        scan_kernel,
+        "scan",
+        2.0,
+        (sds(8 * GY, NY), sds(2 * TX, NY), sds(8, NY), TOKEN),
+        [VM] * 5 + [ANY],
+    )(
+        recv.reshape(GX * BLK, NY), tab["wmain"], tab["t12"], tab["cs"], tabs, done
+    )
+    got = lax.all_to_all(msg.reshape(GY, 8, NY), "gy", 0, 0, tiled=True)
+    stars_hq, lhs, cell_in, state, done = call(
         heat_kernel,
         "heat",
         3.0,
         (
-            sds(2 * ROWS, NY), sds(2 * NY, 2 * ROWS, dtype=BF16),
-            sds(9, CAP, dtype=jnp.int32), sds(11, 9, CAP),
+            sds(2 * ROWS, NY), sds(4 * NY, ROWS, dtype=BF16),
+            sds(9, CAP, dtype=jnp.int32), sds(11, 9, CAP), TOKEN,
         ),
-        [VM] * 6 + [ANY],
+        [VM] * 8 + [ANY],
         [pltpu.VMEM((2 * NX, NZ + 16, NY), F32)],
-    )(fields, mid, mlo, mhi, clo, chi, stars)
-    msg, keep, cols, kink = call(
-        scan_kernel,
-        "scan",
-        2.0,
-        (sds(8 * GY, 2 * TX), sds(2 * TX, NY), sds(2 * TX, NY), sds(8, NY)),
-        [VM] * 6 + [ANY],
-    )(
-        recv.reshape(GX * BLK, NY), tab["wmain"], tab["t12"], tab["cs"], tabs, tab["absd"], state
-    )
-    got = lax.all_to_all(msg.reshape(GY, 8, 2 * TX), "gy", 0, 0, tiled=True)
-    state, gain = call(
+    )(fields, ylo, yhi, mid, mlo, mhi, clo, chi, done)
+    state, gain, done = call(
         growth_kernel,
         "growth",
         5.0,
-        (sds(11, 9, CAP), sds(9, CAP)),
+        (sds(11, 9, CAP), sds(9, CAP), TOKEN),
         [VM] * 3 + [ANY],
         [pltpu.VMEM((2, 9, CAP), F32)],
-    )(lhs, cell_in, state, keep)
-    (send,) = call(
-        solve_kernel, "solve", 2.0, (sds(GX * BLK, NY),), [VM] * 8 + [ANY]
+    )(lhs, cell_in, state, done)
+    send, done = call(
+        solve_kernel, "solve", 2.0, (sds(GX * BLK, NY), TOKEN), [VM] * 7 + [ANY]
     )(
-        got.reshape(8 * GY, 2 * TX), keep, cols, kink, tab["wback"], tab["t12t"], tab["cs"], tabs,
-        gain,
+        got.reshape(8 * GY, NY), keep, kink, tab["wback"], tab["t12t"], tab["cs"], tabs,
+        done,
     )
     recv = lax.all_to_all(send.reshape(GX, BLK, NY), "gx", 0, 0, tiled=True)
     heat_next, moist_next = call(
@@ -647,19 +668,20 @@
         (sds(ROWS, NY), sds(ROWS, NY)),
         [VM] * 3 + [ANY],
         [pltpu.VMEM((ROWS, 2 * NY), F32)],
-    )(stars_hq, cell_in, gain, send)
+    )(stars_hq, cell_in, gain, done)
     east_next, north_next, up_next, drops_out = call(
         final_kernel,
         "final",
         8.0,
         (sds(ROWS, NY), sds(ROWS, NY), sds(ROWS, NY), sds(3, 10, 3, CAP)),
-        [VM] * 5,
+        [VM] * 7,
         [
-            pltpu.VMEM((3 * NY, 2 * ROWS), BF16),
+            pltpu.VMEM((6 * NY, ROWS), BF16),
             pltpu.VMEM((3, ROWS, NY), F32),
             pltpu.VMEM((3, 9, CAP), F32),
         ],
-    )(recv.reshape(GX * BLK, NY), stars, tab["zback"], cell_in, state)
+        aliases={1: 0, 2: 1, 3: 2},
+    )(recv.reshape(GX * BLK, NY), east_s, north_s, rise_s, tab["zback"], cell_in, state)
     out = (
         a.reshape(NZ, NX, NY) for a in (east_next, north_next, up_next, heat_next, moist_next)
     )

time: 88.5 us -> 76.9 us (0.87)
  local copies, waits for them, and re-layouts: 17.6 us -> 4.52 us
  starting transfers between devices: 32.5 us -> 35.8 us
  Pallas kernels: 27.5 us -> 25.9 us
    unnamed x58 -> x32, local copies, waits for them, and re-layouts: 17.6 us -> 4.52 us
    ppermute x0 -> x2, starting transfers between devices: none -> 2.74 us  [the longest x1 2.53 us: per_device(): ylo = lax.ppermute(ylo, 'gy', ring('gy', 1))]
    pallas_call x1, Pallas kernels: 3.99 us -> 2.17 us  [per_device(): call(scatter_kernel, 'scatter', 4.0, (sds(ROWS, NY), sds(ROWS, NY)), [VM]...]
    pallas_call x7 -> x8, Pallas kernels: 15.7 us -> 17.4 us  [the longest x1 3.6 us: per_device(): call(pack_kernel, 'pack', 2.5, (sds(40, CAP), sds(40, CAP), sds(16, CAP),...]
    ppermute x1, starting transfers between devices: 3.04 us -> 1.54 us  [per_device(): mlo = lax.ppermute(up, 'gy', ring('gy', 1))]
    ppermute x1, starting transfers between devices: 0.24 us -> 1.73 us  [per_device(): mhi = lax.ppermute(down, 'gy', ring('gy', -1))]
    pallas_call x1, Pallas kernels: 7.82 us -> 6.39 us  [per_device(): call(final_kernel, 'final', 8.0, (sds(ROWS, NY), sds(ROWS, NY), sds(ROWS,...]
    ppermute x1, starting transfers between devices: 0.97 us -> 2.12 us  [per_device(): xlo = lax.ppermute(xlo, 'gx', ring('gx', 1))]
  transfers between devices with their start and end apart: 9 -> 11, of which waited for: 4 -> 3; matrix products, arithmetic and copies ran while one was open for 0% -> 0% of each run, Pallas kernels for 15% -> 20%
where the time goes in v3:
time: 76.9 us; the launch traced here: 76.4 us
  starting transfers between devices  35.8 us (47%)
  Pallas kernels  25.9 us (34%)
  waiting for transfers between devices  9.29 us (12%)
  local copies, waits for them, and re-layouts  4.52 us (6%)
  between operations  0.82 us (1%)
    all_to_all x1, starting transfers between devices, per_device(): got = lax.all_to_all(msg.reshape(GY, 8, NY), 'gy', 0, 0, tiled=True)  11.9 us
    all_to_all x2, starting transfers between devices, per_device(): recv = lax.all_to_all(send.reshape(GX, BLK, NY), 'gx', 0, 0, tiled=True)  7.18 us
    all_to_all x2, waiting for transfers between devices, per_device(): recv = lax.all_to_all(send.reshape(GX, BLK, NY), 'gx', 0, 0, tiled=True)  6.97 us
    pallas_call x1, Pallas kernels, per_device(): call(final_kernel, 'final', 8.0, (sds(ROWS, NY), sds(ROWS, NY), sds(ROWS,...  6.39 us
    unnamed x32, local copies, waits for them, and re-layouts  4.52 us
    ppermute x1, starting transfers between devices, per_device(): xhi = lax.ppermute(xhi, 'gx', ring('gx', -1))  3.81 us
    pallas_call x1, Pallas kernels, per_device(): call(pack_kernel, 'pack', 2.5, (sds(40, CAP), sds(40, CAP), sds(16, CAP),...  3.6 us
    ppermute x1, starting transfers between devices, per_device(): chi = lax.ppermute(cdown, 'gx', ring('gx', -1))  3.54 us
  transfers between devices with their start and end apart: 11, of which 3 were waited for; matrix products, arithmetic and copies ran while one was open for 0% of the time, Pallas kernels for 20%

profile of v3, /device:TPU:1, one launch (start us, length us, event | category | flops | bytes accessed | tf_op | source)
XLA Modules:
  0.0 76.4 jit_solution(6875656978664750069)
XLA Ops:
  0.6 0.0 copy-start.11
  0.6 2.4 %sides.1 = (f32[288,128]{1,0:T(8,128)}, f32[288,128]{1,0:T(8,128)}, f32[288,128]{1,0:T(8,128)}, f32[288,128]{1,0:T(8,128)}, f32[8,128]{1,0:T(8,128)}) custom-call(f32[256,128]{1,0:T(8,128)} %bitcast.22, f32[256,128]{1,0:T(8,128)} %bitcast.24, f32[256,128]{1,0:T(8,128)} %bitcast.26, f32[256,128]{1,0:T(8,128)} %bitcast.28, f32[256,128]{1,0:T(8,128)} %bitcast.30), custom_call_target="tpu_custom_call" | custom-call | flops 1000000000 | bytes 4000000 | tf_op jit(solution)/shard_map/sides/pallas_call | solution.py:584
  3.0 2.1 %collective-permute-start = (f32[288,128]{1,0:T(8,128)}, f32[288,128]{1,0:T(8,128)S(1)}, u32[]{:S(2)}, u32[]{:S(2)}) collective-permute-start(f32[288,128]{1,0:T(8,128)} %get-tuple-element.47), channel_id=1, source_target_pairs={{0,16},{16,32},{32,48},{48,64},{64,80},{80,96},{96,112},{112,128},... | collective-permute-start | bytes 442376 | tf_op jit(solution)/shard_map/ppermute | solution.py:593
  5.1 3.8 %collective-permute-start.1 = (f32[288,128]{1,0:T(8,128)}, f32[288,128]{1,0:T(8,128)S(1)}, u32[]{:S(2)}, u32[]{:S(2)}) collective-permute-start(f32[288,128]{1,0:T(8,128)} %get-tuple-element.48), channel_id=1, source_target_pairs={{0,240},{16,0},{32,16},{48,32},{64,48},{80,64},{96,80},{112,96},{1... | collective-permute-start | bytes 442376 | tf_op jit(solution)/shard_map/ppermute | solution.py:594
  8.9 2.5 %collective-permute-start.2 = (f32[288,128]{1,0:T(8,128)}, f32[288,128]{1,0:T(8,128)S(1)}, u32[]{:S(2)}, u32[]{:S(2)}) collective-permute-start(f32[288,128]{1,0:T(8,128)} %get-tuple-element.49), channel_id=1, source_target_pairs={{0,1},{1,2},{2,3},{3,4},{4,5},{5,6},{6,7},{7,8},{8,9},{9,10},{10,1... | collective-permute-start | bytes 442376 | tf_op jit(solution)/shard_map/ppermute | solution.py:595
  11.5 0.2 collective-permute-start.3
  11.7 0.0 copy-start.6
  11.7 0.0 copy-start.7
  11.7 3.6 %pack.1 = (f32[40,1024]{1,0:T(8,128)}, f32[40,1024]{1,0:T(8,128)}, f32[16,1024]{1,0:T(8,128)}, f32[80,1024]{1,0:T(8,128)}, f32[1280,128]{1,0:T(8,128)}, /*index=5*/f32[784,128]{1,0:T(8,128)}) custom-call(f32[256,128]{1,0:T(8,128)} %bitcast.23, f32[256,128]{1,0:T(8,128)} %bitcast.25, f32[256,128]{1,0:T(8,128)} %bitcast.27, f32[256,128]{1,0:T(8,128)} %bitcast.29, ...), custom_call_target="tpu_custom_call" | custom-call | flops 1250000000 | bytes 5000000 | tf_op jit(solution)/shard_map/pack/pallas_call | solution.py:597
  15.3 1.5 %collective-permute-start.4 = (f32[40,1024]{1,0:T(8,128)}, f32[40,1024]{1,0:T(8,128)S(1)}, u32[]{:S(2)}, u32[]{:S(2)}) collective-permute-start(f32[40,1024]{1,0:T(8,128)} %get-tuple-element.54), channel_id=1, source_target_pairs={{0,1},{1,2},{2,3},{3,4},{4,5},{5,6},{6,7},{7,8},{8,9},{9,10},{10,1... | collective-permute-start | bytes 491528 | tf_op jit(solution)/shard_map/ppermute | solution.py:612
  16.8 0.0 collective-permute-done.xlo
  16.8 1.7 %collective-permute-start.5 = (f32[40,1024]{1,0:T(8,128)}, f32[40,1024]{1,0:T(8,128)S(1)}, u32[]{:S(2)}, u32[]{:S(2)}) collective-permute-start(f32[40,1024]{1,0:T(8,128)} %get-tuple-element.55), channel_id=1, source_target_pairs={{0,15},{1,0},{2,1},{3,2},{4,3},{5,4},{6,5},{7,6},{8,7},{9,8},{10,9... | collective-permute-start | bytes 491528 | tf_op jit(solution)/shard_map/ppermute | solution.py:613
  18.6 0.0 collective-permute-done.1.xhi
  18.6 0.0 collective-permute-done.2.ylo_in
  18.6 0.0 collective-permute-done.3.yhi_in
  18.6 0.0 copy-done.11
  18.6 0.0 copy-start
  18.6 1.1 %copy-done = f32[1280,128]{1,0:T(8,128)S(1)} copy-done((f32[1280,128]{1,0:T(8,128)S(1)}, f32[1280,128]{1,0:T(8,128)}, u32[]{:S(2)}) %copy-start) | copy-done | bytes 655384
  19.7 0.0 copy-start.2
  19.7 0.0 copy-start.1
  19.7 0.0 copy-start.4
  19.7 3.0 %winds.1 = (f32[256,128]{1,0:T(8,128)}, f32[256,128]{1,0:T(8,128)}, f32[256,128]{1,0:T(8,128)}, f32[384,128]{1,0:T(8,128)}, f32[8,128]{1,0:T(8,128)S(1)}) custom-call(f32[1280,128]{1,0:T(8,128)S(1)} %copy-done, f32[288,128]{1,0:T(8,128)S(1)} %collective-permute-done.xlo, f32[288,128]{1,0:T(8,128)S(1)} %collective-permute-done.1.xhi, ...), custom_call_target="tpu_custom_call" | custom-call | flops 1500000000 | bytes 6000000 | tf_op jit(solution)/shard_map/winds/pallas_call | solution.py:614
  22.7 3.5 %all-to-all-start = ((f32[16,24,128]{2,1,0:T(8,128)}), f32[16,24,128]{2,1,0:T(8,128)S(1)}, u32[]{:S(2)}, u32[]{:S(2)}) async-start(f32[16,24,128]{2,1,0:T(8,128)} %bitcast.6), calls=%async_computation | async-start | bytes 393216 | tf_op jit(solution)/shard_map/all_to_all | solution.py:622
  26.2 0.0 collective-permute-done.4.mlo
  26.2 0.0 collective-permute-done.5.mhi
  26.2 0.0 copy-start.3
  26.2 1.0 %copy-done.3 = f32[80,1024]{1,0:T(8,128)S(1)} copy-done((f32[80,1024]{1,0:T(8,128)S(1)}, f32[80,1024]{1,0:T(8,128)}, u32[]{:S(2)}) %copy-start.3) | copy-done | bytes 327704
  27.2 1.3 %collective-permute-start.6 = (f32[64,1024]{1,0:T(8,128)S(1)}, f32[64,1024]{1,0:T(8,128)S(1)}, u32[]{:S(2)}, u32[]{:S(2)}) collective-permute-start(f32[64,1024]{1,0:T(8,128)S(1)} %get-tuple-element.62), channel_id=1, source_target_pairs={{0,16},{16,32},{32,48},{48,64},{64,80},{80,96},{96,112},{112,128},... | collective-permute-start | bytes 786440 | tf_op jit(solution)/shard_map/ppermute | solution.py:626
  28.5 3.5 %collective-permute-start.7 = (f32[64,1024]{1,0:T(8,128)S(1)}, f32[64,1024]{1,0:T(8,128)S(1)}, u32[]{:S(2)}, u32[]{:S(2)}) collective-permute-start(f32[64,1024]{1,0:T(8,128)S(1)} %get-tuple-element.63), channel_id=1, source_target_pairs={{0,240},{16,0},{32,16},{48,32},{64,48},{80,64},{96,80},{112,96},{1... | collective-permute-start | bytes 786440 | tf_op jit(solution)/shard_map/ppermute | solution.py:627
  32.1 1.3 %all-to-all-done = f32[16,24,128]{2,1,0:T(8,128)S(1)} async-done(((f32[16,24,128]{2,1,0:T(8,128)}), f32[16,24,128]{2,1,0:T(8,128)S(1)}, u32[]{:S(2)}, u32[]{:S(2)}) %all-to-all-start) | async-done | bytes 196640 | tf_op jit(solution)/shard_map/all_to_all | solution.py:622
  33.3 0.0 copy-done.6
  33.3 0.0 copy-done.7
  33.4 0.0 copy-done.2
  33.4 0.0 copy-start.8
  33.4 0.9 %copy-done.8 = f32[256,16]{1,0:T(8,128)S(1)} copy-done((f32[256,16]{1,0:T(8,128)S(1)}, f32[256,16]{1,0:T(8,128)}, u32[]{:S(2)}) %copy-start.8) | copy-done | bytes 16408
  34.3 2.1 %scan.1 = (f32[128,128]{1,0:T(8,128)}, f32[256,128]{1,0:T(8,128)S(1)}, f32[8,128]{1,0:T(8,128)S(1)}, f32[8,128]{1,0:T(8,128)S(1)}) custom-call(f32[384,128]{1,0:T(8,128)S(1)} %bitcast.18, f32[256,384]{1,0:T(8,128)S(1)} %copy-done.6, f32[256,16]{1,0:T(8,128)S(1)} %copy-done.8, f32[256,128]{1,0:T(8,128)S(1)} %copy-done.7, f32[784,128]{1,0:T(8,128)S(1)} %copy-done.2, ...), custom_call_target="tpu_custom_call" | custom-call | flops 1000000000 | bytes 4000000 | tf_op jit(solution)/shard_map/scan/pallas_call | solution.py:628
  36.4 0.0 copy-start.12
  36.4 0.7 copy-done.12
  37.0 11.9 %all-to-all-start.1 = ((f32[16,8,128]{2,1,0:T(8,128)}), f32[16,8,128]{2,1,0:T(8,128)S(1)}, u32[]{:S(2)}, u32[]{:S(2)}) async-start(f32[16,8,128]{2,1,0:T(8,128)} %bitcast.8), calls=%async_computation.1 | async-start | bytes 131072 | tf_op jit(solution)/shard_map/all_to_all | solution.py:637
  48.9 0.0 collective-permute-done.6.clo
  48.9 0.0 collective-permute-done.7.chi
  48.9 0.0 copy-done.1
  48.9 0.0 copy-done.4
  48.9 0.0 copy-start.5
  48.9 0.0 copy-start.10
  49.0 0.0 copy-start.13
  49.0 1.7 %heat.1 = (f32[512,128]{1,0:T(8,128)S(1)}, bf16[512,256]{1,0:T(8,128)(2,1)S(1)}, s32[9,1024]{1,0:T(8,128)S(1)}, f32[11,9,1024]{2,1,0:T(8,128)S(1)}, f32[8,128]{1,0:T(8,128)S(1)}) custom-call(f32[1280,128]{1,0:T(8,128)S(1)} %copy-done.1, f32[288,128]{1,0:T(8,128)S(1)} %collective-permute-done.2.ylo_in, f32[288,128]{1,0:T(8,128)S(1)} %collective-permute-done.3.yhi_in, ...), custom_call_target="tpu_custom_call" | custom-call | flops 1500000000 | bytes 6000000 | tf_op jit(solution)/shard_map/heat/pallas_call | solution.py:638
  50.7 2.9 %growth.1 = (f32[11,9,1024]{2,1,0:T(8,128)S(1)}, f32[9,1024]{1,0:T(8,128)S(1)}, f32[8,128]{1,0:T(8,128)S(1)}) custom-call(bf16[512,256]{1,0:T(8,128)(2,1)S(1)} %get-tuple-element.65.lhs, s32[9,1024]{1,0:T(8,128)S(1)} %get-tuple-element.66.cell, f32[11,9,1024]{2,1,0:T(8,128)S(1)} %get-tuple-element.67.state, f32[8,128]{1,0:T(8,128)S(1)} %get-tuple-element.68.after), custom_call_target="tpu_custom_call" | custom-call | flops 2500000000 | bytes 10000000 | tf_op jit(solution)/shard_map/growth/pallas_call | solution.py:649
  53.5 0.0 copy-start.14
  53.5 0.9 %copy-done.14 = f32[11,9,1024]{2,1,0:T(8,128)} copy-done((f32[11,9,1024]{2,1,0:T(8,128)}, f32[11,9,1024]{2,1,0:T(8,128)S(1)}, u32[]{:S(2)}) %copy-start.14) | copy-done | bytes 405528
  54.4 0.0 copy-start.9
  54.4 2.3 %all-to-all-done.1 = f32[16,8,128]{2,1,0:T(8,128)S(1)} async-done(((f32[16,8,128]{2,1,0:T(8,128)}), f32[16,8,128]{2,1,0:T(8,128)S(1)}, u32[]{:S(2)}, u32[]{:S(2)}) %all-to-all-start.1) | async-done | bytes 65568 | tf_op jit(solution)/shard_map/all_to_all | solution.py:637
  56.7 0.0 copy-done.5
  56.7 0.0 copy-done.10
  56.7 0.0 copy-done.13
  56.7 1.7 %solve.1 = (f32[384,128]{1,0:T(8,128)}, f32[8,128]{1,0:T(8,128)S(1)}) custom-call(f32[128,128]{1,0:T(8,128)S(1)} %bitcast.20, f32[256,128]{1,0:T(8,128)S(1)} %copy-done.13, f32[8,128]{1,0:T(8,128)S(1)} %get-tuple-element.60.kink, f32[384,256]{1,0:T(8,128)S(1)} %copy-done.5, f32[16,256]{1,0:T(8,128)S(1)} %copy-done.10, f32[256,128]{1,0:T(8,128)S(1)} %copy-done.7, ...), custom_call_target="tpu_custom_call" | custom-call | flops 1000000000 | bytes 4000000 | tf_op jit(solution)/shard_map/solve/pallas_call | solution.py:657
  58.4 0.0 copy-start.15
  58.4 3.7 %all-to-all-start.2 = ((f32[16,24,128]{2,1,0:T(8,128)}), f32[16,24,128]{2,1,0:T(8,128)S(1)}, u32[]{:S(2)}, u32[]{:S(2)}) async-start(f32[16,24,128]{2,1,0:T(8,128)} %bitcast.10), calls=%async_computation.2 | async-start | bytes 393216 | tf_op jit(solution)/shard_map/all_to_all | solution.py:663
  62.1 2.2 %scatter.1 = (f32[256,128]{1,0:T(8,128)}, f32[256,128]{1,0:T(8,128)}) custom-call(f32[512,128]{1,0:T(8,128)S(1)} %get-tuple-element.78.stars, s32[9,1024]{1,0:T(8,128)S(1)} %get-tuple-element.66.cell, f32[9,1024]{1,0:T(8,128)S(1)} %get-tuple-element.79.gain, f32[8,128]{1,0:T(8,128)S(1)} %get-tuple-element.80.after), custom_call_target="tpu_custom_call" | custom-call | flops 2000000000 | bytes 8000000 | tf_op jit(solution)/shard_map/scatter/pallas_call | solution.py:664
  64.3 5.7 %all-to-all-done.2 = f32[16,24,128]{2,1,0:T(8,128)S(1)} async-done(((f32[16,24,128]{2,1,0:T(8,128)}), f32[16,24,128]{2,1,0:T(8,128)S(1)}, u32[]{:S(2)}, u32[]{:S(2)}) %all-to-all-start.2) | async-done | bytes 196640 | tf_op jit(solution)/shard_map/all_to_all | solution.py:663
  70.0 0.0 copy-done.9
  70.0 0.0 copy-done.15
  70.0 6.4 %final.1 = (f32[256,128]{1,0:T(8,128)}, f32[256,128]{1,0:T(8,128)}, f32[256,128]{1,0:T(8,128)}, f32[3,10,3,1024]{3,2,1,0:T(4,128)}) custom-call(f32[384,128]{1,0:T(8,128)S(1)} %bitcast.19, f32[256,128]{1,0:T(8,128)} %get-tuple-element.71.east_s, f32[256,128]{1,0:T(8,128)} %get-tuple-element.72.north_s, ...), custom_call_target="tpu_custom_call", output_to_operand_aliasing={{0}: (1, {}), {1}: (2, {}), {2}: (3, {})} | custom-call | flops 4000000000 | bytes 16000000 | tf_op jit(solution)/shard_map/final/pallas_call | solution.py:672
  (1 shorter events, 0.0 us)
Async XLA Ops:
  0.6 18.0 %copy-start.11 = (f32[32,32]{1,0:T(8,128)S(1)}, f32[32,32]{1,0:T(8,128)}, u32[]{:S(2)}) copy-start(f32[32,32]{1,0:T(8,128)} %constant.16.clone.ztab) | copy-start | bytes 12292
  3.0 13.8 %collective-permute-start = (f32[288,128]{1,0:T(8,128)}, f32[288,128]{1,0:T(8,128)S(1)}, u32[]{:S(2)}, u32[]{:S(2)}) collective-permute-start(f32[288,128]{1,0:T(8,128)} %get-tuple-element.47), channel_id=1, source_target_pairs={{0,16},{16,32},{32,48},{48,64},{64,80},{80,96},{96,112},{112,128},... | collective-permute-start | bytes 442376 | tf_op jit(solution)/shard_map/ppermute | solution.py:593
  5.1 13.4 %collective-permute-start.1 = (f32[288,128]{1,0:T(8,128)}, f32[288,128]{1,0:T(8,128)S(1)}, u32[]{:S(2)}, u32[]{:S(2)}) collective-permute-start(f32[288,128]{1,0:T(8,128)} %get-tuple-element.48), channel_id=1, source_target_pairs={{0,240},{16,0},{32,16},{48,32},{64,48},{80,64},{96,80},{112,96},{1... | collective-permute-start | bytes 442376 | tf_op jit(solution)/shard_map/ppermute | solution.py:594
  8.9 9.6 %collective-permute-start.2 = (f32[288,128]{1,0:T(8,128)}, f32[288,128]{1,0:T(8,128)S(1)}, u32[]{:S(2)}, u32[]{:S(2)}) collective-permute-start(f32[288,128]{1,0:T(8,128)} %get-tuple-element.49), channel_id=1, source_target_pairs={{0,1},{1,2},{2,3},{3,4},{4,5},{5,6},{6,7},{7,8},{8,9},{9,10},{10,1... | collective-permute-start | bytes 442376 | tf_op jit(solution)/shard_map/ppermute | solution.py:595
  11.5 7.1 %collective-permute-start.3 = (f32[288,128]{1,0:T(8,128)}, f32[288,128]{1,0:T(8,128)S(1)}, u32[]{:S(2)}, u32[]{:S(2)}) collective-permute-start(f32[288,128]{1,0:T(8,128)} %get-tuple-element.50), channel_id=1, source_target_pairs={{0,15},{1,0},{2,1},{3,2},{4,3},{5,4},{6,5},{7,6},{8,7},{9,8},{10,9... | collective-permute-start | bytes 442376 | tf_op jit(solution)/shard_map/ppermute | solution.py:596
  11.7 21.7 %copy-start.6 = (f32[256,384]{1,0:T(8,128)S(1)}, f32[256,384]{1,0:T(8,128)}, u32[]{:S(2)}) copy-start(f32[256,384]{1,0:T(8,128)} %constant.18.clone.wmain) | copy-start | bytes 1179652
  11.7 21.7 %copy-start.7 = (f32[256,128]{1,0:T(8,128)S(1)}, f32[256,128]{1,0:T(8,128)}, u32[]{:S(2)}) copy-start(f32[256,128]{1,0:T(8,128)} %constant.22.clone.cs) | copy-start | bytes 393220
  15.3 10.9 %collective-permute-start.4 = (f32[40,1024]{1,0:T(8,128)}, f32[40,1024]{1,0:T(8,128)S(1)}, u32[]{:S(2)}, u32[]{:S(2)}) collective-permute-start(f32[40,1024]{1,0:T(8,128)} %get-tuple-element.54), channel_id=1, source_target_pairs={{0,1},{1,2},{2,3},{3,4},{4,5},{5,6},{6,7},{7,8},{8,9},{9,10},{10,1... | collective-permute-start | bytes 491528 | tf_op jit(solution)/shard_map/ppermute | solution.py:612
  16.8 9.4 %collective-permute-start.5 = (f32[40,1024]{1,0:T(8,128)}, f32[40,1024]{1,0:T(8,128)S(1)}, u32[]{:S(2)}, u32[]{:S(2)}) collective-permute-start(f32[40,1024]{1,0:T(8,128)} %get-tuple-element.55), channel_id=1, source_target_pairs={{0,15},{1,0},{2,1},{3,2},{4,3},{5,4},{6,5},{7,6},{8,7},{9,8},{10,9... | collective-permute-start | bytes 491528 | tf_op jit(solution)/shard_map/ppermute | solution.py:613
  18.6 1.1 %copy-start = (f32[1280,128]{1,0:T(8,128)S(1)}, f32[1280,128]{1,0:T(8,128)}, u32[]{:S(2)}) copy-start(f32[1280,128]{1,0:T(8,128)} %get-tuple-element.46.fields) | copy-start | bytes 1966084
  19.7 13.7 %copy-start.2 = (f32[784,128]{1,0:T(8,128)S(1)}, f32[784,128]{1,0:T(8,128)}, u32[]{:S(2)}) copy-start(f32[784,128]{1,0:T(8,128)} %get-tuple-element.52.tabs) | copy-start | bytes 1204228
  19.7 29.2 %copy-start.1 = (f32[1280,128]{1,0:T(8,128)S(1)}, f32[1280,128]{1,0:T(8,128)}, u32[]{:S(2)}) copy-start(f32[1280,128]{1,0:T(8,128)} %get-tuple-element.46.fields) | copy-start | bytes 1966084
  19.7 29.2 %copy-start.4 = (f32[16,1024]{1,0:T(8,128)S(1)}, f32[16,1024]{1,0:T(8,128)}, u32[]{:S(2)}) copy-start(f32[16,1024]{1,0:T(8,128)} %get-tuple-element.61.mid) | copy-start | bytes 196612
  22.7 10.7 %all-to-all-start = ((f32[16,24,128]{2,1,0:T(8,128)}), f32[16,24,128]{2,1,0:T(8,128)S(1)}, u32[]{:S(2)}, u32[]{:S(2)}) async-start(f32[16,24,128]{2,1,0:T(8,128)} %bitcast.6), calls=%async_computation | async-start | bytes 393216 | tf_op jit(solution)/shard_map/all_to_all | solution.py:622
  26.2 1.0 %copy-start.3 = (f32[80,1024]{1,0:T(8,128)S(1)}, f32[80,1024]{1,0:T(8,128)}, u32[]{:S(2)}) copy-start(f32[80,1024]{1,0:T(8,128)} %get-tuple-element.53.part) | copy-start | bytes 983044
  27.2 21.7 %collective-permute-start.6 = (f32[64,1024]{1,0:T(8,128)S(1)}, f32[64,1024]{1,0:T(8,128)S(1)}, u32[]{:S(2)}, u32[]{:S(2)}) collective-permute-start(f32[64,1024]{1,0:T(8,128)S(1)} %get-tuple-element.62), channel_id=1, source_target_pairs={{0,16},{16,32},{32,48},{48,64},{64,80},{80,96},{96,112},{112,128},... | collective-permute-start | bytes 786440 | tf_op jit(solution)/shard_map/ppermute | solution.py:626
  28.5 20.4 %collective-permute-start.7 = (f32[64,1024]{1,0:T(8,128)S(1)}, f32[64,1024]{1,0:T(8,128)S(1)}, u32[]{:S(2)}, u32[]{:S(2)}) collective-permute-start(f32[64,1024]{1,0:T(8,128)S(1)} %get-tuple-element.63), channel_id=1, source_target_pairs={{0,240},{16,0},{32,16},{48,32},{64,48},{80,64},{96,80},{112,96},{1... | collective-permute-start | bytes 786440 | tf_op jit(solution)/shard_map/ppermute | solution.py:627
  33.4 0.9 %copy-start.8 = (f32[256,16]{1,0:T(8,128)S(1)}, f32[256,16]{1,0:T(8,128)}, u32[]{:S(2)}) copy-start(f32[256,16]{1,0:T(8,128)} %constant.20.clone.t12) | copy-start | bytes 49156
  36.4 0.7 copy-start.12
  37.0 19.7 %all-to-all-start.1 = ((f32[16,8,128]{2,1,0:T(8,128)}), f32[16,8,128]{2,1,0:T(8,128)S(1)}, u32[]{:S(2)}, u32[]{:S(2)}) async-start(f32[16,8,128]{2,1,0:T(8,128)} %bitcast.8), calls=%async_computation.1 | async-start | bytes 131072 | tf_op jit(solution)/shard_map/all_to_all | solution.py:637
  48.9 7.8 %copy-start.5 = (f32[384,256]{1,0:T(8,128)S(1)}, f32[384,256]{1,0:T(8,128)}, u32[]{:S(2)}) copy-start(f32[384,256]{1,0:T(8,128)} %constant.19.clone.wback) | copy-start | bytes 1179652
  48.9 7.8 %copy-start.10 = (f32[16,256]{1,0:T(8,128)S(1)}, f32[16,256]{1,0:T(8,128)}, u32[]{:S(2)}) copy-start(f32[16,256]{1,0:T(8,128)} %constant.21.clone.t12t) | copy-start | bytes 49156
  49.0 7.8 %copy-start.13 = (f32[256,128]{1,0:T(8,128)S(1)}, f32[256,128]{1,0:T(8,128)}, u32[]{:S(2)}) copy-start(f32[256,128]{1,0:T(8,128)} %copy-done.12) | copy-start | bytes 393220
  53.5 0.9 %copy-start.14 = (f32[11,9,1024]{2,1,0:T(8,128)}, f32[11,9,1024]{2,1,0:T(8,128)S(1)}, u32[]{:S(2)}) copy-start(f32[11,9,1024]{2,1,0:T(8,128)S(1)} %get-tuple-element.74.state) | copy-start | bytes 1216516
  54.4 15.6 %copy-start.9 = (f32[64,32]{1,0:T(8,128)S(1)}, f32[64,32]{1,0:T(8,128)}, u32[]{:S(2)}) copy-start(f32[64,32]{1,0:T(8,128)} %constant.17.clone.zback) | copy-start | bytes 24580
  58.4 11.6 %copy-start.15 = (f32[11,9,1024]{2,1,0:T(8,128)S(1)}, f32[11,9,1024]{2,1,0:T(8,128)}, u32[]{:S(2)}) copy-start(f32[11,9,1024]{2,1,0:T(8,128)} %copy-done.14) | copy-start | bytes 1216516
  58.4 11.5 %all-to-all-start.2 = ((f32[16,24,128]{2,1,0:T(8,128)}), f32[16,24,128]{2,1,0:T(8,128)S(1)}, u32[]{:S(2)}, u32[]{:S(2)}) async-start(f32[16,24,128]{2,1,0:T(8,128)} %bitcast.10), calls=%async_computation.2 | async-start | bytes 393216 | tf_op jit(solution)/shard_map/all_to_all | solution.py:663

commit v4 on v3

--- a/solution.py
+++ b/solution.py
@@ -73,8 +73,6 @@
     coef = np.where(zero, 0.0, -1.0 / (2.0 * np.sinh(-lnr)))
     lnr = lnr.reshape(2, GX, TX).transpose(1, 0, 2).reshape(GX, 2 * TX)
     coef = coef.reshape(2, GX, TX).transpose(1, 0, 2).reshape(GX, 2 * TX)
-    rpow = np.exp(lnr[:, :, None] * lane)
-    rrev = np.exp(lnr[:, :, None] * (NY - lane))
     misc = np.zeros((GX, 2 * TX, NY))
     for k in range(8):
         misc[:, :, k] = np.exp(lnr * (1 << k))
@@ -82,7 +80,8 @@
     rowtab = np.zeros((GX, 8, 2 * TX))
     rowtab[:, 0] = NY * lnr
     rowtab[:, 1] = 1.0 / (1.0 - np.exp(lnr * TY))
-    own = np.concatenate([rpow, rrev, misc, rowtab[:, :, :NY], rowtab[:, :, NY:]], axis=1)
+    misc[:, :, 9] = lnr
+    own = np.concatenate([misc, rowtab[:, :, :NY], rowtab[:, :, NY:]], axis=1)
 
     def f(a):
         return jnp.asarray(np.asarray(a, np.float32))
@@ -153,7 +152,7 @@
     return out
 
 
-def sides_kernel(u, v, w, h, q, xlo, xhi, ylo, yhi, done, fields, sems):
+def sides_kernel(u, v, w, h, q, xlo, xhi, ylo, yhi, fields, done, sems):
     done[...] = jnp.zeros_like(done)
     copies = [
         pltpu.make_async_copy(ref, fields.at[pl.ds(f * ROWS, ROWS)], sems.at[f])
@@ -163,7 +162,7 @@
         copy.start()
     for copy in copies:
         copy.wait()
-    for f in range(3):
+    for f in range(5):
         for i in range(3):
             n = f * 3 + i
             xlo[n * NZ : (n + 1) * NZ, :] = field_row(fields, f, 5 + i)
@@ -185,41 +184,31 @@
 
 
 def pack_kernel(
-    u, v, w, h, q, drops_in, cells, counts, own, after,
-    up, down, mid, part, fields, tabs, drops, sems,
+    drops_in, cells, counts, own, after, up, down, mid, part, tabs, drops, sems
 ):
     copies = [
-        pltpu.make_async_copy(ref, fields.at[pl.ds(f * ROWS, ROWS)], sems.at[f])
-        for f, ref in enumerate((u, v, w, h, q))
+        pltpu.make_async_copy(drops_in, drops, sems.at[0]),
+        pltpu.make_async_copy(own.at[lax.axis_index("gx")], tabs, sems.at[1]),
     ]
-    copies.append(pltpu.make_async_copy(drops_in, drops, sems.at[5]))
-    copies.append(pltpu.make_async_copy(own.at[lax.axis_index("gx")], tabs, sems.at[6]))
     for copy in copies:
         copy.start()
-    copies[5].wait()
+    copies[0].wait()
     for out, at, r, s in (
         [(up, r * SLOT, r, 2) for r in range(3)]
         + [(down, r * SLOT, r, 0) for r in range(3)]
-        + [(mid, 0, 1, 1), (part, 0, 2, 1), (part, 40, 0, 1)]
+        + [(mid, 0, 1, 1), (part, 0, 2, 1), (part, 16, 0, 1)]
     ):
         for a in range(10):
             out[at + a : at + a + 1, :] = drops[r, a, s : s + 1, :]
         out[at + 10 : at + 11, :] = cells[r, s : s + 1, :].astype(F32)
         out[at + 11 : at + 12, :] = jnp.full((1, CAP), counts[r, s], jnp.int32).astype(F32)
-    for out, at, rows in ((up, 36, 4), (down, 36, 4), (mid, 12, 4), (part, 12, 4), (part, 52, 4)):
+    for out, at, rows in ((up, 36, 4), (down, 36, 4), (mid, 12, 4), (part, 12, 4), (part, 28, 4)):
         out[at : at + rows, :] = jnp.zeros((rows, CAP), F32)
-    copies[3].wait()
-    copies[4].wait()
-    for k, x0 in enumerate((5, 0)):
-        for f in range(2):
-            for i in range(3):
-                row = field_row(fields, 3 + f, x0 + i)
-                for g in range(4):
-                    n = (f * 3 + i) * 4 + g
-                    a, c = 40 * k + 16 + 8 * (n // 8), NY * (n % 8)
-                    part[a : a + 8, c : c + NY] = row[g * 8 : (g + 1) * 8]
-    for k in (0, 1, 2, 6):
-        copies[k].wait()
+    copies[1].wait()
+
+
+def hop_kernel(up, down, after, up_out, down_out, done):
+    done[...] = jnp.zeros_like(done)
 
 
 def block_of(msg, n):
@@ -235,7 +224,7 @@
     for n, (out, r) in enumerate(((up, 2), (down, 0))):
         out[0:12, :] = mlo[r * SLOT : (r + 1) * SLOT, :]
         out[12:24, :] = mhi[r * SLOT : (r + 1) * SLOT, :]
-        out[24:64, :] = part[n * 40 : (n + 1) * 40, :]
+        out[24:40, :] = part[n * 16 : (n + 1) * 16, :]
 
 
 def wind_kernel(fields, xlo, xhi, ylo_in, yhi_in, ztab, east_s, north_s, rise_s, send, done, zs):
@@ -282,12 +271,12 @@
 
 def own_tables(tabs):
     n = 2 * TX
-    return tabs.at[0:n], tabs.at[n : 2 * n], tabs.at[2 * n : 3 * n], tabs.at[3 * n : 3 * n + 16]
+    return tabs.at[0:n], tabs.at[n : n + 16]
 
 
 def scan_kernel(recv, wmain, t12, cs, tabs, after, msg, keep, kink, done):
     done[...] = jnp.zeros_like(done)
-    rpow, rrev, misc, rowtab = own_tables(tabs)
+    misc, rowtab = own_tables(tabs)
     lane = iota((2 * TX, NY), 1)
     d = dot(wmain[...], recv[...])
     ends = []
@@ -307,7 +296,8 @@
     r128 = misc[:, 7:8]
     out_right = r1 * fwd[:, NY - 1 : NY] + e
     out_left = bwd[:, 0:1] + r128 * e
-    keep[...] = fwd + bwd - d + rrev[...] * e
+    from_end = float(NY) - lane.astype(F32)
+    keep[...] = fwd + bwd - d + jnp.exp(from_end * misc[:, 9:10]) * e
     lane1 = lane[:TX]
     table = jnp.zeros((TX, NY), F32)
     for b in range(2):
@@ -330,7 +320,7 @@
 
 def solve_kernel(got, keep, kink, wback, t12t, cs, tabs, after, send, done):
     done[...] = jnp.zeros_like(done)
-    rpow, rrev, misc, rowtab = own_tables(tabs)
+    misc, rowtab = own_tables(tabs)
     here = lax.axis_index("gy")
     first = (lax.axis_index("gx") == 0).astype(F32)
     who = iota((GY, 2 * TX), 0)
@@ -353,7 +343,11 @@
     in_left = turned[:, 0:1]
     in_right = turned[:, 1:2]
     coef = misc[:, 8:9]
-    pres = coef * (keep[...] + rpow[...] * in_left + rrev[...] * in_right)
+    lnc = jnp.broadcast_to(misc[:, 9:10], (2 * TX, NY))
+    at = iota((2 * TX, NY), 1).astype(F32)
+    pres = coef * (
+        keep[...] + jnp.exp(at * lnc) * in_left + jnp.exp((float(NY) - at) * lnc) * in_right
+    )
     edge = coef * (turned[:, 2:3] + misc[:, 7:8] * in_left + in_right)
     who1 = iota((GY, 1), 0)
     far = (NY * ((here - who1) & (GY - 1))).astype(F32)
@@ -412,30 +406,25 @@
 CHUNK = 512
 
 
-def heat_kernel(fields, ylo_in, yhi_in, mid, mlo, mhi, clo, chi, after, stars, lhs, cell_out, state, done, zs):
+def heat_kernel(fields, ylo_in, yhi_in, xlo, xhi, after, stars, lhs, done, zs):
     done[...] = jnp.zeros_like(done)
     lane = iota((NZ, NY), 1)
     ylo = ylo_in[0:NZ, :]
     yhi = yhi_in[0:NZ, :]
     vel = [velocity_rows(fields, x) for x in range(NX)]
 
-    def side(msg, n):
-        parts = []
-        for g in range(4):
-            k = n * 4 + g
-            a, c = 40 + 8 * (k // 8), NY * (k % 8)
-            parts.append(msg[a : a + 8, c : c + NY])
-        return jnp.concatenate(parts, axis=0)
-
     for f in range(2):
-        rows = [side(clo, f * 3 + i) for i in range(3)]
+        rows = [xlo[(f * 3 + i + 9) * NZ : (f * 3 + i + 10) * NZ, :] for i in range(3)]
         rows += [field_row(fields, 3 + f, x) for x in range(NX)]
-        rows += [side(chi, f * 3 + i) for i in range(3)]
+        rows += [xhi[(f * 3 + i + 9) * NZ : (f * 3 + i + 10) * NZ, :] for i in range(3)]
         for x in range(NX):
             star = star_row(x, rows, ylo, yhi, 3 + f, vel[x], zs.at[f * NX + x], lane)
             at = (f * NX + x) * NZ
             stars[at : at + NZ, :] = star
         store_table(lhs, f, stars[f * ROWS : (f + 1) * ROWS, :])
+
+
+def unpack_kernel(mid, mlo, mhi, clo, chi, after, cell_out, state):
     for r in range(3):
         for s in range(3):
             n = r * 3 + s
@@ -451,8 +440,7 @@
             state[10, n : n + 1, :] = jnp.where(slot < count, 1.0, 0.0)
 
 
-def growth_kernel(lhs, cell, state, after, state_out, gain_out, done, air):
-    done[...] = jnp.zeros_like(done)
+def growth_kernel(lhs, cell, state, state_out, gain, air):
     gather_all(lhs, 2, cell, air)
     live = state[10]
     radius = state[6]
@@ -463,7 +451,7 @@
         saturation - CURVATURE / radius + SOLUTE_EFFECT * state[8] / cubed
     )
     new_radius = jnp.sqrt(jnp.maximum(squared, RADIUS_FLOOR * RADIUS_FLOOR))
-    gain_out[...] = live * state[7] * (new_radius * new_radius * new_radius - cubed)
+    gain[...] = live * state[7] * (new_radius * new_radius * new_radius - cubed)
     state_out[6] = new_radius * live
     state_out[7] = state[7] * live
     state_out[8] = state[8] * live
@@ -474,7 +462,7 @@
     state_out[10] = (1.0 - keeping) * live
 
 
-def scatter_kernel(stars, cell, gain, after, heat_next, moist_next, acc):
+def scatter_kernel(stars, cell, gain, heat_next, moist_next, acc):
     acc[...] = jnp.zeros_like(acc)
 
     for n in range(9):
@@ -556,12 +544,12 @@
 TOKEN = sds(8, NY)
 
 
-def call(kernel, name, us, out_shape, in_specs, scratch=(), mib=6, aliases=None):
+def call(kernel, name, us, out_shape, in_specs, scratch=(), mib=6, aliases=None, outs=None):
     return pl.pallas_call(
         kernel,
         out_shape=out_shape,
         in_specs=in_specs,
-        out_specs=tuple(VM for _ in out_shape),
+        out_specs=tuple(outs or [VM] * len(out_shape)),
         scratch_shapes=list(scratch),
         input_output_aliases=aliases or {},
         compiler_params=pltpu.CompilerParams(vmem_limit_bytes=mib * 1024 * 1024),
@@ -581,36 +569,31 @@
     tab = make_tables()
     u, v, w, h, q = (a.reshape(ROWS, NY) for a in (u, v, w, h, q))
     drops = droplets.transpose(0, 2, 1, 3)
-    xlo, xhi, ylo, yhi, done = call(
+    xlo, xhi, ylo, yhi, fields, done = call(
         sides_kernel,
         "sides",
         2.0,
-        (sds(9 * NZ, NY), sds(9 * NZ, NY), sds(9 * NZ, NY), sds(9 * NZ, NY), TOKEN),
+        (
+            sds(15 * NZ, NY), sds(15 * NZ, NY), sds(9 * NZ, NY), sds(9 * NZ, NY),
+            sds(5 * ROWS, NY), TOKEN,
+        ),
         [HBM] * 5,
-        [pltpu.VMEM((5 * ROWS, NY), F32), pltpu.SemaphoreType.DMA((5,))],
+        [pltpu.SemaphoreType.DMA((5,))],
         60,
     )(u, v, w, h, q)
     xlo = lax.ppermute(xlo, "gx", ring("gx", 1))
     xhi = lax.ppermute(xhi, "gx", ring("gx", -1))
     ylo = lax.ppermute(ylo, "gy", ring("gy", 1))
     yhi = lax.ppermute(yhi, "gy", ring("gy", -1))
-    up, down, mid, part, fields, tabs = call(
+    up, down, mid, part, tabs = call(
         pack_kernel,
         "pack",
         2.5,
-        (
-            sds(40, CAP), sds(40, CAP), sds(16, CAP), sds(80, CAP), sds(5 * ROWS, NY),
-            sds(6 * TX + 16, NY),
-        ),
-        [HBM] * 6 + [VM, SM, HBM, ANY],
-        [
-            pltpu.VMEM((3, 10, 3, CAP), F32),
-            pltpu.SemaphoreType.DMA((7,)),
-        ],
+        (sds(40, CAP), sds(40, CAP), sds(16, CAP), sds(32, CAP), sds(2 * TX + 16, NY)),
+        [HBM, VM, SM, HBM, ANY],
+        [pltpu.VMEM((3, 10, 3, CAP), F32), pltpu.SemaphoreType.DMA((2,))],
         60,
-    )(u, v, w, h, q, drops, cells, counts, tab["own"], done)
-    mlo = lax.ppermute(up, "gy", ring("gy", 1))
-    mhi = lax.ppermute(down, "gy", ring("gy", -1))
+    )(drops, cells, counts, tab["own"], done)
     east_s, north_s, rise_s, send, done = call(
         wind_kernel,
         "winds",
@@ -620,11 +603,17 @@
         [pltpu.VMEM((3 * NX, NZ + 16, NY), F32)],
     )(fields, xlo, xhi, ylo, yhi, tab["ztab"])
     recv = lax.all_to_all(send.reshape(GX, BLK, NY), "gx", 0, 0, tiled=True)
-    cup, cdown, done = call(
-        relay_kernel, "relay", 1.0, (sds(64, CAP), sds(64, CAP), TOKEN), [VM] * 3 + [ANY]
-    )(part, mlo, mhi, done)
-    clo = lax.ppermute(cup, "gx", ring("gx", 1))
-    chi = lax.ppermute(cdown, "gx", ring("gx", -1))
+    up, down, done = call(
+        hop_kernel,
+        "hop",
+        0.5,
+        (sds(40, CAP), sds(40, CAP), TOKEN),
+        [ANY] * 3,
+        aliases={0: 0, 1: 1},
+        outs=[ANY, ANY, VM],
+    )(up, down, done)
+    mlo = lax.ppermute(up, "gy", ring("gy", 1))
+    mhi = lax.ppermute(down, "gy", ring("gy", -1))
     msg, keep, kink, done = call(
         scan_kernel,
         "scan",
@@ -635,25 +624,19 @@
         recv.reshape(GX * BLK, NY), tab["wmain"], tab["t12"], tab["cs"], tabs, done
     )
     got = lax.all_to_all(msg.reshape(GY, 8, NY), "gy", 0, 0, tiled=True)
-    stars_hq, lhs, cell_in, state, done = call(
+    stars_hq, lhs, done = call(
         heat_kernel,
         "heat",
-        3.0,
-        (
-            sds(2 * ROWS, NY), sds(4 * NY, ROWS, dtype=BF16),
-            sds(9, CAP, dtype=jnp.int32), sds(11, 9, CAP), TOKEN,
-        ),
-        [VM] * 8 + [ANY],
+        4.0,
+        (sds(2 * ROWS, NY), sds(4 * NY, ROWS, dtype=BF16), TOKEN),
+        [VM] * 5 + [ANY],
         [pltpu.VMEM((2 * NX, NZ + 16, NY), F32)],
-    )(fields, ylo, yhi, mid, mlo, mhi, clo, chi, done)
-    state, gain, done = call(
-        growth_kernel,
-        "growth",
-        5.0,
-        (sds(11, 9, CAP), sds(9, CAP), TOKEN),
-        [VM] * 3 + [ANY],
-        [pltpu.VMEM((2, 9, CAP), F32)],
-    )(lhs, cell_in, state, done)
+    )(fields, ylo, yhi, xlo, xhi, done)
+    cup, cdown, done = call(
+        relay_kernel, "relay", 1.0, (sds(40, CAP), sds(40, CAP), TOKEN), [VM] * 3 + [ANY]
+    )(part, mlo, mhi, done)
+    clo = lax.ppermute(cup, "gx", ring("gx", 1))
+    chi = lax.ppermute(cdown, "gx", ring("gx", -1))
     send, done = call(
         solve_kernel, "solve", 2.0, (sds(GX * BLK, NY), TOKEN), [VM] * 7 + [ANY]
     )(
@@ -661,14 +644,29 @@
         done,
     )
     recv = lax.all_to_all(send.reshape(GX, BLK, NY), "gx", 0, 0, tiled=True)
+    cell_in, state = call(
+        unpack_kernel,
+        "unpack",
+        1.0,
+        (sds(9, CAP, dtype=jnp.int32), sds(11, 9, CAP)),
+        [VM] * 5 + [ANY],
+    )(mid, mlo, mhi, clo, chi, done)
+    state, gain = call(
+        growth_kernel,
+        "growth",
+        5.0,
+        (sds(11, 9, CAP), sds(9, CAP)),
+        [VM] * 3,
+        [pltpu.VMEM((2, 9, CAP), F32)],
+    )(lhs, cell_in, state)
     heat_next, moist_next = call(
         scatter_kernel,
         "scatter",
         4.0,
         (sds(ROWS, NY), sds(ROWS, NY)),
-        [VM] * 3 + [ANY],
+        [VM] * 3,
         [pltpu.VMEM((ROWS, 2 * NY), F32)],
-    )(stars_hq, cell_in, gain, done)
+    )(stars_hq, cell_in, gain)
     east_next, north_next, up_next, drops_out = call(
         final_kernel,
         "final",

time: 76.9 us -> 75.2 us (0.978)
  local copies, waits for them, and re-layouts: 4.52 us -> 2.05 us
  starting transfers between devices: 35.8 us -> 37.5 us
    all_to_all x2, waiting for transfers between devices: 6.97 us -> 2.74 us  [per_device(): recv = lax.all_to_all(send.reshape(GX, BLK, NY), 'gx', 0, 0, tiled=True)]
    ppermute x1, waiting for transfers between devices: 0.01 us -> 2.66 us  [per_device(): yhi = lax.ppermute(yhi, 'gy', ring('gy', -1))]
    unnamed x32 -> x26, local copies, waits for them, and re-layouts: 4.52 us -> 2.05 us
    ppermute x1, starting transfers between devices: 1.54 us -> 3.88 us  [per_device(): mlo = lax.ppermute(up, 'gy', ring('gy', 1))]
    ppermute x1, waiting for transfers between devices: 0.01 us -> 2.2 us  [per_device(): ylo = lax.ppermute(ylo, 'gy', ring('gy', 1))]
    ppermute x1, starting transfers between devices: 1.73 us -> 0.01 us  [per_device(): mhi = lax.ppermute(down, 'gy', ring('gy', -1))]
    all_to_all x1, waiting for transfers between devices: 2.3 us -> 1.2 us  [per_device(): got = lax.all_to_all(msg.reshape(GY, 8, NY), 'gy', 0, 0, tiled=True)]
    ppermute x1, starting transfers between devices: 3.54 us -> 4.5 us  [per_device(): chi = lax.ppermute(cdown, 'gx', ring('gx', -1))]
  transfers between devices with their start and end apart: 11 -> 11, of which waited for: 3 -> 5; matrix products, arithmetic and copies ran while one was open for 0% -> 0% of each run, Pallas kernels for 20% -> 18%
where the time goes in v4:
time: 75.2 us; the launch traced here: 74.8 us
  starting transfers between devices  37.5 us (50%)
  Pallas kernels  25.5 us (34%)
  waiting for transfers between devices  8.82 us (12%)
  local copies, waits for them, and re-layouts  2.05 us (3%)
  between operations  0.88 us (1%)
    all_to_all x1, starting transfers between devices, per_device(): got = lax.all_to_all(msg.reshape(GY, 8, NY), 'gy', 0, 0, tiled=True)  12 us
    all_to_all x2, starting transfers between devices, per_device(): recv = lax.all_to_all(send.reshape(GX, BLK, NY), 'gx', 0, 0, tiled=True)  8.09 us
    pallas_call x1, Pallas kernels, per_device(): call(final_kernel, 'final', 8.0, (sds(ROWS, NY), sds(ROWS, NY), sds(ROWS,...  6.38 us
    ppermute x1, starting transfers between devices, per_device(): chi = lax.ppermute(cdown, 'gx', ring('gx', -1))  4.5 us
    ppermute x1, starting transfers between devices, per_device(): mlo = lax.ppermute(up, 'gy', ring('gy', 1))  3.88 us
    ppermute x1, starting transfers between devices, per_device(): xhi = lax.ppermute(xhi, 'gx', ring('gx', -1))  3.81 us
    pallas_call x1, Pallas kernels, per_device(): call(wind_kernel, 'winds', 3.0, (sds(ROWS, NY), sds(ROWS, NY), sds(ROWS,...  2.96 us
    pallas_call x1, Pallas kernels, per_device(): call(growth_kernel, 'growth', 5.0, (sds(11, 9, CAP), sds(9, CAP)), [VM] *...  2.92 us
  transfers between devices with their start and end apart: 11, of which 5 were waited for; matrix products, arithmetic and copies ran while one was open for 0% of the time, Pallas kernels for 18%

profile of v4, /device:TPU:1, one launch (start us, length us, event | category | flops | bytes accessed | tf_op | source)
XLA Modules:
  0.0 74.8 jit_solution(5730920077039327961)
XLA Ops:
  0.6 0.0 copy-start.6
  0.6 2.7 %sides.1 = (f32[480,128]{1,0:T(8,128)}, f32[480,128]{1,0:T(8,128)}, f32[288,128]{1,0:T(8,128)}, f32[288,128]{1,0:T(8,128)}, f32[1280,128]{1,0:T(8,128)}, /*index=5*/f32[8,128]{1,0:T(8,128)}) custom-call(f32[256,128]{1,0:T(8,128)} %bitcast.22, f32[256,128]{1,0:T(8,128)} %bitcast.23, f32[256,128]{1,0:T(8,128)} %bitcast.24, f32[256,128]{1,0:T(8,128)} %bitcast.25, ...), custom_call_target="tpu_custom_call" | custom-call | flops 1000000000 | bytes 4000000 | tf_op jit(solution)/shard_map/sides/pallas_call | solution.py:572
  3.3 2.1 %collective-permute-start = (f32[480,128]{1,0:T(8,128)}, f32[480,128]{1,0:T(8,128)S(1)}, u32[]{:S(2)}, u32[]{:S(2)}) collective-permute-start(f32[480,128]{1,0:T(8,128)} %get-tuple-element.48), channel_id=1, source_target_pairs={{0,16},{16,32},{32,48},{48,64},{64,80},{80,96},{96,112},{112,128},... | collective-permute-start | bytes 737288 | tf_op jit(solution)/shard_map/ppermute | solution.py:584
  5.4 3.8 %collective-permute-start.1 = (f32[480,128]{1,0:T(8,128)}, f32[480,128]{1,0:T(8,128)S(1)}, u32[]{:S(2)}, u32[]{:S(2)}) collective-permute-start(f32[480,128]{1,0:T(8,128)} %get-tuple-element.49), channel_id=1, source_target_pairs={{0,240},{16,0},{32,16},{48,32},{64,48},{80,64},{96,80},{112,96},{1... | collective-permute-start | bytes 737288 | tf_op jit(solution)/shard_map/ppermute | solution.py:585
  9.2 2.5 %collective-permute-start.2 = (f32[288,128]{1,0:T(8,128)}, f32[288,128]{1,0:T(8,128)S(1)}, u32[]{:S(2)}, u32[]{:S(2)}) collective-permute-start(f32[288,128]{1,0:T(8,128)} %get-tuple-element.50), channel_id=1, source_target_pairs={{0,1},{1,2},{2,3},{3,4},{4,5},{5,6},{6,7},{7,8},{8,9},{9,10},{10,1... | collective-permute-start | bytes 442376 | tf_op jit(solution)/shard_map/ppermute | solution.py:586
  11.8 0.2 collective-permute-start.3
  12.0 2.2 %collective-permute-done.2.ylo_in = f32[288,128]{1,0:T(8,128)S(1)} collective-permute-done((f32[288,128]{1,0:T(8,128)}, f32[288,128]{1,0:T(8,128)S(1)}, u32[]{:S(2)}, u32[]{:S(2)}) %collective-permute-start.2) | collective-permute-done | bytes 147488 | tf_op jit(solution)/shard_map/ppermute | solution.py:586
  14.2 2.7 %collective-permute-done.3.yhi_in = f32[288,128]{1,0:T(8,128)S(1)} collective-permute-done((f32[288,128]{1,0:T(8,128)}, f32[288,128]{1,0:T(8,128)S(1)}, u32[]{:S(2)}, u32[]{:S(2)}) %collective-permute-start.3) | collective-permute-done | bytes 147488 | tf_op jit(solution)/shard_map/ppermute | solution.py:587
  16.8 0.0 collective-permute-done.xlo
  16.8 0.0 collective-permute-done.1.xhi
  16.9 0.0 copy-done.6
  16.9 0.0 copy-start.7
  16.9 1.1 %copy-done.7 = f32[1280,128]{1,0:T(8,128)S(1)} copy-done((f32[1280,128]{1,0:T(8,128)S(1)}, f32[1280,128]{1,0:T(8,128)}, u32[]{:S(2)}) %copy-start.7) | copy-done | bytes 655384
  17.9 3.0 %winds.1 = (f32[256,128]{1,0:T(8,128)}, f32[256,128]{1,0:T(8,128)}, f32[256,128]{1,0:T(8,128)}, f32[384,128]{1,0:T(8,128)}, f32[8,128]{1,0:T(8,128)S(1)}) custom-call(f32[1280,128]{1,0:T(8,128)S(1)} %copy-done.7, f32[480,128]{1,0:T(8,128)S(1)} %collective-permute-done.xlo, f32[480,128]{1,0:T(8,128)S(1)} %collective-permute-done.1.xhi, ...), custom_call_target="tpu_custom_call" | custom-call | flops 1500000000 | bytes 6000000 | tf_op jit(solution)/shard_map/winds/pallas_call | solution.py:597
  20.9 3.6 %all-to-all-start = ((f32[16,24,128]{2,1,0:T(8,128)}), f32[16,24,128]{2,1,0:T(8,128)S(1)}, u32[]{:S(2)}, u32[]{:S(2)}) async-start(f32[16,24,128]{2,1,0:T(8,128)} %bitcast.5), calls=%async_computation | async-start | bytes 393216 | tf_op jit(solution)/shard_map/all_to_all | solution.py:605
  24.5 0.0 copy-start.1
  24.5 0.0 copy-start.2
  24.5 0.0 copy-start.3
  24.6 2.8 %pack.1 = (f32[40,1024]{1,0:T(8,128)}, f32[40,1024]{1,0:T(8,128)}, f32[16,1024]{1,0:T(8,128)}, f32[32,1024]{1,0:T(8,128)}, f32[272,128]{1,0:T(8,128)}) custom-call(f32[3,10,3,1024]{3,2,1,0:T(4,128)} %bitcast.21, s32[3,3,1024]{2,1,0:T(4,128)} %cells.1, s32[3,3]{1,0:T(4,128)} %counts.1, f32[16,272,128]{2,1,0:T(8,128)} %constant.23.clone.own, ...), custom_call_target="tpu_custom_call" | custom-call | flops 1250000000 | bytes 5000000 | tf_op jit(solution)/shard_map/pack/pallas_call | solution.py:588
  27.4 0.0 copy-start.8
  27.4 3.9 %collective-permute-start.4 = (f32[40,1024]{1,0:T(8,128)}, f32[40,1024]{1,0:T(8,128)S(1)}, u32[]{:S(2)}, u32[]{:S(2)}) collective-permute-start(f32[40,1024]{1,0:T(8,128)} %get-tuple-element.63), channel_id=1, source_target_pairs={{0,1},{1,2},{2,3},{3,4},{4,5},{5,6},{6,7},{7,8},{8,9},{9,10},{10,1... | collective-permute-start | bytes 491528 | tf_op jit(solution)/shard_map/ppermute | solution.py:615
  31.3 0.0 collective-permute-start.5
  31.3 0.4 all-to-all-done
  31.7 0.0 copy-done.1
  31.7 0.0 copy-done.2
  31.7 0.0 copy-done.3
  31.7 0.0 copy-start.11
  31.7 0.9 %copy-done.11 = f32[272,128]{1,0:T(8,128)S(1)} copy-done((f32[272,128]{1,0:T(8,128)S(1)}, f32[272,128]{1,0:T(8,128)}, u32[]{:S(2)}) %copy-start.11) | copy-done | bytes 139288
  32.6 2.1 %scan.1 = (f32[128,128]{1,0:T(8,128)}, f32[256,128]{1,0:T(8,128)S(1)}, f32[8,128]{1,0:T(8,128)S(1)}, f32[8,128]{1,0:T(8,128)S(1)}) custom-call(f32[384,128]{1,0:T(8,128)S(1)} %bitcast.19, f32[256,384]{1,0:T(8,128)S(1)} %copy-done.1, f32[256,16]{1,0:T(8,128)S(1)} %copy-done.3, f32[256,128]{1,0:T(8,128)S(1)} %copy-done.2, f32[272,128]{1,0:T(8,128)S(1)} %copy-done.11, ...), custom_call_target="tpu_custom_call" | custom-call | flops 1000000000 | bytes 4000000 | tf_op jit(solution)/shard_map/scan/pallas_call | solution.py:617
  34.7 12.0 %all-to-all-start.1 = ((f32[16,8,128]{2,1,0:T(8,128)}), f32[16,8,128]{2,1,0:T(8,128)S(1)}, u32[]{:S(2)}, u32[]{:S(2)}) async-start(f32[16,8,128]{2,1,0:T(8,128)} %bitcast.8), calls=%async_computation.1 | async-start | bytes 131072 | tf_op jit(solution)/shard_map/all_to_all | solution.py:626
  46.7 0.0 copy-done.8
  46.7 0.0 copy-start.9
  46.7 0.0 copy-start
  46.7 0.0 copy-start.5
  46.8 0.0 copy-start.12
  46.8 1.6 %heat.1 = (f32[512,128]{1,0:T(8,128)S(1)}, bf16[512,256]{1,0:T(8,128)(2,1)S(1)}, f32[8,128]{1,0:T(8,128)S(1)}) custom-call(f32[1280,128]{1,0:T(8,128)S(1)} %copy-done.8, f32[288,128]{1,0:T(8,128)S(1)} %collective-permute-done.2.ylo_in, f32[288,128]{1,0:T(8,128)S(1)} %collective-permute-done.3.yhi_in, f32[480,128]{1,0:T(8,128)S(1)} %collective-permute-done.xlo, ...), custom_call_target="tpu_custom_call" | custom-call | flops 2000000000 | bytes 8000000 | tf_op jit(solution)/shard_map/heat/pallas_call | solution.py:627
  48.3 0.0 collective-permute-done.4.mlo
  48.4 0.0 collective-permute-done.5.mhi
  48.4 0.0 copy-done.9
  48.4 0.0 copy-start.10
  48.4 0.4 collective-permute-start.6
  48.8 4.5 %collective-permute-start.7 = (f32[40,1024]{1,0:T(8,128)S(1)}, f32[40,1024]{1,0:T(8,128)S(1)}, u32[]{:S(2)}, u32[]{:S(2)}) collective-permute-start(f32[40,1024]{1,0:T(8,128)S(1)} %get-tuple-element.74), channel_id=1, source_target_pairs={{0,240},{16,0},{32,16},{48,32},{64,48},{80,64},{96,80},{112,96},{1... | collective-permute-start | bytes 491528 | tf_op jit(solution)/shard_map/ppermute | solution.py:639
  53.3 1.2 %all-to-all-done.1 = f32[16,8,128]{2,1,0:T(8,128)S(1)} async-done(((f32[16,8,128]{2,1,0:T(8,128)}), f32[16,8,128]{2,1,0:T(8,128)S(1)}, u32[]{:S(2)}, u32[]{:S(2)}) %all-to-all-start.1) | async-done | bytes 65568 | tf_op jit(solution)/shard_map/all_to_all | solution.py:626
  54.5 0.0 copy-done
  54.5 0.0 copy-done.5
  54.5 0.0 copy-done.12
  54.5 1.7 %solve.1 = (f32[384,128]{1,0:T(8,128)}, f32[8,128]{1,0:T(8,128)S(1)}) custom-call(f32[128,128]{1,0:T(8,128)S(1)} %bitcast.20, f32[256,128]{1,0:T(8,128)S(1)} %get-tuple-element.60.keep, f32[8,128]{1,0:T(8,128)S(1)} %get-tuple-element.61.kink, f32[384,256]{1,0:T(8,128)S(1)} %copy-done, f32[16,256]{1,0:T(8,128)S(1)} %copy-done.5, f32[256,128]{1,0:T(8,128)S(1)} %copy-done.2, ...), custom_call_target="tpu_custom_call" | custom-call | flops 1000000000 | bytes 4000000 | tf_op jit(solution)/shard_map/solve/pallas_call | solution.py:640
  56.3 4.5 %all-to-all-start.2 = ((f32[16,24,128]{2,1,0:T(8,128)}), f32[16,24,128]{2,1,0:T(8,128)S(1)}, u32[]{:S(2)}, u32[]{:S(2)}) async-start(f32[16,24,128]{2,1,0:T(8,128)} %bitcast.10), calls=%async_computation.2 | async-start | bytes 393216 | tf_op jit(solution)/shard_map/all_to_all | solution.py:646
  60.7 0.0 collective-permute-done.6.clo
  60.8 0.0 collective-permute-done.7.chi
  60.8 0.0 copy-done.10
  60.8 0.1 unpack.1
  60.9 2.9 %growth.1 = (f32[11,9,1024]{2,1,0:T(8,128)S(1)}, f32[9,1024]{1,0:T(8,128)S(1)}) custom-call(bf16[512,256]{1,0:T(8,128)(2,1)S(1)} %get-tuple-element.77.lhs, s32[9,1024]{1,0:T(8,128)S(1)} %get-tuple-element.76.cell, f32[11,9,1024]{2,1,0:T(8,128)S(1)} %get-tuple-element.78.state), custom_call_target="tpu_custom_call" | custom-call | flops 2500000000 | bytes 10000000 | tf_op jit(solution)/shard_map/growth/pallas_call | solution.py:654
  63.9 0.0 copy-start.4
  63.9 2.2 %scatter.1 = (f32[256,128]{1,0:T(8,128)}, f32[256,128]{1,0:T(8,128)}) custom-call(f32[512,128]{1,0:T(8,128)S(1)} %get-tuple-element.83.stars, s32[9,1024]{1,0:T(8,128)S(1)} %get-tuple-element.76.cell, f32[9,1024]{1,0:T(8,128)S(1)} %get-tuple-element.84.gain), custom_call_target="tpu_custom_call" | custom-call | flops 2000000000 | bytes 8000000 | tf_op jit(solution)/shard_map/scatter/pallas_call | solution.py:662
  66.0 2.3 %all-to-all-done.2 = f32[16,24,128]{2,1,0:T(8,128)S(1)} async-done(((f32[16,24,128]{2,1,0:T(8,128)}), f32[16,24,128]{2,1,0:T(8,128)S(1)}, u32[]{:S(2)}, u32[]{:S(2)}) %all-to-all-start.2) | async-done | bytes 196640 | tf_op jit(solution)/shard_map/all_to_all | solution.py:646
  68.4 0.0 copy-done.4
  68.4 6.4 %final.1 = (f32[256,128]{1,0:T(8,128)}, f32[256,128]{1,0:T(8,128)}, f32[256,128]{1,0:T(8,128)}, f32[3,10,3,1024]{3,2,1,0:T(4,128)}) custom-call(f32[384,128]{1,0:T(8,128)S(1)} %bitcast.18, f32[256,128]{1,0:T(8,128)} %get-tuple-element.69.east_s, f32[256,128]{1,0:T(8,128)} %get-tuple-element.70.north_s, ...), custom_call_target="tpu_custom_call", output_to_operand_aliasing={{0}: (1, {}), {1}: (2, {}), {2}: (3, {})} | custom-call | flops 4000000000 | bytes 16000000 | tf_op jit(solution)/shard_map/final/pallas_call | solution.py:670
  (2 shorter events, 0.0 us)
Async XLA Ops:
  0.6 16.2 %copy-start.6 = (f32[32,32]{1,0:T(8,128)S(1)}, f32[32,32]{1,0:T(8,128)}, u32[]{:S(2)}) copy-start(f32[32,32]{1,0:T(8,128)} %constant.16.clone.ztab) | copy-start | bytes 12292
  3.3 13.5 %collective-permute-start = (f32[480,128]{1,0:T(8,128)}, f32[480,128]{1,0:T(8,128)S(1)}, u32[]{:S(2)}, u32[]{:S(2)}) collective-permute-start(f32[480,128]{1,0:T(8,128)} %get-tuple-element.48), channel_id=1, source_target_pairs={{0,16},{16,32},{32,48},{48,64},{64,80},{80,96},{96,112},{112,128},... | collective-permute-start | bytes 737288 | tf_op jit(solution)/shard_map/ppermute | solution.py:584
  5.4 11.4 %collective-permute-start.1 = (f32[480,128]{1,0:T(8,128)}, f32[480,128]{1,0:T(8,128)S(1)}, u32[]{:S(2)}, u32[]{:S(2)}) collective-permute-start(f32[480,128]{1,0:T(8,128)} %get-tuple-element.49), channel_id=1, source_target_pairs={{0,240},{16,0},{32,16},{48,32},{64,48},{80,64},{96,80},{112,96},{1... | collective-permute-start | bytes 737288 | tf_op jit(solution)/shard_map/ppermute | solution.py:585
  9.2 4.9 %collective-permute-start.2 = (f32[288,128]{1,0:T(8,128)}, f32[288,128]{1,0:T(8,128)S(1)}, u32[]{:S(2)}, u32[]{:S(2)}) collective-permute-start(f32[288,128]{1,0:T(8,128)} %get-tuple-element.50), channel_id=1, source_target_pairs={{0,1},{1,2},{2,3},{3,4},{4,5},{5,6},{6,7},{7,8},{8,9},{9,10},{10,1... | collective-permute-start | bytes 442376 | tf_op jit(solution)/shard_map/ppermute | solution.py:586
  11.8 5.1 %collective-permute-start.3 = (f32[288,128]{1,0:T(8,128)}, f32[288,128]{1,0:T(8,128)S(1)}, u32[]{:S(2)}, u32[]{:S(2)}) collective-permute-start(f32[288,128]{1,0:T(8,128)} %get-tuple-element.51), channel_id=1, source_target_pairs={{0,15},{1,0},{2,1},{3,2},{4,3},{5,4},{6,5},{7,6},{8,7},{9,8},{10,9... | collective-permute-start | bytes 442376 | tf_op jit(solution)/shard_map/ppermute | solution.py:587
  16.9 1.1 %copy-start.7 = (f32[1280,128]{1,0:T(8,128)S(1)}, f32[1280,128]{1,0:T(8,128)}, u32[]{:S(2)}) copy-start(f32[1280,128]{1,0:T(8,128)} %get-tuple-element.47.fields) | copy-start | bytes 1966084
  20.9 10.8 %all-to-all-start = ((f32[16,24,128]{2,1,0:T(8,128)}), f32[16,24,128]{2,1,0:T(8,128)S(1)}, u32[]{:S(2)}, u32[]{:S(2)}) async-start(f32[16,24,128]{2,1,0:T(8,128)} %bitcast.5), calls=%async_computation | async-start | bytes 393216 | tf_op jit(solution)/shard_map/all_to_all | solution.py:605
  24.5 7.2 %copy-start.1 = (f32[256,384]{1,0:T(8,128)S(1)}, f32[256,384]{1,0:T(8,128)}, u32[]{:S(2)}) copy-start(f32[256,384]{1,0:T(8,128)} %constant.18.clone.wmain) | copy-start | bytes 1179652
  24.5 7.2 %copy-start.2 = (f32[256,128]{1,0:T(8,128)S(1)}, f32[256,128]{1,0:T(8,128)}, u32[]{:S(2)}) copy-start(f32[256,128]{1,0:T(8,128)} %constant.22.clone.cs) | copy-start | bytes 393220
  24.5 7.2 %copy-start.3 = (f32[256,16]{1,0:T(8,128)S(1)}, f32[256,16]{1,0:T(8,128)}, u32[]{:S(2)}) copy-start(f32[256,16]{1,0:T(8,128)} %constant.20.clone.t12) | copy-start | bytes 49156
  27.4 19.3 %copy-start.8 = (f32[1280,128]{1,0:T(8,128)S(1)}, f32[1280,128]{1,0:T(8,128)}, u32[]{:S(2)}) copy-start(f32[1280,128]{1,0:T(8,128)} %get-tuple-element.47.fields) | copy-start | bytes 1966084
  27.4 20.9 %collective-permute-start.4 = (f32[40,1024]{1,0:T(8,128)}, f32[40,1024]{1,0:T(8,128)S(1)}, u32[]{:S(2)}, u32[]{:S(2)}) collective-permute-start(f32[40,1024]{1,0:T(8,128)} %get-tuple-element.63), channel_id=1, source_target_pairs={{0,1},{1,2},{2,3},{3,4},{4,5},{5,6},{6,7},{7,8},{8,9},{9,10},{10,1... | collective-permute-start | bytes 491528 | tf_op jit(solution)/shard_map/ppermute | solution.py:615
  31.3 17.0 %collective-permute-start.5 = (f32[40,1024]{1,0:T(8,128)}, f32[40,1024]{1,0:T(8,128)S(1)}, u32[]{:S(2)}, u32[]{:S(2)}) collective-permute-start(f32[40,1024]{1,0:T(8,128)} %get-tuple-element.64), channel_id=1, source_target_pairs={{0,15},{1,0},{2,1},{3,2},{4,3},{5,4},{6,5},{7,6},{8,7},{9,8},{10,9... | collective-permute-start | bytes 491528 | tf_op jit(solution)/shard_map/ppermute | solution.py:616
  31.7 0.9 %copy-start.11 = (f32[272,128]{1,0:T(8,128)S(1)}, f32[272,128]{1,0:T(8,128)}, u32[]{:S(2)}) copy-start(f32[272,128]{1,0:T(8,128)} %get-tuple-element.54.tabs) | copy-start | bytes 417796
  34.7 19.8 %all-to-all-start.1 = ((f32[16,8,128]{2,1,0:T(8,128)}), f32[16,8,128]{2,1,0:T(8,128)S(1)}, u32[]{:S(2)}, u32[]{:S(2)}) async-start(f32[16,8,128]{2,1,0:T(8,128)} %bitcast.8), calls=%async_computation.1 | async-start | bytes 131072 | tf_op jit(solution)/shard_map/all_to_all | solution.py:626
  46.7 1.6 %copy-start.9 = (f32[32,1024]{1,0:T(8,128)S(1)}, f32[32,1024]{1,0:T(8,128)}, u32[]{:S(2)}) copy-start(f32[32,1024]{1,0:T(8,128)} %get-tuple-element.62.part) | copy-start | bytes 393220
  46.7 7.8 %copy-start = (f32[384,256]{1,0:T(8,128)S(1)}, f32[384,256]{1,0:T(8,128)}, u32[]{:S(2)}) copy-start(f32[384,256]{1,0:T(8,128)} %constant.19.clone.wback) | copy-start | bytes 1179652
  46.7 7.8 %copy-start.5 = (f32[16,256]{1,0:T(8,128)S(1)}, f32[16,256]{1,0:T(8,128)}, u32[]{:S(2)}) copy-start(f32[16,256]{1,0:T(8,128)} %constant.21.clone.t12t) | copy-start | bytes 49156
  46.8 7.8 %copy-start.12 = (f32[272,128]{1,0:T(8,128)S(1)}, f32[272,128]{1,0:T(8,128)}, u32[]{:S(2)}) copy-start(f32[272,128]{1,0:T(8,128)} %get-tuple-element.54.tabs) | copy-start | bytes 417796
  48.4 12.4 %copy-start.10 = (f32[16,1024]{1,0:T(8,128)S(1)}, f32[16,1024]{1,0:T(8,128)}, u32[]{:S(2)}) copy-start(f32[16,1024]{1,0:T(8,128)} %get-tuple-element.72.mid) | copy-start | bytes 196612
  48.4 12.3 %collective-permute-start.6 = (f32[40,1024]{1,0:T(8,128)S(1)}, f32[40,1024]{1,0:T(8,128)S(1)}, u32[]{:S(2)}, u32[]{:S(2)}) collective-permute-start(f32[40,1024]{1,0:T(8,128)S(1)} %get-tuple-element.73), channel_id=1, source_target_pairs={{0,16},{16,32},{32,48},{48,64},{64,80},{80,96},{96,112},{112,128},... | collective-permute-start | bytes 491528 | tf_op jit(solution)/shard_map/ppermute | solution.py:638
  48.8 11.9 %collective-permute-start.7 = (f32[40,1024]{1,0:T(8,128)S(1)}, f32[40,1024]{1,0:T(8,128)S(1)}, u32[]{:S(2)}, u32[]{:S(2)}) collective-permute-start(f32[40,1024]{1,0:T(8,128)S(1)} %get-tuple-element.74), channel_id=1, source_target_pairs={{0,240},{16,0},{32,16},{48,32},{64,48},{80,64},{96,80},{112,96},{1... | collective-permute-start | bytes 491528 | tf_op jit(solution)/shard_map/ppermute | solution.py:639
  56.3 12.1 %all-to-all-start.2 = ((f32[16,24,128]{2,1,0:T(8,128)}), f32[16,24,128]{2,1,0:T(8,128)S(1)}, u32[]{:S(2)}, u32[]{:S(2)}) async-start(f32[16,24,128]{2,1,0:T(8,128)} %bitcast.10), calls=%async_computation.2 | async-start | bytes 393216 | tf_op jit(solution)/shard_map/all_to_all | solution.py:646
  63.9 4.5 %copy-start.4 = (f32[64,32]{1,0:T(8,128)S(1)}, f32[64,32]{1,0:T(8,128)}, u32[]{:S(2)}) copy-start(f32[64,32]{1,0:T(8,128)} %constant.17.clone.zback) | copy-start | bytes 24580

commit v5 on v4

--- a/solution.py
+++ b/solution.py
@@ -179,8 +179,6 @@
             thi = jnp.where(mask, pltpu.roll(row, at, 1), thi)
     ylo[0:NZ, :] = tlo
     yhi[0:NZ, :] = thi
-    ylo[NZ:, :] = jnp.zeros((8 * NZ, NY), F32)
-    yhi[NZ:, :] = jnp.zeros((8 * NZ, NY), F32)
 
 
 def pack_kernel(
@@ -574,7 +572,7 @@
         "sides",
         2.0,
         (
-            sds(15 * NZ, NY), sds(15 * NZ, NY), sds(9 * NZ, NY), sds(9 * NZ, NY),
+            sds(15 * NZ, NY), sds(15 * NZ, NY), sds(1 * NZ, NY), sds(1 * NZ, NY),
             sds(5 * ROWS, NY), TOKEN,
         ),
         [HBM] * 5,

time: 75.2 us -> 75.2 us (level)
  waiting for transfers between devices: 8.82 us -> 7.42 us
  starting transfers between devices: 37.5 us -> 38.9 us
    all_to_all x2, starting transfers between devices: 8.09 us -> 9.49 us  [per_device(): recv = lax.all_to_all(send.reshape(GX, BLK, NY), 'gx', 0, 0, tiled=True)]
    ppermute x1, waiting for transfers between devices: 2.2 us -> 0.88 us  [per_device(): ylo = lax.ppermute(ylo, 'gy', ring('gy', 1))]
where the time goes in v5:
time: 75.2 us; the launch traced here: 74.7 us
  starting transfers between devices  38.9 us (52%)
  Pallas kernels  25.4 us (34%)
  waiting for transfers between devices  7.42 us (10%)
  local copies, waits for them, and re-layouts  2.05 us (3%)
  between operations  0.88 us (1%)
    all_to_all x1, starting transfers between devices, per_device(): got = lax.all_to_all(msg.reshape(GY, 8, NY), 'gy', 0, 0, tiled=True)  12 us
    all_to_all x2, starting transfers between devices, per_device(): recv = lax.all_to_all(send.reshape(GX, BLK, NY), 'gx', 0, 0, tiled=True)  9.49 us
    pallas_call x1, Pallas kernels, per_device(): call(final_kernel, 'final', 8.0, (sds(ROWS, NY), sds(ROWS, NY), sds(ROWS,...  6.39 us
    ppermute x1, starting transfers between devices, per_device(): chi = lax.ppermute(cdown, 'gx', ring('gx', -1))  4.5 us
    ppermute x1, starting transfers between devices, per_device(): mlo = lax.ppermute(up, 'gy', ring('gy', 1))  3.88 us
    ppermute x1, starting transfers between devices, per_device(): xhi = lax.ppermute(xhi, 'gx', ring('gx', -1))  3.81 us
    pallas_call x1, Pallas kernels, per_device(): call(wind_kernel, 'winds', 3.0, (sds(ROWS, NY), sds(ROWS, NY), sds(ROWS,...  2.96 us
    pallas_call x1, Pallas kernels, per_device(): call(growth_kernel, 'growth', 5.0, (sds(11, 9, CAP), sds(9, CAP)), [VM] *...  2.92 us
  transfers between devices with their start and end apart: 11, of which 5 were waited for; matrix products, arithmetic and copies ran while one was open for 0% of the time, Pallas kernels for 18%

profile of v5, /device:TPU:1, one launch (start us, length us, event | category | flops | bytes accessed | tf_op | source)
XLA Modules:
  0.0 74.7 jit_solution(703545655493716281)
XLA Ops:
  0.6 0.0 copy-start.6
  0.6 2.6 %sides.1 = (f32[480,128]{1,0:T(8,128)}, f32[480,128]{1,0:T(8,128)}, f32[32,128]{1,0:T(8,128)}, f32[32,128]{1,0:T(8,128)}, f32[1280,128]{1,0:T(8,128)}, /*index=5*/f32[8,128]{1,0:T(8,128)}) custom-call(f32[256,128]{1,0:T(8,128)} %bitcast.22, f32[256,128]{1,0:T(8,128)} %bitcast.23, f32[256,128]{1,0:T(8,128)} %bitcast.24, f32[256,128]{1,0:T(8,128)} %bitcast.25, ...), custom_call_target="tpu_custom_call" | custom-call | flops 1000000000 | bytes 4000000 | tf_op jit(solution)/shard_map/sides/pallas_call | solution.py:570
  3.2 2.1 %collective-permute-start = (f32[480,128]{1,0:T(8,128)}, f32[480,128]{1,0:T(8,128)S(1)}, u32[]{:S(2)}, u32[]{:S(2)}) collective-permute-start(f32[480,128]{1,0:T(8,128)} %get-tuple-element.48), channel_id=1, source_target_pairs={{0,16},{16,32},{32,48},{48,64},{64,80},{80,96},{96,112},{112,128},... | collective-permute-start | bytes 737288 | tf_op jit(solution)/shard_map/ppermute | solution.py:582
  5.4 3.8 %collective-permute-start.1 = (f32[480,128]{1,0:T(8,128)}, f32[480,128]{1,0:T(8,128)S(1)}, u32[]{:S(2)}, u32[]{:S(2)}) collective-permute-start(f32[480,128]{1,0:T(8,128)} %get-tuple-element.49), channel_id=1, source_target_pairs={{0,240},{16,0},{32,16},{48,32},{64,48},{80,64},{96,80},{112,96},{1... | collective-permute-start | bytes 737288 | tf_op jit(solution)/shard_map/ppermute | solution.py:583
  9.2 2.5 %collective-permute-start.2 = (f32[32,128]{1,0:T(8,128)}, f32[32,128]{1,0:T(8,128)S(1)}, u32[]{:S(2)}, u32[]{:S(2)}) collective-permute-start(f32[32,128]{1,0:T(8,128)} %get-tuple-element.50), channel_id=1, source_target_pairs={{0,1},{1,2},{2,3},{3,4},{4,5},{5,6},{6,7},{7,8},{8,9},{9,10},{10,1... | collective-permute-start | bytes 49160 | tf_op jit(solution)/shard_map/ppermute | solution.py:584
  11.7 0.2 collective-permute-start.3
  11.9 0.9 %collective-permute-done.2.ylo_in = f32[32,128]{1,0:T(8,128)S(1)} collective-permute-done((f32[32,128]{1,0:T(8,128)}, f32[32,128]{1,0:T(8,128)S(1)}, u32[]{:S(2)}, u32[]{:S(2)}) %collective-permute-start.2) | collective-permute-done | bytes 16416 | tf_op jit(solution)/shard_map/ppermute | solution.py:584
  12.8 2.6 %collective-permute-done.3.yhi_in = f32[32,128]{1,0:T(8,128)S(1)} collective-permute-done((f32[32,128]{1,0:T(8,128)}, f32[32,128]{1,0:T(8,128)S(1)}, u32[]{:S(2)}, u32[]{:S(2)}) %collective-permute-start.3) | collective-permute-done | bytes 16416 | tf_op jit(solution)/shard_map/ppermute | solution.py:585
  15.4 0.0 collective-permute-done.xlo
  15.4 0.0 collective-permute-done.1.xhi
  15.4 0.0 copy-done.6
  15.4 0.0 copy-start.7
  15.4 1.1 %copy-done.7 = f32[1280,128]{1,0:T(8,128)S(1)} copy-done((f32[1280,128]{1,0:T(8,128)S(1)}, f32[1280,128]{1,0:T(8,128)}, u32[]{:S(2)}) %copy-start.7) | copy-done | bytes 655384
  16.5 3.0 %winds.1 = (f32[256,128]{1,0:T(8,128)}, f32[256,128]{1,0:T(8,128)}, f32[256,128]{1,0:T(8,128)}, f32[384,128]{1,0:T(8,128)}, f32[8,128]{1,0:T(8,128)S(1)}) custom-call(f32[1280,128]{1,0:T(8,128)S(1)} %copy-done.7, f32[480,128]{1,0:T(8,128)S(1)} %collective-permute-done.xlo, f32[480,128]{1,0:T(8,128)S(1)} %collective-permute-done.1.xhi, ...), custom_call_target="tpu_custom_call" | custom-call | flops 1500000000 | bytes 6000000 | tf_op jit(solution)/shard_map/winds/pallas_call | solution.py:595
  19.4 5.0 %all-to-all-start = ((f32[16,24,128]{2,1,0:T(8,128)}), f32[16,24,128]{2,1,0:T(8,128)S(1)}, u32[]{:S(2)}, u32[]{:S(2)}) async-start(f32[16,24,128]{2,1,0:T(8,128)} %bitcast.5), calls=%async_computation | async-start | bytes 393216 | tf_op jit(solution)/shard_map/all_to_all | solution.py:603
  24.4 0.0 copy-start.1
  24.4 0.0 copy-start.2
  24.5 0.0 copy-start.3
  24.5 2.8 %pack.1 = (f32[40,1024]{1,0:T(8,128)}, f32[40,1024]{1,0:T(8,128)}, f32[16,1024]{1,0:T(8,128)}, f32[32,1024]{1,0:T(8,128)}, f32[272,128]{1,0:T(8,128)}) custom-call(f32[3,10,3,1024]{3,2,1,0:T(4,128)} %bitcast.21, s32[3,3,1024]{2,1,0:T(4,128)} %cells.1, s32[3,3]{1,0:T(4,128)} %counts.1, f32[16,272,128]{2,1,0:T(8,128)} %constant.23.clone.own, ...), custom_call_target="tpu_custom_call" | custom-call | flops 1250000000 | bytes 5000000 | tf_op jit(solution)/shard_map/pack/pallas_call | solution.py:586
  27.3 0.0 copy-start.8
  27.3 3.9 %collective-permute-start.4 = (f32[40,1024]{1,0:T(8,128)}, f32[40,1024]{1,0:T(8,128)S(1)}, u32[]{:S(2)}, u32[]{:S(2)}) collective-permute-start(f32[40,1024]{1,0:T(8,128)} %get-tuple-element.63), channel_id=1, source_target_pairs={{0,1},{1,2},{2,3},{3,4},{4,5},{5,6},{6,7},{7,8},{8,9},{9,10},{10,1... | collective-permute-start | bytes 491528 | tf_op jit(solution)/shard_map/ppermute | solution.py:613
  31.2 0.0 collective-permute-start.5
  31.2 0.4 all-to-all-done
  31.6 0.0 copy-done.1
  31.6 0.0 copy-done.2
  31.6 0.0 copy-done.3
  31.6 0.0 copy-start.11
  31.6 0.9 %copy-done.11 = f32[272,128]{1,0:T(8,128)S(1)} copy-done((f32[272,128]{1,0:T(8,128)S(1)}, f32[272,128]{1,0:T(8,128)}, u32[]{:S(2)}) %copy-start.11) | copy-done | bytes 139288
  32.5 2.1 %scan.1 = (f32[128,128]{1,0:T(8,128)}, f32[256,128]{1,0:T(8,128)S(1)}, f32[8,128]{1,0:T(8,128)S(1)}, f32[8,128]{1,0:T(8,128)S(1)}) custom-call(f32[384,128]{1,0:T(8,128)S(1)} %bitcast.19, f32[256,384]{1,0:T(8,128)S(1)} %copy-done.1, f32[256,16]{1,0:T(8,128)S(1)} %copy-done.3, f32[256,128]{1,0:T(8,128)S(1)} %copy-done.2, f32[272,128]{1,0:T(8,128)S(1)} %copy-done.11, ...), custom_call_target="tpu_custom_call" | custom-call | flops 1000000000 | bytes 4000000 | tf_op jit(solution)/shard_map/scan/pallas_call | solution.py:615
  34.7 12.0 %all-to-all-start.1 = ((f32[16,8,128]{2,1,0:T(8,128)}), f32[16,8,128]{2,1,0:T(8,128)S(1)}, u32[]{:S(2)}, u32[]{:S(2)}) async-start(f32[16,8,128]{2,1,0:T(8,128)} %bitcast.8), calls=%async_computation.1 | async-start | bytes 131072 | tf_op jit(solution)/shard_map/all_to_all | solution.py:624
  46.6 0.0 copy-done.8
  46.6 0.0 copy-start.9
  46.6 0.0 copy-start
  46.7 0.0 copy-start.5
  46.7 0.0 copy-start.12
  46.7 1.6 %heat.1 = (f32[512,128]{1,0:T(8,128)S(1)}, bf16[512,256]{1,0:T(8,128)(2,1)S(1)}, f32[8,128]{1,0:T(8,128)S(1)}) custom-call(f32[1280,128]{1,0:T(8,128)S(1)} %copy-done.8, f32[32,128]{1,0:T(8,128)S(1)} %collective-permute-done.2.ylo_in, f32[32,128]{1,0:T(8,128)S(1)} %collective-permute-done.3.yhi_in, f32[480,128]{1,0:T(8,128)S(1)} %collective-permute-done.xlo, ...), custom_call_target="tpu_custom_call" | custom-call | flops 2000000000 | bytes 8000000 | tf_op jit(solution)/shard_map/heat/pallas_call | solution.py:625
  48.3 0.0 collective-permute-done.4.mlo
  48.3 0.0 collective-permute-done.5.mhi
  48.3 0.0 copy-done.9
  48.3 0.0 copy-start.10
  48.3 0.4 collective-permute-start.6
  48.7 4.5 %collective-permute-start.7 = (f32[40,1024]{1,0:T(8,128)S(1)}, f32[40,1024]{1,0:T(8,128)S(1)}, u32[]{:S(2)}, u32[]{:S(2)}) collective-permute-start(f32[40,1024]{1,0:T(8,128)S(1)} %get-tuple-element.74), channel_id=1, source_target_pairs={{0,240},{16,0},{32,16},{48,32},{64,48},{80,64},{96,80},{112,96},{1... | collective-permute-start | bytes 491528 | tf_op jit(solution)/shard_map/ppermute | solution.py:637
  53.2 1.2 %all-to-all-done.1 = f32[16,8,128]{2,1,0:T(8,128)S(1)} async-done(((f32[16,8,128]{2,1,0:T(8,128)}), f32[16,8,128]{2,1,0:T(8,128)S(1)}, u32[]{:S(2)}, u32[]{:S(2)}) %all-to-all-start.1) | async-done | bytes 65568 | tf_op jit(solution)/shard_map/all_to_all | solution.py:624
  54.4 0.0 copy-done
  54.4 0.0 copy-done.5
  54.4 0.0 copy-done.12
  54.4 1.7 %solve.1 = (f32[384,128]{1,0:T(8,128)}, f32[8,128]{1,0:T(8,128)S(1)}) custom-call(f32[128,128]{1,0:T(8,128)S(1)} %bitcast.20, f32[256,128]{1,0:T(8,128)S(1)} %get-tuple-element.60.keep, f32[8,128]{1,0:T(8,128)S(1)} %get-tuple-element.61.kink, f32[384,256]{1,0:T(8,128)S(1)} %copy-done, f32[16,256]{1,0:T(8,128)S(1)} %copy-done.5, f32[256,128]{1,0:T(8,128)S(1)} %copy-done.2, ...), custom_call_target="tpu_custom_call" | custom-call | flops 1000000000 | bytes 4000000 | tf_op jit(solution)/shard_map/solve/pallas_call | solution.py:638
  56.2 4.5 %all-to-all-start.2 = ((f32[16,24,128]{2,1,0:T(8,128)}), f32[16,24,128]{2,1,0:T(8,128)S(1)}, u32[]{:S(2)}, u32[]{:S(2)}) async-start(f32[16,24,128]{2,1,0:T(8,128)} %bitcast.10), calls=%async_computation.2 | async-start | bytes 393216 | tf_op jit(solution)/shard_map/all_to_all | solution.py:644
  60.7 0.0 collective-permute-done.6.clo
  60.7 0.0 collective-permute-done.7.chi
  60.7 0.0 copy-done.10
  60.7 0.1 unpack.1
  60.8 2.9 %growth.1 = (f32[11,9,1024]{2,1,0:T(8,128)S(1)}, f32[9,1024]{1,0:T(8,128)S(1)}) custom-call(bf16[512,256]{1,0:T(8,128)(2,1)S(1)} %get-tuple-element.77.lhs, s32[9,1024]{1,0:T(8,128)S(1)} %get-tuple-element.76.cell, f32[11,9,1024]{2,1,0:T(8,128)S(1)} %get-tuple-element.78.state), custom_call_target="tpu_custom_call" | custom-call | flops 2500000000 | bytes 10000000 | tf_op jit(solution)/shard_map/growth/pallas_call | solution.py:652
  63.8 0.0 copy-start.4
  63.8 2.2 %scatter.1 = (f32[256,128]{1,0:T(8,128)}, f32[256,128]{1,0:T(8,128)}) custom-call(f32[512,128]{1,0:T(8,128)S(1)} %get-tuple-element.83.stars, s32[9,1024]{1,0:T(8,128)S(1)} %get-tuple-element.76.cell, f32[9,1024]{1,0:T(8,128)S(1)} %get-tuple-element.84.gain), custom_call_target="tpu_custom_call" | custom-call | flops 2000000000 | bytes 8000000 | tf_op jit(solution)/shard_map/scatter/pallas_call | solution.py:660
  66.0 2.3 %all-to-all-done.2 = f32[16,24,128]{2,1,0:T(8,128)S(1)} async-done(((f32[16,24,128]{2,1,0:T(8,128)}), f32[16,24,128]{2,1,0:T(8,128)S(1)}, u32[]{:S(2)}, u32[]{:S(2)}) %all-to-all-start.2) | async-done | bytes 196640 | tf_op jit(solution)/shard_map/all_to_all | solution.py:644
  68.3 0.0 copy-done.4
  68.3 6.4 %final.1 = (f32[256,128]{1,0:T(8,128)}, f32[256,128]{1,0:T(8,128)}, f32[256,128]{1,0:T(8,128)}, f32[3,10,3,1024]{3,2,1,0:T(4,128)}) custom-call(f32[384,128]{1,0:T(8,128)S(1)} %bitcast.18, f32[256,128]{1,0:T(8,128)} %get-tuple-element.69.east_s, f32[256,128]{1,0:T(8,128)} %get-tuple-element.70.north_s, ...), custom_call_target="tpu_custom_call", output_to_operand_aliasing={{0}: (1, {}), {1}: (2, {}), {2}: (3, {})} | custom-call | flops 4000000000 | bytes 16000000 | tf_op jit(solution)/shard_map/final/pallas_call | solution.py:668
  (2 shorter events, 0.0 us)
Async XLA Ops:
  0.6 14.7 %copy-start.6 = (f32[32,32]{1,0:T(8,128)S(1)}, f32[32,32]{1,0:T(8,128)}, u32[]{:S(2)}) copy-start(f32[32,32]{1,0:T(8,128)} %constant.16.clone.ztab) | copy-start | bytes 12292
  3.2 12.1 %collective-permute-start = (f32[480,128]{1,0:T(8,128)}, f32[480,128]{1,0:T(8,128)S(1)}, u32[]{:S(2)}, u32[]{:S(2)}) collective-permute-start(f32[480,128]{1,0:T(8,128)} %get-tuple-element.48), channel_id=1, source_target_pairs={{0,16},{16,32},{32,48},{48,64},{64,80},{80,96},{96,112},{112,128},... | collective-permute-start | bytes 737288 | tf_op jit(solution)/shard_map/ppermute | solution.py:582
  5.4 10.0 %collective-permute-start.1 = (f32[480,128]{1,0:T(8,128)}, f32[480,128]{1,0:T(8,128)S(1)}, u32[]{:S(2)}, u32[]{:S(2)}) collective-permute-start(f32[480,128]{1,0:T(8,128)} %get-tuple-element.49), channel_id=1, source_target_pairs={{0,240},{16,0},{32,16},{48,32},{64,48},{80,64},{96,80},{112,96},{1... | collective-permute-start | bytes 737288 | tf_op jit(solution)/shard_map/ppermute | solution.py:583
  9.2 3.6 %collective-permute-start.2 = (f32[32,128]{1,0:T(8,128)}, f32[32,128]{1,0:T(8,128)S(1)}, u32[]{:S(2)}, u32[]{:S(2)}) collective-permute-start(f32[32,128]{1,0:T(8,128)} %get-tuple-element.50), channel_id=1, source_target_pairs={{0,1},{1,2},{2,3},{3,4},{4,5},{5,6},{6,7},{7,8},{8,9},{9,10},{10,1... | collective-permute-start | bytes 49160 | tf_op jit(solution)/shard_map/ppermute | solution.py:584
  11.7 3.7 %collective-permute-start.3 = (f32[32,128]{1,0:T(8,128)}, f32[32,128]{1,0:T(8,128)S(1)}, u32[]{:S(2)}, u32[]{:S(2)}) collective-permute-start(f32[32,128]{1,0:T(8,128)} %get-tuple-element.51), channel_id=1, source_target_pairs={{0,15},{1,0},{2,1},{3,2},{4,3},{5,4},{6,5},{7,6},{8,7},{9,8},{10,9... | collective-permute-start | bytes 49160 | tf_op jit(solution)/shard_map/ppermute | solution.py:585
  15.4 1.1 %copy-start.7 = (f32[1280,128]{1,0:T(8,128)S(1)}, f32[1280,128]{1,0:T(8,128)}, u32[]{:S(2)}) copy-start(f32[1280,128]{1,0:T(8,128)} %get-tuple-element.47.fields) | copy-start | bytes 1966084
  19.4 12.2 %all-to-all-start = ((f32[16,24,128]{2,1,0:T(8,128)}), f32[16,24,128]{2,1,0:T(8,128)S(1)}, u32[]{:S(2)}, u32[]{:S(2)}) async-start(f32[16,24,128]{2,1,0:T(8,128)} %bitcast.5), calls=%async_computation | async-start | bytes 393216 | tf_op jit(solution)/shard_map/all_to_all | solution.py:603
  24.4 7.2 %copy-start.1 = (f32[256,384]{1,0:T(8,128)S(1)}, f32[256,384]{1,0:T(8,128)}, u32[]{:S(2)}) copy-start(f32[256,384]{1,0:T(8,128)} %constant.18.clone.wmain) | copy-start | bytes 1179652
  24.4 7.2 %copy-start.2 = (f32[256,128]{1,0:T(8,128)S(1)}, f32[256,128]{1,0:T(8,128)}, u32[]{:S(2)}) copy-start(f32[256,128]{1,0:T(8,128)} %constant.22.clone.cs) | copy-start | bytes 393220
  24.5 7.2 %copy-start.3 = (f32[256,16]{1,0:T(8,128)S(1)}, f32[256,16]{1,0:T(8,128)}, u32[]{:S(2)}) copy-start(f32[256,16]{1,0:T(8,128)} %constant.20.clone.t12) | copy-start | bytes 49156
  27.3 19.3 %copy-start.8 = (f32[1280,128]{1,0:T(8,128)S(1)}, f32[1280,128]{1,0:T(8,128)}, u32[]{:S(2)}) copy-start(f32[1280,128]{1,0:T(8,128)} %get-tuple-element.47.fields) | copy-start | bytes 1966084
  27.3 20.9 %collective-permute-start.4 = (f32[40,1024]{1,0:T(8,128)}, f32[40,1024]{1,0:T(8,128)S(1)}, u32[]{:S(2)}, u32[]{:S(2)}) collective-permute-start(f32[40,1024]{1,0:T(8,128)} %get-tuple-element.63), channel_id=1, source_target_pairs={{0,1},{1,2},{2,3},{3,4},{4,5},{5,6},{6,7},{7,8},{8,9},{9,10},{10,1... | collective-permute-start | bytes 491528 | tf_op jit(solution)/shard_map/ppermute | solution.py:613
  31.2 17.0 %collective-permute-start.5 = (f32[40,1024]{1,0:T(8,128)}, f32[40,1024]{1,0:T(8,128)S(1)}, u32[]{:S(2)}, u32[]{:S(2)}) collective-permute-start(f32[40,1024]{1,0:T(8,128)} %get-tuple-element.64), channel_id=1, source_target_pairs={{0,15},{1,0},{2,1},{3,2},{4,3},{5,4},{6,5},{7,6},{8,7},{9,8},{10,9... | collective-permute-start | bytes 491528 | tf_op jit(solution)/shard_map/ppermute | solution.py:614
  31.6 0.9 %copy-start.11 = (f32[272,128]{1,0:T(8,128)S(1)}, f32[272,128]{1,0:T(8,128)}, u32[]{:S(2)}) copy-start(f32[272,128]{1,0:T(8,128)} %get-tuple-element.54.tabs) | copy-start | bytes 417796
  34.7 19.8 %all-to-all-start.1 = ((f32[16,8,128]{2,1,0:T(8,128)}), f32[16,8,128]{2,1,0:T(8,128)S(1)}, u32[]{:S(2)}, u32[]{:S(2)}) async-start(f32[16,8,128]{2,1,0:T(8,128)} %bitcast.8), calls=%async_computation.1 | async-start | bytes 131072 | tf_op jit(solution)/shard_map/all_to_all | solution.py:624
  46.6 1.6 %copy-start.9 = (f32[32,1024]{1,0:T(8,128)S(1)}, f32[32,1024]{1,0:T(8,128)}, u32[]{:S(2)}) copy-start(f32[32,1024]{1,0:T(8,128)} %get-tuple-element.62.part) | copy-start | bytes 393220
  46.6 7.8 %copy-start = (f32[384,256]{1,0:T(8,128)S(1)}, f32[384,256]{1,0:T(8,128)}, u32[]{:S(2)}) copy-start(f32[384,256]{1,0:T(8,128)} %constant.19.clone.wback) | copy-start | bytes 1179652
  46.7 7.8 %copy-start.5 = (f32[16,256]{1,0:T(8,128)S(1)}, f32[16,256]{1,0:T(8,128)}, u32[]{:S(2)}) copy-start(f32[16,256]{1,0:T(8,128)} %constant.21.clone.t12t) | copy-start | bytes 49156
  46.7 7.8 %copy-start.12 = (f32[272,128]{1,0:T(8,128)S(1)}, f32[272,128]{1,0:T(8,128)}, u32[]{:S(2)}) copy-start(f32[272,128]{1,0:T(8,128)} %get-tuple-element.54.tabs) | copy-start | bytes 417796
  48.3 12.4 %copy-start.10 = (f32[16,1024]{1,0:T(8,128)S(1)}, f32[16,1024]{1,0:T(8,128)}, u32[]{:S(2)}) copy-start(f32[16,1024]{1,0:T(8,128)} %get-tuple-element.72.mid) | copy-start | bytes 196612
  48.3 12.3 %collective-permute-start.6 = (f32[40,1024]{1,0:T(8,128)S(1)}, f32[40,1024]{1,0:T(8,128)S(1)}, u32[]{:S(2)}, u32[]{:S(2)}) collective-permute-start(f32[40,1024]{1,0:T(8,128)S(1)} %get-tuple-element.73), channel_id=1, source_target_pairs={{0,16},{16,32},{32,48},{48,64},{64,80},{80,96},{96,112},{112,128},... | collective-permute-start | bytes 491528 | tf_op jit(solution)/shard_map/ppermute | solution.py:636
  48.7 11.9 %collective-permute-start.7 = (f32[40,1024]{1,0:T(8,128)S(1)}, f32[40,1024]{1,0:T(8,128)S(1)}, u32[]{:S(2)}, u32[]{:S(2)}) collective-permute-start(f32[40,1024]{1,0:T(8,128)S(1)} %get-tuple-element.74), channel_id=1, source_target_pairs={{0,240},{16,0},{32,16},{48,32},{64,48},{80,64},{96,80},{112,96},{1... | collective-permute-start | bytes 491528 | tf_op jit(solution)/shard_map/ppermute | solution.py:637
  56.2 12.1 %all-to-all-start.2 = ((f32[16,24,128]{2,1,0:T(8,128)}), f32[16,24,128]{2,1,0:T(8,128)S(1)}, u32[]{:S(2)}, u32[]{:S(2)}) async-start(f32[16,24,128]{2,1,0:T(8,128)} %bitcast.10), calls=%async_computation.2 | async-start | bytes 393216 | tf_op jit(solution)/shard_map/all_to_all | solution.py:644
  63.8 4.5 %copy-start.4 = (f32[64,32]{1,0:T(8,128)S(1)}, f32[64,32]{1,0:T(8,128)}, u32[]{:S(2)}) copy-start(f32[64,32]{1,0:T(8,128)} %constant.17.clone.zback) | copy-start | bytes 24580
